TPU v7x, 128 devices: a whole 4x4x4 slice. The times are simulated.
128 devices in a mesh: rep: 4 (over z), vocab: 32 (over y, x, core).
Axes of the slice: x: 4, y: 4, z: 4, core: 2. Of those that a mesh axis runs over, the one named last changes fastest.
Arguments:
- queries: bfloat16 [1024, 8192], P(('rep', 'vocab')), may hold values from -160 to 160
- cache_keys: bfloat16 [1024, 256, 1024], P(('rep', 'vocab')), may hold values from -6 to 6
- cache_values: bfloat16 [1024, 256, 1024], P(('rep', 'vocab')), may hold values from -5 to 5
- new_keys: bfloat16 [1024, 1024], P(('rep', 'vocab')), may hold values from -5 to 5
- new_values: bfloat16 [1024, 1024], P(('rep', 'vocab')), may hold values from -5 to 5
- lengths: int32 [1024], P(('rep', 'vocab')), may hold values from 2 to 256, as said below
- residual: bfloat16 [1024, 8192], P(None, ('rep', 'vocab')), may hold values from -140 to 140
- gain: float32 [8192], replicated, may hold values from 0.1 to 1.9
- out_weight: bfloat16 [8192, 8192], P(None, ('rep', 'vocab')), may hold values from -0.25 to 0.25
- head_weight: bfloat16 [8192, 98304], P(None, ('vocab', 'rep')), may hold values from -2.5 to 2.5
- amateur_hidden: bfloat16 [1024, 896], P('rep'), may hold values from -16 to 16
- amateur_head: bfloat16 [896, 98304], P(None, 'vocab'), may hold values from -7 to 7
- thresholds: int32 [1024], replicated, may hold values from 1 to 8
Outputs:
- contrast: float32 [1024, 98304], P(None, ('vocab', 'rep'))
Inputs may be any that keep to these rules, and one draw needn't show every extreme that they name: `lengths`: some row's cache is full in every draw.
All inputs are finite; a program needn't handle non-finite values.
Results may differ from a plain program's by a relative error of at most 0.0075.
Values may be sent and summed in bfloat16 or wider, within the bound.
No kernel may reach another device: no remote copies, remote signals or barrier semaphores. Data moves between devices by JAX's collectives and lax.ppermute only.
A program may use at most 128 MiB of HBM per device.

v0:
```python
import math

import jax
import jax.numpy as jnp
from jax import lax
from jax.sharding import PartitionSpec as P

QH = 64
KVH = 8


EPSILON = 1e-06
LOG_TWO = math.log(2.0)
MASK_FILL = -1e30


def combined_all(part, axis, combine):
    gathered = jax.tree.map(lambda a: lax.all_gather(a, axis), part)

    def take(source):
        return jax.tree.map(lambda a: lax.dynamic_index_in_dim(a, source, 0, False), gathered)

    return lax.fori_loop(
        1, lax.axis_size(axis), lambda source, state: combine(state, take(source)), take(0)
    )


def attend(queries, cache_keys, cache_values, new_keys, new_values, lengths):
    row_count = queries.shape[0]
    positions = cache_keys.shape[1]
    head_size = queries.shape[1] // QH
    groups = QH // KVH
    scaling = head_size ** (-0.5)
    query_block = queries.reshape(row_count, KVH, groups, head_size)
    key_block = cache_keys.reshape(row_count, positions, KVH, head_size)
    value_block = cache_values.reshape(row_count, positions, KVH, head_size)
    scores = (
        jnp.einsum("rkgd,rlkd->rkgl", query_block, key_block, preferred_element_type=jnp.float32)
        * scaling
    )
    own_score = (
        jnp.einsum(
            "rkgd,rkd->rkg",
            query_block,
            new_keys.reshape(row_count, KVH, head_size),
            preferred_element_type=jnp.float32,
        )
        * scaling
    )
    live_mask = (jnp.arange(positions, dtype=jnp.int32)[None, :] < lengths[:, None])[
        :, None, None, :
    ]
    scores = jnp.where(live_mask, scores, MASK_FILL)
    largest = jnp.maximum(jnp.max(scores, axis=-1), own_score)
    weights = jnp.where(live_mask, jnp.exp(scores - largest[..., None]), 0.0)
    own_weight = jnp.exp(own_score - largest)
    totals = jnp.sum(weights, axis=-1) + own_weight
    probabilities = (weights / totals[..., None]).astype(jnp.bfloat16)
    own_probability = (own_weight / totals).astype(jnp.bfloat16)
    mixture = jnp.einsum(
        "rkgl,rlkd->rkgd", probabilities, value_block, preferred_element_type=jnp.float32
    )
    mixture = mixture + own_probability.astype(jnp.float32)[..., None] * new_values.reshape(
        row_count, KVH, 1, head_size
    ).astype(jnp.float32)
    return mixture.reshape(row_count, QH * head_size).astype(jnp.bfloat16)


def softmax_parts(logits):
    largest = jnp.max(logits, axis=1)
    totals = jnp.sum(jnp.exp(logits - largest[:, None]), axis=1)
    return (largest, totals)


def merge_pair(first, second):
    largest = jnp.maximum(first[0], second[0])
    return (
        largest,
        first[1] * jnp.exp(first[0] - largest) + second[1] * jnp.exp(second[0] - largest),
    )


def body(
    queries,
    cache_keys,
    cache_values,
    new_keys,
    new_values,
    lengths,
    residual,
    gain,
    out_weight,
    head_weight,
    amateur_hidden,
    amateur_head,
    thresholds,
):
    attention = attend(queries, cache_keys, cache_values, new_keys, new_values, lengths)
    branch_out = jnp.dot(
        lax.all_gather(attention, ("rep", "vocab"), axis=0, tiled=True),
        out_weight,
        preferred_element_type=jnp.float32,
    )
    hidden = (residual.astype(jnp.float32) + branch_out).astype(jnp.bfloat16)
    columns = hidden.shape[1]
    features = gain.shape[0]
    gain_part = lax.dynamic_slice_in_dim(gain, lax.axis_index(("rep", "vocab")) * columns, columns)
    widened = hidden.astype(jnp.float32)
    squares = lax.psum(jnp.sum(widened * widened, axis=1), ("rep", "vocab"))
    normed = (
        widened * lax.rsqrt(squares / features + EPSILON)[:, None] * gain_part[None, :]
    ).astype(jnp.bfloat16)
    expert = jnp.dot(
        lax.all_gather(normed, ("rep", "vocab"), axis=1, tiled=True),
        head_weight,
        preferred_element_type=jnp.float32,
    )
    expert_top, expert_totals = softmax_parts(expert)
    local_logits = jnp.dot(amateur_hidden, amateur_head, preferred_element_type=jnp.float32).astype(
        jnp.bfloat16
    )
    local_top, local_totals = softmax_parts(local_logits.astype(jnp.float32))
    local_top, local_totals = combined_all((local_top, local_totals), "vocab", merge_pair)
    amateur_lse = lax.all_gather(local_top + jnp.log(local_totals), "rep", axis=0, tiled=True)
    amateur = lax.all_to_all(local_logits, "rep", split_axis=1, concat_axis=0, tiled=True).astype(
        jnp.float32
    )
    expert_top, expert_totals = combined_all(
        (expert_top, expert_totals), ("rep", "vocab"), merge_pair
    )
    expert_lse = expert_top + jnp.log(expert_totals)
    margin = expert - expert_top[:, None] + thresholds[:, None].astype(jnp.float32) * LOG_TWO
    return (
        expert - expert_lse[:, None] - (amateur - amateur_lse[:, None]) + jnp.minimum(margin, 0.0)
    )


def solution(mesh):
    in_specs = (
        P(("rep", "vocab"), None),
        P(("rep", "vocab"), None, None),
        P(("rep", "vocab"), None, None),
        P(("rep", "vocab"), None),
        P(("rep", "vocab"), None),
        P(("rep", "vocab")),
        P(None, ("rep", "vocab")),
        P(),
        P(None, ("rep", "vocab")),
        P(None, ("vocab", "rep")),
        P("rep", None),
        P(None, "vocab"),
        P(),
    )
    out_specs = P(None, ("vocab", "rep"))
    return jax.shard_map(body, mesh=mesh, in_specs=in_specs, out_specs=out_specs, check_vma=False)
```

profile of v0, /device:TPU:1, one launch (start us, length us, event | category | flops | bytes accessed | tf_op | source)
XLA Modules:
  0.0 368.2 jit_solution(3936136882068520301)
XLA Ops:
  6.5 0.0 copy-start
  6.5 0.0 all-gather.10.cloned.1.call-start
  6.5 0.9 iota_compare_fusion
  7.4 1.6 fusion.28
  9.0 3.5 fusion.35
  12.6 0.3 fusion.23
  12.9 0.0 copy-done.4
  12.9 0.0 copy-done.6
  12.9 0.0 copy-start.3
  13.0 0.7 fusion.20
  13.7 0.8 copy.67
  14.5 0.0 all-gather.10.cloned.1.call-update
  14.5 0.0 all-gather.12.cloned.1.call-start
  14.5 0.8 dynamic_slice.57
  15.3 83.3 %all-gather.10.cloned.1.call-done = bf16[1024,8192]{1,0:T(8,128)(2,1)} async-done(((bf16[8,8192]{1,0:T(8,128)(2,1)}), bf16[1024,8192]{1,0:T(8,128)(2,1)}) %all-gather.10.cloned.1.call-update) | async-done | bytes 16777232 | tf_op jit(solution)/shard_map/all_gather | solution.py:100
  98.6 0.0 copy-done
  98.6 0.0 copy-done.3
  98.6 11.0 %multiply_reduce_fusion = (f32[1024]{0:T(1024)S(1)}, f32[1024,64]{0,1:T(8,128)S(1)}) fusion(bf16[1024,8192]{1,0:T(8,128)(2,1)} %all-gather.10.cloned.1.call-done, bf16[8192,64]{0,1:T(8,128)(2,1)S(1)} %copy-done, bf16[1024,64]{0,1:T(8,128)(2,1)S(1)} %copy-done.3), kind=kOutput, calls=%fused_computation.29 | convolution fusion | flops 1074134016 | bytes 18223104 | tf_op jit(solution)/shard_map/dot_general | solution.py:99
  109.6 64.5 %psum.7 = f32[1024]{0:T(1024)S(1)} all-reduce(f32[1024]{0:T(1024)S(1)} %get-tuple-element.307), channel_id=1, replica_groups=mesh['rep'=4,'vocab'=32] {'rep','vocab'}, use_global_device_ids=true, to_apply=%region_3.4 | all-reduce | flops 1024 | bytes 8192 | tf_op jit(solution)/shard_map/psum | solution.py:109
  174.0 0.7 multiply_convert_fusion
  174.8 0.0 all-gather.12.cloned.1.call-update
  174.8 0.0 copy-done.7
  174.8 4.4 %fusion.37 = (bf16[256]{0:T(256)(128)(2,1)S(1)}, bf16[256,3072]{1,0:T(8,128)(2,1)S(1)}) fusion(bf16[256,896]{1,0:T(8,128)(2,1)S(1)} %copy-done.7, bf16[896,3072]{1,0:T(8,128)(2,1)} %param.28), kind=kOutput, calls=%fused_computation.55 | convolution fusion | flops 1410858752 | bytes 7537152 | tf_op jit(solution)/shard_map/dot_general | solution.py:119
  179.2 1.6 copy.29
  180.8 4.5 %all-to-all-start = ((bf16[256,4,768]{0,2,1:T(8,128)(2,1)}), bf16[256,4,768]{0,2,1:T(8,128)(2,1)}, u32[]{:S(2)}, u32[]{:S(2)}) async-start(bf16[256,4,768]{0,2,1:T(8,128)(2,1)} %bitcast.10), calls=%async_computation | async-start | bytes 3145728 | tf_op jit(solution)/shard_map/all_to_all | solution.py:125
  185.3 0.7 exponential_reduce_fusion
  186.0 24.1 %all-gather.5 = f32[32,1,256]{2,1,0:T(1,128)S(1)} all-gather(f32[1,1,256]{2,1,0:T(1,128)S(1)} %bitcast.92), channel_id=5, replica_groups=mesh['rep'=4,'vocab'=32] {'vocab'}, dimensions={0}, use_global_device_ids=true | all-gather | bytes 33792 | tf_op jit(solution)/shard_map/all_gather | solution.py:18
  210.1 21.9 %all-gather.4 = f32[32,1,256]{2,1,0:T(1,128)S(1)} all-gather(f32[1,1,256]{2,1,0:T(1,128)S(1)} %bitcast.91), channel_id=4, replica_groups=mesh['rep'=4,'vocab'=32] {'vocab'}, dimensions={0}, use_global_device_ids=true | all-gather | bytes 33792 | tf_op jit(solution)/shard_map/all_gather | solution.py:18
  232.0 1.8 while.35
  233.8 9.1 %all-gather.6 = f32[4,1,256]{2,1,0:T(1,128)S(1)} all-gather(f32[1,1,256]{2,1,0:T(1,128)S(1)} %bitcast.93), channel_id=1, replica_groups=mesh['rep'=4,'vocab'=32] {'rep'}, dimensions={0}, use_global_device_ids=true | all-gather | bytes 5120 | tf_op jit(solution)/shard_map/all_gather | solution.py:124
  242.9 0.0 copy-done.5
  242.9 0.0 all-to-all-done
  242.9 1.7 convert_bitcast_fusion
  244.6 2.1 copy.34
  246.7 6.6 %all-gather.12.cloned.1.call-done = bf16[1024,8192]{0,1:T(8,128)(2,1)} async-done(((bf16[1024,64]{0,1:T(8,128)(2,1)}), bf16[1024,8192]{0,1:T(8,128)(2,1)}) %all-gather.12.cloned.1.call-update) | async-done | bytes 16777232 | tf_op jit(solution)/shard_map/all_gather | solution.py:114
  253.3 18.9 %fusion.36 = (f32[1024]{0:T(1024)S(1)}, f32[1024,768]{0,1:T(8,128)S(1)}) fusion(bf16[1024,8192]{0,1:T(8,128)(2,1)} %all-gather.12.cloned.1.call-done, bf16[8192,768]{1,0:T(8,128)(2,1)} %param.26), kind=kOutput, calls=%fused_computation.54 | convolution fusion | flops 12885687296 | bytes 32509952 | tf_op jit(solution)/shard_map/dot_general | solution.py:113
  272.2 0.0 copy-start.2
  272.2 1.7 copy-done.2
  273.9 0.5 exponential_reduce_fusion.1
  274.4 36.2 %all-gather.1 = f32[131072]{0:T(1024)S(1)} all-gather(f32[1024]{0:T(1024)S(1)} %exponential_reduce_fusion.1), channel_id=3, replica_groups=mesh['rep'=4,'vocab'=32] {'rep','vocab'}, dimensions={0}, use_global_device_ids=true | all-gather | bytes 528384 | tf_op jit(solution)/shard_map/all_gather | solution.py:18
  310.5 0.1 reshape.78
  310.6 33.9 %all-gather = f32[131072]{0:T(1024)S(1)} all-gather(f32[1024]{0:T(1024)S(1)} %get-tuple-element.309), channel_id=2, replica_groups=mesh['rep'=4,'vocab'=32] {'rep','vocab'}, dimensions={0}, use_global_device_ids=true | all-gather | bytes 528384 | tf_op jit(solution)/shard_map/all_gather | solution.py:18
  344.5 0.1 reshape.77
  344.6 7.6 %while.34 = (s32[]{:T(128)}, f32[1024]{0:T(1024)S(1)}, f32[1024]{0:T(1024)S(1)}, f32[128,1024]{1,0:T(8,128)S(1)}, f32[128,1024]{1,0:T(8,128)S(1)}, /*index=5*/s32[]{:T(128)}, s32[]{:T(128)}, s32[]{:T(128)}) while((s32[]{:T(128)}, f32[1024]{0:T(1024)S(1)}, f32[1024]{0:T(1024)S(1)}, f32[128,1024]{1,0:T(8,128)S(1)}, f32[128,1024]{1,0:T(8,128)S(1)}, ...), condition=%wide.region_7.8_spmd, body=%wide.region_6.7_spmd.sunk | while | flops 6149 | bytes 41091 | solution.py:23
  352.2 0.0 copy-start.1
  352.2 5.7 %minimum_add_fusion = f32[1024,768]{0,1:T(8,128)} fusion(f32[1024,768]{0,1:T(8,128)} %copy-done.2, f32[1024,768]{0,1:T(8,128)} %bitcast.76, f32[1024]{0:T(1024)S(1)} %convert_multiply_fusion, f32[1024]{0:T(1024)S(1)} %get-tuple-element.271, f32[1024]{0:T(1024)S(1)} %bitcast.90, f32[1024]{0:T(1024)S(1)} %log_add_fusion), kind=kLoop, calls=%fused_computation.14 | loop fusion | flops 5505024 | bytes 9453568 | tf_op jit(solution)/shard_map/add | solution.py:134
  357.9 3.5 copy.26
  361.4 0.0 copy-done.1
  (335 shorter events, 4.4 us)
Async XLA Ops:
  6.5 92.1 %copy-start = (bf16[8192,64]{0,1:T(8,128)(2,1)S(1)}, bf16[8192,64]{0,1:T(8,128)(2,1)}, u32[]{:S(2)}) copy-start(bf16[8192,64]{0,1:T(8,128)(2,1)} %param.25) | copy-start | bytes 3145732
  6.5 6.4 %copy-start.4 = (bf16[8,1024]{1,0:T(8,128)(2,1)S(1)}, bf16[8,1024]{1,0:T(8,128)(2,1)}, u32[]{:S(2)}) copy-start(bf16[8,1024]{1,0:T(8,128)(2,1)} %param.21) | copy-start | bytes 49156
  6.5 92.0 %all-gather.10.cloned.1.call-start = ((), (), s32[]{:S(2)}) async-start(), calls=%async_computation.1 | async-start | bytes 16908288 | tf_op jit(solution)/shard_map/all_gather | solution.py:100
  6.5 6.4 %copy-start.6 = (bf16[8,256,1024]{2,1,0:T(8,128)(2,1)S(1)}, bf16[8,256,1024]{2,1,0:T(8,128)(2,1)}, u32[]{:S(2)}) copy-start(bf16[8,256,1024]{2,1,0:T(8,128)(2,1)} %param.19) | copy-start | bytes 12582916
  12.9 85.6 %copy-start.3 = (bf16[1024,64]{0,1:T(8,128)(2,1)S(1)}, bf16[1024,64]{0,1:T(8,128)(2,1)}, u32[]{:S(2)}) copy-start(bf16[1024,64]{0,1:T(8,128)(2,1)} %param.23) | copy-start | bytes 393220
  14.5 238.9 %all-gather.12.cloned.1.call-start = ((), (), s32[]{:S(2)}) async-start(), calls=%async_computation.2 | async-start | bytes 16908288 | tf_op jit(solution)/shard_map/all_gather | solution.py:114
  15.3 159.5 %copy-start.7 = (bf16[256,896]{1,0:T(8,128)(2,1)S(1)}, bf16[256,896]{1,0:T(8,128)(2,1)}, u32[]{:S(2)}) copy-start(bf16[256,896]{1,0:T(8,128)(2,1)} %param.27) | copy-start | bytes 1376260
  180.8 62.1 %copy-start.5 = (s32[1024]{0:T(1024)S(1)}, s32[1024]{0:T(1024)}, u32[]{:S(2)}) copy-start(s32[1024]{0:T(1024)} %param.29) | copy-start | bytes 12292
  180.8 62.1 %all-to-all-start = ((bf16[256,4,768]{0,2,1:T(8,128)(2,1)}), bf16[256,4,768]{0,2,1:T(8,128)(2,1)}, u32[]{:S(2)}, u32[]{:S(2)}) async-start(bf16[256,4,768]{0,2,1:T(8,128)(2,1)} %bitcast.10), calls=%async_computation | async-start | bytes 3145728 | tf_op jit(solution)/shard_map/all_to_all | solution.py:125
  272.2 1.7 copy-start.2
  352.2 9.2 %copy-start.1 = (bf16[8192,64]{0,1:T(8,128)(2,1)S(1)}, bf16[8192,64]{0,1:T(8,128)(2,1)}, u32[]{:S(2)}) copy-start(bf16[8192,64]{0,1:T(8,128)(2,1)} %param.25) | copy-start | bytes 3145732
Sparse Core Ops, SparseCore 0:
  14.6 83.9 all-gather.9
  174.9 78.3 all-gather.11
where the time goes:
time: 369 us; the launch traced here: 368 us
  blocking collectives  190 us (51%)
  waiting for transfers between devices  89.9 us (24%)
  matrix products  40.2 us (11%)
  between operations  13.6 us (4%)
  local copies, waits for them, and re-layouts  12.9 us (3%)
  other arithmetic  12.6 us (3%)
  loops' own time  5.02 us (1%)
  starting transfers between devices  4.53 us (1%)
    all_gather x4, blocking collectives, combined_all(): gathered = jax.tree.map(lambda a: lax.all_gather(a, axis), part)  116 us
    all_gather x1, waiting for transfers between devices, body(): lax.all_gather(attention, ('rep', 'vocab'), axis=0, tiled=True)  83.3 us
    psum x1, blocking collectives, body(): squares = lax.psum(jnp.sum(widened * widened, axis=1), ('rep', 'vocab'))  64.5 us
    dot_general x1, matrix products, body(): jnp.dot(lax.all_gather(normed, ('rep', 'vocab'), axis=1, tiled=True), hea...  18.9 us
    dot_general x1, matrix products, body(): jnp.dot(lax.all_gather(attention, ('rep', 'vocab'), axis=0, tiled=True),...  11 us
    all_gather x1, blocking collectives, body(): lax.all_gather(local_top + jnp.log(local_totals), 'rep', axis=0, tiled=True)  9.11 us
  transfers between devices with their start and end apart: 3, of which 2 were waited for; matrix products, arithmetic and copies ran while one was open for 3% of the time, Pallas kernels for 0%

commit v1 on v0

v1 whole, which is shorter than its diff:
```python
import functools
import math

import jax
import jax.numpy as jnp
import numpy as np
from jax import lax
from jax.experimental import pallas as pl
from jax.experimental.pallas import tpu as pltpu
from jax.sharding import Mesh
from jax.sharding import PartitionSpec as P

QH = 64
KVH = 8

EPSILON = 1e-06
LOG_TWO = math.log(2.0)
MASK_FILL = -1e30

CHIPS = ("z", "y", "x")
ALL = ("z", "y", "x", "core")
LINE = 128
VMEM = 56 * 1024 * 1024


def attend(queries, cache_keys, cache_values, new_keys, new_values, lengths):
    row_count = queries.shape[0]
    positions = cache_keys.shape[1]
    head_size = queries.shape[1] // QH
    groups = QH // KVH
    scaling = head_size ** (-0.5)
    query_block = queries.reshape(row_count, KVH, groups, head_size)
    key_block = cache_keys.reshape(row_count, positions, KVH, head_size)
    value_block = cache_values.reshape(row_count, positions, KVH, head_size)
    scores = (
        jnp.einsum("rkgd,rlkd->rkgl", query_block, key_block, preferred_element_type=jnp.float32)
        * scaling
    )
    own_score = (
        jnp.einsum(
            "rkgd,rkd->rkg",
            query_block,
            new_keys.reshape(row_count, KVH, head_size),
            preferred_element_type=jnp.float32,
        )
        * scaling
    )
    live_mask = (jnp.arange(positions, dtype=jnp.int32)[None, :] < lengths[:, None])[
        :, None, None, :
    ]
    scores = jnp.where(live_mask, scores, MASK_FILL)
    largest = jnp.maximum(jnp.max(scores, axis=-1), own_score)
    weights = jnp.where(live_mask, jnp.exp(scores - largest[..., None]), 0.0)
    own_weight = jnp.exp(own_score - largest)
    totals = jnp.sum(weights, axis=-1) + own_weight
    probabilities = (weights / totals[..., None]).astype(jnp.bfloat16)
    own_probability = (own_weight / totals).astype(jnp.bfloat16)
    mixture = jnp.einsum(
        "rkgl,rlkd->rkgd", probabilities, value_block, preferred_element_type=jnp.float32
    )
    mixture = mixture + own_probability.astype(jnp.float32)[..., None] * new_values.reshape(
        row_count, KVH, 1, head_size
    ).astype(jnp.float32)
    return mixture.reshape(row_count, QH, head_size).astype(jnp.bfloat16)


def shift(x, axis, step):
    size = lax.axis_size(axis)
    return lax.ppermute(x, axis, [(i, (i + step) % size) for i in range(size)])


def shift_chips(x, offsets):
    sizes = tuple(lax.axis_size(axis) for axis in ALL)
    pairs = []
    for place in np.ndindex(*sizes):
        offset = offsets[place[3]] + (0,)
        target = tuple((a + o) % s for a, o, s in zip(place, offset, sizes))
        pairs.append(
            (int(np.ravel_multi_index(place, sizes)), int(np.ravel_multi_index(target, sizes)))
        )
    return lax.ppermute(x, ALL, pairs)


def quarter_of(z, y, x):
    return (x + 2 * y + z) % 4


def params():
    return pltpu.CompilerParams(vmem_limit_bytes=VMEM)


def laid_along_lanes(largest, totals):
    lane = lax.broadcasted_iota(jnp.int32, (LINE, LINE), 1)
    return jnp.transpose(jnp.where(lane == 0, largest, totals))[:2]


def projection_kernel(left_ref, weight_ref, base_ref, total_ref, sent_ref):
    product = lax.dot_general(
        left_ref[...],
        weight_ref[...],
        (((1,), (1,)), ((), ())),
        preferred_element_type=jnp.float32,
    )
    total_ref[...] = base_ref[...].astype(jnp.float32) + product[:, :LINE]
    for step in range(sent_ref.shape[0]):
        sent_ref[step] = product[:, (step + 1) * LINE : (step + 2) * LINE].astype(jnp.bfloat16)


def project(left, weight, base):
    rows, depth = left.shape
    columns = weight.shape[0]
    return pl.pallas_call(
        projection_kernel,
        out_shape=[
            jax.ShapeDtypeStruct((rows, LINE), jnp.float32),
            jax.ShapeDtypeStruct((columns // LINE - 1, rows, LINE), jnp.bfloat16),
        ],
        compiler_params=params(),
        cost_estimate=pl.CostEstimate(
            flops=2 * rows * depth * columns,
            bytes_accessed=2 * (rows + columns) * depth,
            transcendentals=0,
        ),
        name="projection",
    )(left, weight, base)


def hidden_kernel(places, total_ref, *refs):
    parts, out_ref = refs[:-1], refs[-1]
    total = total_ref[...]
    for part in parts:
        total = total + part[...].astype(jnp.float32)
    hidden = total.astype(jnp.bfloat16)
    for target, quarter in enumerate(places):
        out_ref[target] = hidden[quarter * LINE : quarter * LINE + LINE]


def hidden_copies(total, parts, places):
    return pl.pallas_call(
        functools.partial(hidden_kernel, places),
        out_shape=jax.ShapeDtypeStruct((len(places), LINE, LINE), jnp.bfloat16),
        compiler_params=params(),
        name="hidden",
    )(total, *parts)


def head_kernel(pieces, steps, features, resumed, finished, *refs):
    refs = list(refs)
    gathered = [refs.pop(0) for _ in range(pieces)]
    own_weight, other_weight, gain_ref = [refs.pop(0) for _ in range(3)]
    if resumed:
        own_before, other_before, squares_before = [refs.pop(0) for _ in range(3)]
    own_ref, other_ref, last_ref = [refs.pop(0) for _ in range(3)]
    squares_ref = refs.pop(0) if finished else last_ref
    step = pl.program_id(0)

    @pl.when(step == 0)
    def _():
        own_ref[...] = own_before[...] if resumed else jnp.zeros_like(own_ref)
        other_ref[...] = other_before[...] if resumed else jnp.zeros_like(other_ref)
        squares_ref[...] = squares_before[...] if resumed else jnp.zeros_like(squares_ref)

    rows = []
    for piece in range(pieces):
        blocks = []
        squares = None
        for block in range(gathered[piece].shape[0]):
            wide = gathered[piece][block].astype(jnp.float32)
            squares = wide * wide if squares is None else squares + wide * wide
            blocks.append((wide * gain_ref[block : block + 1]).astype(jnp.bfloat16))
        rows.append(jnp.concatenate(blocks, axis=1))
        squares_ref[piece * LINE : piece * LINE + LINE] += squares
    left = jnp.concatenate(rows, axis=0)
    own_ref[...] += jnp.dot(left, own_weight[...], preferred_element_type=jnp.float32)
    other_ref[...] += jnp.dot(left, other_weight[...], preferred_element_type=jnp.float32)

    if finished:

        @pl.when(step == steps - 1)
        def _():
            for piece in range(pieces):
                tile = slice(piece * LINE, piece * LINE + LINE)
                mean = jnp.sum(squares_ref[tile], axis=1, keepdims=True) / features
                scale = lax.rsqrt(mean + EPSILON)
                own = own_ref[tile] * scale
                other = other_ref[tile] * scale
                own_ref[tile] = own
                other_ref[tile] = other
                largest = jnp.maximum(
                    jnp.max(own, axis=1, keepdims=True), jnp.max(other, axis=1, keepdims=True)
                )
                totals = jnp.sum(jnp.exp(own - largest), axis=1, keepdims=True) + jnp.sum(
                    jnp.exp(other - largest), axis=1, keepdims=True
                )
                last_ref[2 * piece : 2 * piece + 2] = laid_along_lanes(largest, totals)


def head(gathered, own_weight, other_weight, gain, start=0, before=None, finished=True):
    pieces = len(gathered)
    blocks = gathered[0].shape[0]
    features, columns = own_weight.shape
    per = 8
    steps = blocks // per
    first = start // per
    rows = pieces * LINE
    resumed = before is not None
    whole = pl.BlockSpec((rows, columns), lambda i: (0, 0))
    lines = pl.BlockSpec((rows, LINE), lambda i: (0, 0))
    weight = pl.BlockSpec((per * LINE, columns), lambda i: (i + first, 0))
    in_specs = [pl.BlockSpec((per, LINE, LINE), lambda i: (i, 0, 0))] * pieces + [
        weight,
        weight,
        pl.BlockSpec((per, LINE), lambda i: (i + first, 0)),
    ]
    if resumed:
        in_specs += [whole, whole, lines]
    logits = jax.ShapeDtypeStruct((rows, columns), jnp.float32)
    if finished:
        last = jax.ShapeDtypeStruct((2 * pieces, LINE), jnp.float32)
        last_spec = pl.BlockSpec((2 * pieces, LINE), lambda i: (0, 0))
        scratch = [pltpu.VMEM((rows, LINE), jnp.float32)]
    else:
        last = jax.ShapeDtypeStruct((rows, LINE), jnp.float32)
        last_spec = lines
        scratch = []
    return pl.pallas_call(
        functools.partial(head_kernel, pieces, steps, features, resumed, finished),
        grid=(steps,),
        in_specs=in_specs,
        out_specs=[whole, whole, last_spec],
        out_shape=[logits, logits, last],
        scratch_shapes=scratch,
        compiler_params=params(),
        cost_estimate=pl.CostEstimate(
            flops=4 * rows * blocks * LINE * columns,
            bytes_accessed=4 * blocks * LINE * columns,
            transcendentals=0,
        ),
        name="expert_head",
    )(*gathered, own_weight, other_weight, gain, *(before or ()))


def amateur_kernel(place_ref, hidden_ref, weight_ref, logits_ref, stats_ref):
    logits = jnp.dot(
        hidden_ref[...], weight_ref[...], preferred_element_type=jnp.float32
    ).astype(jnp.bfloat16)
    logits_ref[...] = logits
    wide = logits.astype(jnp.float32)
    largest = jnp.max(wide, axis=1, keepdims=True)
    totals = jnp.sum(jnp.exp(wide - largest), axis=1, keepdims=True)
    for plane in range(2):
        picks = range(plane * 8, wide.shape[0], 16)
        stats_ref[0, plane] = laid_along_lanes(
            jnp.concatenate([largest[at : at + 8] for at in picks], axis=0),
            jnp.concatenate([totals[at : at + 8] for at in picks], axis=0),
        )


def amateur_logits(hidden, weight, place, columns):
    rows, width = hidden.shape
    tall = 2 * LINE
    return pl.pallas_call(
        amateur_kernel,
        grid_spec=pltpu.PrefetchScalarGridSpec(
            num_scalar_prefetch=1,
            grid=(rows // tall,),
            in_specs=[
                pl.BlockSpec((tall, width), lambda i, place: (i, 0)),
                pl.BlockSpec((width, columns), lambda i, place: (0, place[0])),
            ],
            out_specs=[
                pl.BlockSpec((tall, columns), lambda i, place: (i, 0)),
                pl.BlockSpec((1, 2, 2, LINE), lambda i, place: (i, 0, 0, 0)),
            ],
        ),
        out_shape=[
            jax.ShapeDtypeStruct((rows, columns), jnp.bfloat16),
            jax.ShapeDtypeStruct((rows // tall, 2, 2, LINE), jnp.float32),
        ],
        compiler_params=params(),
        cost_estimate=pl.CostEstimate(
            flops=2 * rows * width * columns,
            bytes_accessed=2 * (rows * width + width * columns + rows * columns),
            transcendentals=rows * columns,
        ),
        name="amateur_head",
    )(place, hidden, weight)


def merged(parts):
    largest = jnp.max(parts[:, :, 0], axis=0)
    totals = jnp.sum(parts[:, :, 1] * jnp.exp(parts[:, :, 0] - largest[None]), axis=0)
    return largest, totals


def column_of(row):
    return jnp.transpose(jnp.broadcast_to(row, (LINE, LINE)))


def contrast_kernel(
    place_ref,
    own_first,
    own_rest,
    other_first,
    other_rest,
    limit_ref,
    shift_ref,
    amateur_ref,
    out_ref,
    limit_col,
    shift_col,
):
    step = pl.program_id(0)
    tiles = limit_ref.shape[0]
    rows = own_first.shape[0]

    @pl.when(step == 0)
    def _():
        for tile in range(tiles):
            at = slice(tile * LINE, tile * LINE + LINE)
            limit_col[at] = column_of(limit_ref[tile : tile + 1])
            shift_col[at] = column_of(shift_ref[tile : tile + 1])

    def work(own_ref, other_ref):
        first = place_ref[1] == 0
        own, other = own_ref[...], other_ref[...]
        base = lax.rem(place_ref[0] + step // 2, 4) * LINE + lax.rem(step, 2) * rows
        planes = []
        for plane, expert in enumerate(
            (jnp.where(first, own, other), jnp.where(first, other, own))
        ):
            at = pl.ds(pl.multiple_of(base + plane * tiles // 2 * LINE, 8), rows)
            planes.append(
                expert - shift_col[at, :1] + jnp.minimum(expert + limit_col[at, :1], 0.0)
            )
        pieces = []
        for source in range(0, rows, 8):
            pieces += [plane[source : source + 8] for plane in planes]
        out_ref[...] = jnp.concatenate(pieces, axis=0) - amateur_ref[...].astype(jnp.float32)

    @pl.when(step < 2)
    def _():
        work(own_first, other_first)

    @pl.when(step >= 2)
    def _():
        work(own_rest, other_rest)


def contrast(place, own, other, limit, shift, amateur):
    rows, columns = amateur.shape
    half = LINE // 2
    first = pl.BlockSpec((half, columns), lambda i, place: (jnp.minimum(i, 1), 0))
    rest = pl.BlockSpec((half, columns), lambda i, place: (jnp.maximum(i - 2, 0), 0))
    whole = pl.BlockSpec((rows // LINE, LINE), lambda i, place: (0, 0))
    spread = pl.BlockSpec(
        (LINE, columns), lambda i, place: (lax.rem(place[0] + i // 2, 4) * 2 + lax.rem(i, 2), 0)
    )
    return pl.pallas_call(
        contrast_kernel,
        grid_spec=pltpu.PrefetchScalarGridSpec(
            num_scalar_prefetch=1,
            grid=(8,),
            in_specs=[first, rest, first, rest, whole, whole, spread],
            out_specs=spread,
            scratch_shapes=[pltpu.VMEM((rows, LINE), jnp.float32)] * 2,
        ),
        out_shape=jax.ShapeDtypeStruct((rows, columns), jnp.float32),
        compiler_params=params(),
        cost_estimate=pl.CostEstimate(
            flops=6 * rows * columns, bytes_accessed=10 * rows * columns, transcendentals=0
        ),
        name="contrast",
    )(place, own[0], own[1], other[0], other[1], limit, shift, amateur)


def body(
    queries,
    cache_keys,
    cache_values,
    new_keys,
    new_values,
    lengths,
    residual,
    gain,
    out_weight,
    head_weight,
    amateur_hidden,
    amateur_head,
    thresholds,
):
    z, y, x = (lax.axis_index(axis) for axis in CHIPS)
    core = lax.axis_index("core")
    first = core == 0
    sizes = tuple(lax.axis_size(axis) for axis in CHIPS)
    depth, chips = sizes[0], int(np.prod(sizes))
    per, width = queries.shape
    rows = residual.shape[0]
    columns = head_weight.shape[1]
    slab = width // depth
    heads = QH // depth
    quarter = quarter_of(z, y, x)

    other_weight = shift(head_weight, "core", 1)

    turned = out_weight.T
    pieces = []
    for step in range(depth):
        part = lax.dynamic_slice_in_dim(turned, lax.rem(z + step, depth) * slab, slab, 1)
        pieces.append(part if step == 0 else shift(part, "z", step))
    mine = jnp.stack(pieces)
    theirs = shift(mine, "core", 1)
    projection = jnp.stack(
        [jnp.where(first, mine, theirs), jnp.where(first, theirs, mine)], axis=1
    ).reshape(depth * 2 * turned.shape[0], slab)

    planes = residual.T.reshape(-1, chips, 2, per)
    kept = lax.dynamic_index_in_dim(planes, core, 2, False)
    given = shift(lax.dynamic_index_in_dim(planes, 1 - core, 2, False), "core", 1)
    base = jnp.concatenate([jnp.where(first, kept, given), jnp.where(first, given, kept)], axis=0)
    base = base.reshape(-1, chips * per).T

    attention = attend(queries, cache_keys, cache_values, new_keys, new_values, lengths)
    slabs = attention.reshape(per, depth, heads, LINE).transpose(1, 2, 0, 3)
    copies = jnp.broadcast_to(
        slabs.reshape(depth, 1, heads * per, LINE), (depth, chips // depth, heads * per, LINE)
    ).reshape(chips * heads * per, LINE)
    arrived = lax.all_to_all(copies, CHIPS, split_axis=0, concat_axis=0, tiled=True)
    left = arrived.reshape(chips, heads, per, LINE).transpose(0, 2, 1, 3).reshape(chips * per, slab)
    total, sent = project(left, projection, base)
    parts = [shift(sent[step - 1], "z", -step) for step in range(1, depth)]

    places = [quarter_of(*place) for place in np.ndindex(*sizes)]
    quarters = lax.all_to_all(
        hidden_copies(total, parts, places), CHIPS, split_axis=0, concat_axis=0, tiled=True
    )
    moves = (
        ((0, 0, -1), (-1, 0, 0)),
        ((0, -1, 0), (0, 1, 0)),
        ((0, 0, 1), (1, 0, 0)),
    )
    half = chips // 2
    halves = [
        [shift_chips(quarters[at : at + half], move) for move in moves] for at in (0, half)
    ]

    everyone = lax.all_gather(amateur_hidden, "z", axis=0, tiled=True)
    amateur, amateur_stats = amateur_logits(everyone, amateur_head, z.reshape(1), columns)
    by_plane = amateur_stats.transpose(1, 0, 2, 3)
    kept = lax.dynamic_index_in_dim(by_plane, core, 0, False)
    given = shift(lax.dynamic_index_in_dim(by_plane, 1 - core, 0, False), "core", 1)
    amateur_chip = jnp.stack(merged(jnp.stack([kept, given])), axis=1)

    gain_lines = gain.reshape(-1, LINE)
    own_0, other_0, stats_0 = head([quarters], head_weight, other_weight, gain_lines)
    begun = head(halves[0], head_weight, other_weight, gain_lines, finished=False)
    own_1, other_1, stats_1 = head(
        halves[1], head_weight, other_weight, gain_lines, start=half, before=begun
    )
    crossed = [shift(logits, "core", 1) for logits in (other_0, other_1)]

    stats = jnp.concatenate([stats_0, stats_1] * 2).reshape(8, 2, LINE)
    stats = lax.dynamic_slice_in_dim(stats, lax.rem(4 - quarter, 4), 4, 0)
    stats = jnp.concatenate([stats, amateur_chip])
    everywhere = lax.all_to_all(
        jnp.broadcast_to(stats[None], (chips,) + stats.shape).reshape(-1, LINE),
        CHIPS,
        split_axis=0,
        concat_axis=0,
        tiled=True,
    )
    largest, totals = merged(everywhere.reshape((chips,) + stats.shape))
    lse = largest + jnp.log(totals)
    mine = jnp.concatenate([largest[:4], lse[:4] - lse[4:]])
    theirs = shift(mine, "core", 1)
    both = jnp.where(first, jnp.stack([mine, theirs]), jnp.stack([theirs, mine]))
    limit = thresholds.astype(jnp.float32).reshape(chips, 2, per).transpose(1, 0, 2)
    limit = limit.reshape(rows // LINE, LINE) * LOG_TWO - both[:, :4].reshape(rows // LINE, LINE)
    return contrast(
        jnp.stack([quarter, core]),
        (own_0, own_1),
        crossed,
        limit,
        both[:, 4:].reshape(rows // LINE, LINE),
        amateur,
    )


def solution(mesh):
    fine = Mesh(mesh.devices.reshape(4, 4, 4, 2), ALL)
    every = ALL
    by_vocab = ("y", "x", "core")
    in_specs = (
        P(every, None),
        P(every, None, None),
        P(every, None, None),
        P(every, None),
        P(every, None),
        P(every),
        P(None, every),
        P(),
        P(None, every),
        P(None, by_vocab + ("z",)),
        P("z", None),
        P(None, by_vocab),
        P(),
    )
    out_specs = P(None, by_vocab + ("z",))
    return jax.shard_map(body, mesh=fine, in_specs=in_specs, out_specs=out_specs, check_vma=False)
```

time: 369 us -> 228 us (0.62)
  blocking collectives: 190 us -> 0 us
  Pallas kernels: 0 us -> 56.6 us
  starting transfers between devices: 4.53 us -> 45.6 us
  matrix products: 40.2 us -> 5.39 us
  waiting for transfers between devices: 89.9 us -> 79.3 us
  loops' own time: 5.02 us -> 0 us
  local copies, waits for them, and re-layouts: 12.9 us -> 17.7 us
  other arithmetic: 12.6 us -> 8.29 us
    all_gather x5 -> x0, blocking collectives: 125 us -> none  [the longest x4 116 us: combined_all(): gathered = jax.tree.map(lambda a: lax.all_gather(a, axis), part)]
    all_gather x2 -> x1, waiting for transfers between devices: 89.9 us -> 16.4 us  [body(): everyone = lax.all_gather(amateur_hidden, 'z', axis=0, tiled=True)]
    psum x1 -> x0, blocking collectives: 64.5 us -> none  [body(): squares = lax.psum(jnp.sum(widened * widened, axis=1), ('rep', 'vocab'))]
    pallas_call x0 -> x7, Pallas kernels: none -> 56.6 us  [the longest x3 35.4 us: head(): pl.pallas_call(functools.partial(head_kernel, pieces, steps, features, re...]
    all_to_all x1 -> x3, waiting for transfers between devices: 0.01 us -> 53.9 us  [the longest x1 27.2 us: body(): lax.all_to_all(hidden_copies(total, parts, places), CHIPS, split_axis=0,...]
    dot_general x3 -> x0, matrix products: 34.3 us -> none  [the longest x1 18.9 us: body(): jnp.dot(lax.all_gather(normed, ('rep', 'vocab'), axis=1, tiled=True), hea...]
    all_to_all x1 -> x3, starting transfers between devices: 4.49 us -> 27.5 us  [the longest x1 9.78 us: body(): lax.all_to_all(copies, CHIPS, split_axis=0, concat_axis=0, tiled=True)]
    ppermute x0 -> x19, starting transfers between devices: none -> 18.1 us  [the longest x13 14.3 us: shift(): return lax.ppermute(x, axis, [(i, (i + step) % size) for i in range(size)])]
  transfers between devices with their start and end apart: 3 -> 23, of which waited for: 2 -> 9; matrix products, arithmetic and copies ran while one was open for 3% -> 11% of each run, Pallas kernels for 0% -> 16%
where the time goes in v1:
time: 228 us; the launch traced here: 227 us
  waiting for transfers between devices  79.3 us (35%)
  Pallas kernels  56.6 us (25%)
  starting transfers between devices  45.6 us (20%)
  local copies, waits for them, and re-layouts  17.7 us (8%)
  between operations  13.8 us (6%)
  other arithmetic  8.29 us (4%)
  matrix products  5.39 us (2%)
    pallas_call x3, Pallas kernels, head(): pl.pallas_call(functools.partial(head_kernel, pieces, steps, features, re...  35.4 us
    all_to_all x1, waiting for transfers between devices, body(): lax.all_to_all(hidden_copies(total, parts, places), CHIPS, split_axis=0,...  27.2 us
    all_to_all x1, waiting for transfers between devices, body(): lax.all_to_all(copies, CHIPS, split_axis=0, concat_axis=0, tiled=True)  17.7 us
    all_gather x1, waiting for transfers between devices, body(): everyone = lax.all_gather(amateur_hidden, 'z', axis=0, tiled=True)  16.4 us
    ppermute x13, starting transfers between devices, shift(): return lax.ppermute(x, axis, [(i, (i + step) % size) for i in range(size)])  14.3 us
    all_to_all x1, starting transfers between devices, body(): lax.all_to_all(copies, CHIPS, split_axis=0, concat_axis=0, tiled=True)  9.78 us
    all_to_all x1, starting transfers between devices, body(): lax.all_to_all(hidden_copies(total, parts, places), CHIPS, split_axis=0,...  9.25 us
    all_to_all x1, waiting for transfers between devices, body(): lax.all_to_all(jnp.broadcast_to(stats[None], (chips,) + stats.shape).resh...  9.06 us
  transfers between devices with their start and end apart: 23, of which 9 were waited for; matrix products, arithmetic and copies ran while one was open for 11% of the time, Pallas kernels for 16%

profile of v1, /device:TPU:1, one launch (start us, length us, event | category | flops | bytes accessed | tf_op | source)
XLA Modules:
  0.0 226.7 jit_solution(16823195496920391652)
XLA Ops:
  6.5 1.4 collective-permute-start.8
  8.0 2.1 dynamic-slice_bitcast_fusion.3
  10.1 3.8 %collective-permute-start.2 = (bf16[64,2048]{1,0:T(8,128)(2,1)}, bf16[64,2048]{1,0:T(8,128)(2,1)S(1)}, u32[]{:S(2)}, u32[]{:S(2)}) collective-permute-start(bf16[64,2048]{1,0:T(8,128)(2,1)} %get-tuple-element.37), channel_id=1, source_target_pairs={{0,96},{32,0},{64,32},{96,64},{1,97},{33,1},{65,33},{97,65},{2,98}... | collective-permute-start | bytes 786440 | tf_op jit(solution)/shard_map/ppermute | solution.py:69
  15.3 0.7 iota_compare_fusion
  16.1 1.1 fusion.26
  17.2 3.5 %fusion.37 = (f32[8,8,8]{2,1,0:T(8,128)S(1)}, f32[8,8,8,256]{3,2,1,0:T(8,128)S(1)}) fusion(bf16[8,8,8,128]{3,0,2,1:T(8,128)(2,1)} %bitcast.140, pred[8,256]{1,0:T(8,128)(4,1)S(1)} %iota_compare_fusion, bf16[8,256,1024]{2,1,0:T(8,128)(2,1)} %param.14), kind=kOutput, calls=%fused_computation.70 | convolution fusion | flops 33947136 | bytes 4853760 | tf_op jit(solution)/shard_map/rkgd,rlkd->rkgl/dot_general | solution.py:36
  21.1 0.7 fusion.15
  21.9 1.8 broadcast_in_dim.45
  23.7 9.8 %all-to-all-start = ((bf16[64,128,128]{2,1,0:T(8,128)(2,1)}), bf16[64,128,128]{2,1,0:T(8,128)(2,1)S(1)}, u32[]{:S(2)}, u32[]{:S(2)}) async-start(bf16[64,128,128]{2,1,0:T(8,128)(2,1)} %bitcast.122), calls=%async_computation | async-start | bytes 4194304 | tf_op jit(solution)/shard_map/all_to_all | solution.py:428
  34.4 1.1 pad_maximum_fusion.1
  35.6 0.9 collective-permute-start.3
  36.4 0.9 copy.60
  37.3 0.9 dynamic-slice_bitcast_fusion.4
  38.3 1.5 collective-permute-done.4
  39.7 1.0 bitcast_select_fusion.1
  40.7 0.8 maximum_bitcast_fusion.base_ref
  41.5 1.3 select_bitcast_fusion.1
  43.0 1.4 copy.59
  44.4 17.7 %all-to-all-done = bf16[64,128,128]{2,1,0:T(8,128)(2,1)S(1)} async-done(((bf16[64,128,128]{2,1,0:T(8,128)(2,1)}), bf16[64,128,128]{2,1,0:T(8,128)(2,1)S(1)}, u32[]{:S(2)}, u32[]{:S(2)}) %all-to-all-start) | async-done | bytes 2097184 | tf_op jit(solution)/shard_map/all_to_all | solution.py:428
  62.1 1.3 copy-done.3
  63.4 4.4 %projection.1 = (f32[512,128]{1,0:T(8,128)}, bf16[3,512,128]{2,1,0:T(8,128)(2,1)}) custom-call(bf16[512,2048]{1,0:T(8,128)(2,1)} %bitcast.121, bf16[512,2048]{1,0:T(8,128)(2,1)} %bitcast.123, bf16[512,128]{1,0:T(8,128)(2,1)} %maximum_bitcast_fusion.base_ref), custom_call_target="tpu_custom_call" | custom-call | flops 1073741824 | bytes 4194304 | tf_op jit(solution)/shard_map/projection/pallas_call | solution.py:112
  67.8 1.1 slice_bitcast_fusion.1
  68.8 0.8 collective-permute-start.5
  69.6 0.8 collective-permute-start.6
  70.4 2.3 %collective-permute-done.5.refs_0_ = bf16[512,128]{1,0:T(8,128)(2,1)S(1)} collective-permute-done((bf16[512,128]{1,0:T(8,128)(2,1)S(1)}, bf16[512,128]{1,0:T(8,128)(2,1)S(1)}, u32[]{:S(2)}, u32[]{:S(2)}) %collective-permute-start.5) | collective-permute-done | bytes 131104 | tf_op jit(solution)/shard_map/ppermute | solution.py:69
  72.7 2.3 %collective-permute-done.6.refs_1_ = bf16[512,128]{1,0:T(8,128)(2,1)S(1)} collective-permute-done((bf16[512,128]{1,0:T(8,128)(2,1)S(1)}, bf16[512,128]{1,0:T(8,128)(2,1)S(1)}, u32[]{:S(2)}, u32[]{:S(2)}) %collective-permute-start.6) | collective-permute-done | bytes 131104 | tf_op jit(solution)/shard_map/ppermute | solution.py:69
  75.0 1.3 collective-permute-done.7.refs_2_
  77.0 2.6 %hidden.1 = bf16[64,128,128]{2,1,0:T(8,128)(2,1)} custom-call(f32[512,128]{1,0:T(8,128)} %get-tuple-element.18.total_ref, bf16[512,128]{1,0:T(8,128)(2,1)} %copy-done.13, bf16[512,128]{1,0:T(8,128)(2,1)} %copy-done.14, bf16[512,128]{1,0:T(8,128)(2,1)} %copy-done.15), custom_call_target="tpu_custom_call" | custom-call | tf_op jit(solution)/shard_map/hidden/pallas_call | solution.py:139
  79.6 9.2 %all-to-all-start.1 = ((bf16[64,128,128]{2,1,0:T(8,128)(2,1)}), bf16[64,128,128]{2,1,0:T(8,128)(2,1)S(1)}, u32[]{:S(2)}, u32[]{:S(2)}) async-start(bf16[64,128,128]{2,1,0:T(8,128)(2,1)} %hidden.1), calls=%async_computation.1 | async-start | bytes 4194304 | tf_op jit(solution)/shard_map/all_to_all | solution.py:434
  89.6 27.2 %all-to-all-done.1.refs_0_ = bf16[64,128,128]{2,1,0:T(8,128)(2,1)S(1)} async-done(((bf16[64,128,128]{2,1,0:T(8,128)(2,1)}), bf16[64,128,128]{2,1,0:T(8,128)(2,1)S(1)}, u32[]{:S(2)}, u32[]{:S(2)}) %all-to-all-start.1) | async-done | bytes 2097184 | tf_op jit(solution)/shard_map/all_to_all | solution.py:434
  116.9 1.6 fusion.35
  119.6 1.1 collective-permute-start.14
  120.7 16.4 %all-gather.2.cloned.1.call-done.hidden_ref = bf16[1024,896]{1,0:T(8,128)(2,1)} async-done(((bf16[256,896]{1,0:T(8,128)(2,1)}), bf16[1024,896]{1,0:T(8,128)(2,1)}) %all-gather.2.cloned.1.call-update) | async-done | bytes 1835024 | tf_op jit(solution)/shard_map/all_gather | solution.py:447
  137.1 6.1 %amateur_head.1 = (bf16[1024,768]{1,0:T(8,128)(2,1)}, f32[4,2,2,128]{3,2,1,0:T(2,128)}) custom-call(s32[1]{0:T(128)} %bitcast.39.place_ref, bf16[1024,896]{1,0:T(8,128)(2,1)} %all-gather.2.cloned.1.call-done.hidden_ref, bf16[896,3072]{1,0:T(8,128)(2,1)} %weight_ref.1), custom_call_target="tpu_custom_call" | custom-call | flops 1409286144 | bytes 4784128 | tf_op jit(solution)/shard_map/amateur_head/pallas_call | solution.py:262
  144.4 0.8 collective-permute-done.17
  145.2 1.1 collective-permute-start.9
  146.8 13.3 %expert_head.3 = (f32[128,768]{1,0:T(8,128)}, f32[128,768]{1,0:T(8,128)}, f32[2,128]{1,0:T(2,128)}) custom-call(bf16[64,128,128]{2,1,0:T(8,128)(2,1)} %copy-done.2, bf16[8192,768]{1,0:T(8,128)(2,1)} %refs_3_.3, bf16[8192,768]{1,0:T(8,128)(2,1)} %collective-permute-done.8.refs_2_.refs_4_, f32[64,128]{1,0:T(8,128)} %bitcast.135), custom_call_target="tpu_custom_call" | custom-call | flops 3221225472 | bytes 25165824 | tf_op jit(solution)/shard_map/expert_head/pallas_call | solution.py:226
  160.1 9.9 %expert_head.4 = (f32[384,768]{1,0:T(8,128)}, f32[384,768]{1,0:T(8,128)}, f32[384,128]{1,0:T(8,128)}) custom-call(bf16[32,128,128]{2,1,0:T(8,128)(2,1)} %copy-done.5, bf16[32,128,128]{2,1,0:T(8,128)(2,1)} %collective-permute-done.13.refs_1_, bf16[32,128,128]{2,1,0:T(8,128)(2,1)} %collective-permute-done.14.refs_2_, bf16[8192,768]{1,0:T(8,128)(2,1)} %refs_3_.3, ...), custom_call_target="tpu_custom_call" | custom-call | flops 4831838208 | bytes 12582912 | tf_op jit(solution)/shard_map/expert_head/pallas_call | solution.py:226
  170.0 1.0 copy-done.6
  171.4 12.3 %expert_head.5 = (f32[384,768]{1,0:T(8,128)}, f32[384,768]{1,0:T(8,128)}, f32[6,128]{1,0:T(8,128)}) custom-call(bf16[32,128,128]{2,1,0:T(8,128)(2,1)} %copy-done.6, bf16[32,128,128]{2,1,0:T(8,128)(2,1)} %copy-done.7, bf16[32,128,128]{2,1,0:T(8,128)(2,1)} %collective-permute-done.11.refs_2_, bf16[8192,768]{1,0:T(8,128)(2,1)} %refs_3_.3, ...), custom_call_target="tpu_custom_call" | custom-call | flops 4831838208 | bytes 12582912 | tf_op jit(solution)/shard_map/expert_head/pallas_call | solution.py:226
  183.6 0.8 pad_maximum_fusion.2
  184.4 0.8 broadcast_in_dim.47
  185.2 8.5 %all-to-all-start.2 = ((f32[64,16,128]{2,1,0:T(8,128)}), f32[64,16,128]{2,1,0:T(8,128)S(1)}, u32[]{:S(2)}, u32[]{:S(2)}) async-start(f32[64,16,128]{2,1,0:T(8,128)} %broadcast_in_dim.47), calls=%async_computation.2 | async-start | bytes 1048576 | tf_op jit(solution)/shard_map/all_to_all | solution.py:465
  193.8 2.0 collective-permute-start.15
  195.9 9.1 %all-to-all-done.2 = f32[64,16,128]{2,1,0:T(8,128)S(1)} async-done(((f32[64,16,128]{2,1,0:T(8,128)}), f32[64,16,128]{2,1,0:T(8,128)S(1)}, u32[]{:S(2)}, u32[]{:S(2)}) %all-to-all-start.2) | async-done | bytes 524320 | tf_op jit(solution)/shard_map/all_to_all | solution.py:465
  205.3 3.2 %collective-permute-start.18 = (f32[8,128]{1,0:T(8,128)S(1)}, f32[8,128]{1,0:T(8,128)S(1)}, u32[]{:S(2)}, u32[]{:S(2)}) collective-permute-start(f32[8,128]{1,0:T(8,128)S(1)} %get-tuple-element.53), channel_id=1, source_target_pairs={{0,1},{1,0},{2,3},{3,2},{4,5},{5,4},{6,7},{7,6},{8,9},{9,8},{10,11... | collective-permute-start | bytes 12296 | tf_op jit(solution)/shard_map/ppermute | solution.py:69
  210.6 0.7 copy-done.11
  211.7 8.1 %contrast.1 = f32[1024,768]{1,0:T(8,128)} custom-call(s32[2]{0:T(128)} %pad_add_fusion.place_ref, f32[128,768]{1,0:T(8,128)} %get-tuple-element.20.own_first, f32[384,768]{1,0:T(8,128)} %get-tuple-element.24.own_rest, f32[128,768]{1,0:T(8,128)} %copy-done.11, f32[384,768]{1,0:T(8,128)} %copy-done.4, f32[8,128]{1,0:T(8,128)} %sub.50.limit_ref, ...), custom_call_target="tpu_custom_call" | custom-call | flops 4718592 | bytes 7864320 | tf_op jit(solution)/shard_map/contrast/pallas_call | solution.py:359
  (91 shorter events, 10.5 us)
Async XLA Ops:
  6.5 9.5 %copy-start = (bf16[8,1024]{1,0:T(8,128)(2,1)S(1)}, bf16[8,1024]{1,0:T(8,128)(2,1)}, u32[]{:S(2)}) copy-start(bf16[8,1024]{1,0:T(8,128)(2,1)} %param.16) | copy-start | bytes 49156
  6.5 139.7 %collective-permute-start.8 = (bf16[8192,768]{1,0:T(8,128)(2,1)}, bf16[8192,768]{1,0:T(8,128)(2,1)}, u32[]{:S(2)}, u32[]{:S(2)}) collective-permute-start(bf16[8192,768]{1,0:T(8,128)(2,1)} %refs_3_.3), channel_id=1, source_target_pairs={{0,1},{1,0},{2,3},{3,2},{4,5},{5,4},{6,7},{7,6},{8,9},{9,8},{10,11... | collective-permute-start | bytes 37748744 | tf_op jit(solution)/shard_map/ppermute | solution.py:69
  10.1 11.0 %copy-start.18 = (bf16[8,256,1024]{2,1,0:T(8,128)(2,1)S(1)}, bf16[8,256,1024]{2,1,0:T(8,128)(2,1)}, u32[]{:S(2)}) copy-start(bf16[8,256,1024]{2,1,0:T(8,128)(2,1)} %param.15) | copy-start | bytes 12582916
  10.1 23.5 %collective-permute-start.2 = (bf16[64,2048]{1,0:T(8,128)(2,1)}, bf16[64,2048]{1,0:T(8,128)(2,1)S(1)}, u32[]{:S(2)}, u32[]{:S(2)}) collective-permute-start(bf16[64,2048]{1,0:T(8,128)(2,1)} %get-tuple-element.37), channel_id=1, source_target_pairs={{0,96},{32,0},{64,32},{96,64},{1,97},{33,1},{65,33},{97,65},{2,98}... | collective-permute-start | bytes 786440 | tf_op jit(solution)/shard_map/ppermute | solution.py:69
  13.9 19.6 %collective-permute-start.1 = (bf16[64,2048]{1,0:T(8,128)(2,1)}, bf16[64,2048]{1,0:T(8,128)(2,1)S(1)}, u32[]{:S(2)}, u32[]{:S(2)}) collective-permute-start(bf16[64,2048]{1,0:T(8,128)(2,1)} %get-tuple-element.38), channel_id=1, source_target_pairs={{0,64},{32,96},{64,0},{96,32},{1,65},{33,97},{65,1},{97,33},{2,66}... | collective-permute-start | bytes 786440 | tf_op jit(solution)/shard_map/ppermute | solution.py:69
  13.9 19.7 %collective-permute-start = (bf16[64,2048]{1,0:T(8,128)(2,1)S(1)}, bf16[64,2048]{1,0:T(8,128)(2,1)S(1)}, u32[]{:S(2)}, u32[]{:S(2)}) collective-permute-start(bf16[64,2048]{1,0:T(8,128)(2,1)S(1)} %get-tuple-element.36), channel_id=1, source_target_pairs={{0,32},{32,64},{64,96},{96,0},{1,33},{33,65},{65,97},{97,1},{2,34}... | collective-permute-start | bytes 786440 | tf_op jit(solution)/shard_map/ppermute | solution.py:69
  23.7 12.7 %copy-start.12 = (bf16[1024,64]{0,1:T(8,128)(2,1)S(1)}, bf16[1024,64]{0,1:T(8,128)(2,1)}, u32[]{:S(2)}) copy-start(bf16[1024,64]{0,1:T(8,128)(2,1)} %param.19) | copy-start | bytes 393220
  23.7 38.3 %all-to-all-start = ((bf16[64,128,128]{2,1,0:T(8,128)(2,1)}), bf16[64,128,128]{2,1,0:T(8,128)(2,1)S(1)}, u32[]{:S(2)}, u32[]{:S(2)}) async-start(bf16[64,128,128]{2,1,0:T(8,128)(2,1)} %bitcast.122), calls=%async_computation | async-start | bytes 4194304 | tf_op jit(solution)/shard_map/all_to_all | solution.py:428
  33.5 0.7 copy-start.8
  33.6 0.8 copy-start.9
  33.6 0.9 copy-start.10
  35.6 5.9 %collective-permute-start.3 = (bf16[4,64,2048]{2,1,0:T(8,128)(2,1)}, bf16[4,64,2048]{2,1,0:T(8,128)(2,1)S(1)}, u32[]{:S(2)}, u32[]{:S(2)}) collective-permute-start(bf16[4,64,2048]{2,1,0:T(8,128)(2,1)} %pad_maximum_fusion.1), channel_id=1, source_target_pairs={{0,1},{1,0},{2,3},{3,2},{4,5},{5,4},{6,7},{7,6},{8,9},{9,8},{10,11... | collective-permute-start | bytes 3145736 | tf_op jit(solution)/shard_map/ppermute | solution.py:69
  38.2 1.6 collective-permute-start.4
  62.1 1.3 copy-start.3
  68.8 3.9 %collective-permute-start.5 = (bf16[512,128]{1,0:T(8,128)(2,1)S(1)}, bf16[512,128]{1,0:T(8,128)(2,1)S(1)}, u32[]{:S(2)}, u32[]{:S(2)}) collective-permute-start(bf16[512,128]{1,0:T(8,128)(2,1)S(1)} %get-tuple-element.41), channel_id=1, source_target_pairs={{0,96},{32,0},{64,32},{96,64},{1,97},{33,1},{65,33},{97,65},{2,98}... | collective-permute-start | bytes 393224 | tf_op jit(solution)/shard_map/ppermute | solution.py:69
  69.6 5.4 %collective-permute-start.6 = (bf16[512,128]{1,0:T(8,128)(2,1)S(1)}, bf16[512,128]{1,0:T(8,128)(2,1)S(1)}, u32[]{:S(2)}, u32[]{:S(2)}) collective-permute-start(bf16[512,128]{1,0:T(8,128)(2,1)S(1)} %get-tuple-element.40), channel_id=1, source_target_pairs={{0,64},{32,96},{64,0},{96,32},{1,65},{33,97},{65,1},{97,33},{2,66}... | collective-permute-start | bytes 393224 | tf_op jit(solution)/shard_map/ppermute | solution.py:69
  70.4 5.9 %collective-permute-start.7 = (bf16[512,128]{1,0:T(8,128)(2,1)S(1)}, bf16[512,128]{1,0:T(8,128)(2,1)S(1)}, u32[]{:S(2)}, u32[]{:S(2)}) collective-permute-start(bf16[512,128]{1,0:T(8,128)(2,1)S(1)} %get-tuple-element.39), channel_id=1, source_target_pairs={{0,32},{32,64},{64,96},{96,0},{1,33},{33,65},{65,97},{97,1},{2,34}... | collective-permute-start | bytes 393224 | tf_op jit(solution)/shard_map/ppermute | solution.py:69
  72.7 3.6 %copy-start.13 = (bf16[512,128]{1,0:T(8,128)(2,1)}, bf16[512,128]{1,0:T(8,128)(2,1)S(1)}, u32[]{:S(2)}) copy-start(bf16[512,128]{1,0:T(8,128)(2,1)S(1)} %collective-permute-done.5.refs_0_) | copy-start | bytes 393220
  75.0 1.3 copy-start.14
  76.3 0.6 copy-start.15
  79.6 37.2 %all-to-all-start.1 = ((bf16[64,128,128]{2,1,0:T(8,128)(2,1)}), bf16[64,128,128]{2,1,0:T(8,128)(2,1)S(1)}, u32[]{:S(2)}, u32[]{:S(2)}) async-start(bf16[64,128,128]{2,1,0:T(8,128)(2,1)} %hidden.1), calls=%async_computation.1 | async-start | bytes 4194304 | tf_op jit(solution)/shard_map/all_to_all | solution.py:434
  88.9 48.2 %all-gather.2.cloned.1.call-start = ((), (), s32[]{:S(2)}) async-start(), calls=%async_computation.3 | async-start | bytes 2293760 | tf_op jit(solution)/shard_map/all_gather | solution.py:447
  116.9 26.4 %copy-start.2 = (bf16[64,128,128]{2,1,0:T(8,128)(2,1)}, bf16[64,128,128]{2,1,0:T(8,128)(2,1)S(1)}, u32[]{:S(2)}) copy-start(bf16[64,128,128]{2,1,0:T(8,128)(2,1)S(1)} %all-to-all-done.1.refs_0_) | copy-start | bytes 6291460
  118.4 27.8 %collective-permute-start.12 = (bf16[32,128,128]{2,1,0:T(8,128)(2,1)}, bf16[32,128,128]{2,1,0:T(8,128)(2,1)S(1)}, u32[]{:S(2)}, u32[]{:S(2)}) collective-permute-start(bf16[32,128,128]{2,1,0:T(8,128)(2,1)} %get-tuple-element.31), channel_id=1, source_target_pairs={{0,6},{1,97},{2,0},{3,99},{4,2},{5,101},{6,4},{7,103},{8,14},{9,10... | collective-permute-start | bytes 3145736 | tf_op jit(solution)/shard_map/ppermute | solution.py:81
  119.2 40.9 %collective-permute-start.13 = (bf16[32,128,128]{2,1,0:T(8,128)(2,1)}, bf16[32,128,128]{2,1,0:T(8,128)(2,1)}, u32[]{:S(2)}, u32[]{:S(2)}) collective-permute-start(bf16[32,128,128]{2,1,0:T(8,128)(2,1)} %get-tuple-element.31), channel_id=1, source_target_pairs={{0,24},{1,9},{2,26},{3,11},{4,28},{5,13},{6,30},{7,15},{8,0},{9,17... | collective-permute-start | bytes 3145736 | tf_op jit(solution)/shard_map/ppermute | solution.py:81
  119.6 40.5 %collective-permute-start.14 = (bf16[32,128,128]{2,1,0:T(8,128)(2,1)}, bf16[32,128,128]{2,1,0:T(8,128)(2,1)}, u32[]{:S(2)}, u32[]{:S(2)}) collective-permute-start(bf16[32,128,128]{2,1,0:T(8,128)(2,1)} %get-tuple-element.31), channel_id=1, source_target_pairs={{0,2},{1,33},{2,4},{3,35},{4,6},{5,37},{6,0},{7,39},{8,10},{9,41},... | collective-permute-start | bytes 3145736 | tf_op jit(solution)/shard_map/ppermute | solution.py:81
  143.9 1.3 collective-permute-start.17
  145.2 24.8 %collective-permute-start.9 = (bf16[32,128,128]{2,1,0:T(8,128)(2,1)}, bf16[32,128,128]{2,1,0:T(8,128)(2,1)S(1)}, u32[]{:S(2)}, u32[]{:S(2)}) collective-permute-start(bf16[32,128,128]{2,1,0:T(8,128)(2,1)} %get-tuple-element.32), channel_id=1, source_target_pairs={{0,6},{1,97},{2,0},{3,99},{4,2},{5,101},{6,4},{7,103},{8,14},{9,10... | collective-permute-start | bytes 3145736 | tf_op jit(solution)/shard_map/ppermute | solution.py:81
  146.3 13.8 %copy-start.5 = (bf16[32,128,128]{2,1,0:T(8,128)(2,1)}, bf16[32,128,128]{2,1,0:T(8,128)(2,1)S(1)}, u32[]{:S(2)}) copy-start(bf16[32,128,128]{2,1,0:T(8,128)(2,1)S(1)} %collective-permute-done.12.refs_0_) | copy-start | bytes 3145732
  146.3 23.7 %collective-permute-start.10 = (bf16[32,128,128]{2,1,0:T(8,128)(2,1)}, bf16[32,128,128]{2,1,0:T(8,128)(2,1)S(1)}, u32[]{:S(2)}, u32[]{:S(2)}) collective-permute-start(bf16[32,128,128]{2,1,0:T(8,128)(2,1)} %get-tuple-element.32), channel_id=1, source_target_pairs={{0,24},{1,9},{2,26},{3,11},{4,28},{5,13},{6,30},{7,15},{8,0},{9,17... | collective-permute-start | bytes 3145736 | tf_op jit(solution)/shard_map/ppermute | solution.py:81
  146.3 23.7 %collective-permute-start.11 = (bf16[32,128,128]{2,1,0:T(8,128)(2,1)}, bf16[32,128,128]{2,1,0:T(8,128)(2,1)}, u32[]{:S(2)}, u32[]{:S(2)}) collective-permute-start(bf16[32,128,128]{2,1,0:T(8,128)(2,1)} %get-tuple-element.32), channel_id=1, source_target_pairs={{0,2},{1,33},{2,4},{3,35},{4,6},{5,37},{6,0},{7,39},{8,10},{9,41},... | collective-permute-start | bytes 3145736 | tf_op jit(solution)/shard_map/ppermute | solution.py:81
  170.0 1.0 copy-start.6
  170.0 1.4 copy-start.7
  171.4 12.3 %copy-start.17 = (f32[2,128]{1,0:T(2,128)S(1)}, f32[2,128]{1,0:T(2,128)}, u32[]{:S(2)}) copy-start(f32[2,128]{1,0:T(2,128)} %get-tuple-element.27) | copy-start | bytes 3076
  171.4 22.4 %copy-start.16 = (s32[1024]{0:T(1024)S(1)}, s32[1024]{0:T(1024)}, u32[]{:S(2)}) copy-start(s32[1024]{0:T(1024)} %param.25) | copy-start | bytes 12292
  171.4 22.4 %copy-start.19 = (f32[128,768]{1,0:T(8,128)S(1)}, f32[128,768]{1,0:T(8,128)}, u32[]{:S(2)}) copy-start(f32[128,768]{1,0:T(8,128)} %get-tuple-element.25) | copy-start | bytes 1179652
  185.2 19.7 %all-to-all-start.2 = ((f32[64,16,128]{2,1,0:T(8,128)}), f32[64,16,128]{2,1,0:T(8,128)S(1)}, u32[]{:S(2)}, u32[]{:S(2)}) async-start(f32[64,16,128]{2,1,0:T(8,128)} %broadcast_in_dim.47), calls=%async_computation.2 | async-start | bytes 1048576 | tf_op jit(solution)/shard_map/all_to_all | solution.py:465
  193.8 16.8 %collective-permute-start.15 = (f32[128,768]{1,0:T(8,128)S(1)}, f32[128,768]{1,0:T(8,128)S(1)}, u32[]{:S(2)}, u32[]{:S(2)}) collective-permute-start(f32[128,768]{1,0:T(8,128)S(1)} %copy-done.19), channel_id=1, source_target_pairs={{0,1},{1,0},{2,3},{3,2},{4,5},{5,4},{6,7},{7,6},{8,9},{9,8},{10,11... | collective-permute-start | bytes 1179656 | tf_op jit(solution)/shard_map/ppermute | solution.py:69
  195.8 14.8 %collective-permute-start.16 = (f32[384,768]{1,0:T(8,128)}, f32[384,768]{1,0:T(8,128)S(1)}, u32[]{:S(2)}, u32[]{:S(2)}) collective-permute-start(f32[384,768]{1,0:T(8,128)} %get-tuple-element.26), channel_id=1, source_target_pairs={{0,1},{1,0},{2,3},{3,2},{4,5},{5,4},{6,7},{7,6},{8,9},{9,8},{10,11... | collective-permute-start | bytes 3538952 | tf_op jit(solution)/shard_map/ppermute | solution.py:69
  205.3 4.1 %collective-permute-start.18 = (f32[8,128]{1,0:T(8,128)S(1)}, f32[8,128]{1,0:T(8,128)S(1)}, u32[]{:S(2)}, u32[]{:S(2)}) collective-permute-start(f32[8,128]{1,0:T(8,128)S(1)} %get-tuple-element.53), channel_id=1, source_target_pairs={{0,1},{1,0},{2,3},{3,2},{4,5},{5,4},{6,7},{7,6},{8,9},{9,8},{10,11... | collective-permute-start | bytes 12296 | tf_op jit(solution)/shard_map/ppermute | solution.py:69
  210.6 0.8 copy-start.11
  210.6 1.1 copy-start.4
  210.6 9.2 %copy-start.1 = (bf16[8,1024]{1,0:T(8,128)(2,1)S(1)}, bf16[8,1024]{1,0:T(8,128)(2,1)}, u32[]{:S(2)}) copy-start(bf16[8,1024]{1,0:T(8,128)(2,1)} %param.16) | copy-start | bytes 49156
Sparse Core Ops, SparseCore 0:
  91.4 45.6 all-gather.1

commit v2 on v1

--- a/solution.py
+++ b/solution.py
@@ -20,7 +20,6 @@
 CHIPS = ("z", "y", "x")
 ALL = ("z", "y", "x", "core")
 LINE = 128
-VMEM = 56 * 1024 * 1024
 
 
 def attend(queries, cache_keys, cache_values, new_keys, new_values, lengths):
@@ -85,8 +84,8 @@
     return (x + 2 * y + z) % 4
 
 
-def params():
-    return pltpu.CompilerParams(vmem_limit_bytes=VMEM)
+def params(mebibytes):
+    return pltpu.CompilerParams(vmem_limit_bytes=mebibytes * 1024 * 1024)
 
 
 def laid_along_lanes(largest, totals):
@@ -94,7 +93,7 @@
     return jnp.transpose(jnp.where(lane == 0, largest, totals))[:2]
 
 
-def projection_kernel(left_ref, weight_ref, base_ref, total_ref, sent_ref):
+def projection_kernel(left_ref, weight_ref, base_ref, total_ref, *sent):
     product = lax.dot_general(
         left_ref[...],
         weight_ref[...],
@@ -102,8 +101,8 @@
         preferred_element_type=jnp.float32,
     )
     total_ref[...] = base_ref[...].astype(jnp.float32) + product[:, :LINE]
-    for step in range(sent_ref.shape[0]):
-        sent_ref[step] = product[:, (step + 1) * LINE : (step + 2) * LINE].astype(jnp.bfloat16)
+    for step, sent_ref in enumerate(sent, 1):
+        sent_ref[...] = product[:, step * LINE : (step + 1) * LINE].astype(jnp.bfloat16)
 
 
 def project(left, weight, base):
@@ -111,11 +110,9 @@
     columns = weight.shape[0]
     return pl.pallas_call(
         projection_kernel,
-        out_shape=[
-            jax.ShapeDtypeStruct((rows, LINE), jnp.float32),
-            jax.ShapeDtypeStruct((columns // LINE - 1, rows, LINE), jnp.bfloat16),
-        ],
-        compiler_params=params(),
+        out_shape=[jax.ShapeDtypeStruct((rows, LINE), jnp.float32)]
+        + [jax.ShapeDtypeStruct((rows, LINE), jnp.bfloat16)] * (columns // LINE - 1),
+        compiler_params=params(16),
         cost_estimate=pl.CostEstimate(
             flops=2 * rows * depth * columns,
             bytes_accessed=2 * (rows + columns) * depth,
@@ -125,21 +122,38 @@
     )(left, weight, base)
 
 
-def hidden_kernel(places, total_ref, *refs):
-    parts, out_ref = refs[:-1], refs[-1]
+def hidden_kernel(turns, total_ref, *refs):
+    parts, out_ref, hidden_ref, sem = refs[:-3], refs[-3], refs[-2], refs[-1]
     total = total_ref[...]
     for part in parts:
         total = total + part[...].astype(jnp.float32)
     hidden = total.astype(jnp.bfloat16)
-    for target, quarter in enumerate(places):
-        out_ref[target] = hidden[quarter * LINE : quarter * LINE + LINE]
-
-
-def hidden_copies(total, parts, places):
-    return pl.pallas_call(
-        functools.partial(hidden_kernel, places),
-        out_shape=jax.ShapeDtypeStruct((len(places), LINE, LINE), jnp.bfloat16),
-        compiler_params=params(),
+    rows = hidden.shape[0]
+    hidden_ref[:rows] = hidden
+    hidden_ref[rows:] = hidden
+    copies = [
+        pltpu.make_async_copy(
+            hidden_ref.at[pl.ds(turn * LINE, rows)], out_ref.at[line], sem.at[line]
+        )
+        for line, turn in enumerate(turns)
+    ]
+    for copy in copies:
+        copy.start()
+    for copy in copies:
+        copy.wait()
+
+
+def hidden_copies(total, parts, turns):
+    rows = total.shape[0]
+    return pl.pallas_call(
+        functools.partial(hidden_kernel, turns),
+        out_specs=pl.BlockSpec(memory_space=pl.ANY),
+        out_shape=jax.ShapeDtypeStruct((len(turns), rows, LINE), jnp.bfloat16),
+        scratch_shapes=[
+            pltpu.VMEM((2 * rows, LINE), jnp.bfloat16),
+            pltpu.SemaphoreType.DMA((len(turns),)),
+        ],
+        compiler_params=params(60),
         name="hidden",
     )(total, *parts)
 
@@ -230,7 +244,7 @@
         out_specs=[whole, whole, last_spec],
         out_shape=[logits, logits, last],
         scratch_shapes=scratch,
-        compiler_params=params(),
+        compiler_params=params(26),
         cost_estimate=pl.CostEstimate(
             flops=4 * rows * blocks * LINE * columns,
             bytes_accessed=4 * blocks * LINE * columns,
@@ -277,7 +291,7 @@
             jax.ShapeDtypeStruct((rows, columns), jnp.bfloat16),
             jax.ShapeDtypeStruct((rows // tall, 2, 2, LINE), jnp.float32),
         ],
-        compiler_params=params(),
+        compiler_params=params(16),
         cost_estimate=pl.CostEstimate(
             flops=2 * rows * width * columns,
             bytes_accessed=2 * (rows * width + width * columns + rows * columns),
@@ -293,85 +307,173 @@
     return largest, totals
 
 
+def spread_kernel(
+    place_ref, first_ref, rest_ref, amateur_ref, out_ref, stats_ref, group_ref, sem
+):
+    quarters = amateur_ref.shape[0] // 2
+    for piece in range(quarters):
+        at = pl.ds(2 * lax.rem(place_ref[0] + piece, quarters), 2)
+        stats_ref[at] = first_ref[...] if piece == 0 else rest_ref[2 * piece - 2 : 2 * piece]
+    stats_ref[2 * quarters :] = amateur_ref[...]
+    for target in range(group_ref.shape[0]):
+        group_ref[target] = stats_ref[...]
+    many = group_ref.shape[0]
+    copies = [
+        pltpu.make_async_copy(group_ref, out_ref.at[pl.ds(at, many)], sem.at[at // many])
+        for at in range(0, out_ref.shape[0], many)
+    ]
+    for copy in copies:
+        copy.start()
+    for copy in copies:
+        copy.wait()
+
+
+def spread(place, first, rest, amateur, targets):
+    rows = 2 * amateur.shape[0]
+    vmem = pl.BlockSpec(memory_space=pltpu.VMEM)
+    return pl.pallas_call(
+        spread_kernel,
+        in_specs=[pl.BlockSpec(memory_space=pltpu.SMEM)] + [vmem] * 3,
+        out_specs=pl.BlockSpec(memory_space=pl.ANY),
+        out_shape=jax.ShapeDtypeStruct((targets, rows, LINE), jnp.float32),
+        scratch_shapes=[
+            pltpu.VMEM((rows, LINE), jnp.float32),
+            pltpu.VMEM((8, rows, LINE), jnp.float32),
+            pltpu.SemaphoreType.DMA((targets // 8,)),
+        ],
+        compiler_params=params(60),
+        name="spread_stats",
+    )(place, first, rest, amateur)
+
+
+def merge_kernel(parts_ref, out_ref):
+    parts = parts_ref[...]
+    largest = jnp.max(parts, axis=0)
+    quarters = out_ref.shape[0] // 2
+    tops, sums = [], []
+    for tile in range(2 * quarters):
+        top = largest[2 * tile : 2 * tile + 1]
+        scales = jnp.exp(parts[:, 2 * tile] - top)
+        tops.append(top)
+        sums.append(
+            top + jnp.log(jnp.sum(parts[:, 2 * tile + 1] * scales, axis=0, keepdims=True))
+        )
+    shifts = [sums[tile] - sums[quarters + tile] for tile in range(quarters)]
+    out_ref[...] = jnp.concatenate(tops[:quarters] + shifts, axis=0)
+
+
+def merge(parts):
+    return pl.pallas_call(
+        merge_kernel,
+        out_shape=jax.ShapeDtypeStruct((parts.shape[1] // 2, LINE), jnp.float32),
+        compiler_params=params(8),
+        name="merge_stats",
+    )(parts)
+
+
 def column_of(row):
     return jnp.transpose(jnp.broadcast_to(row, (LINE, LINE)))
 
 
 def contrast_kernel(
     place_ref,
+    mine_ref,
+    theirs_ref,
+    limit_ref,
+    own_first_in,
+    own_rest_in,
+    other_first_in,
+    other_rest_in,
+    amateur_in,
+    out_ref,
     own_first,
     own_rest,
     other_first,
     other_rest,
-    limit_ref,
-    shift_ref,
     amateur_ref,
-    out_ref,
-    limit_col,
-    shift_col,
+    result_ref,
+    sem,
+    sem_in,
 ):
-    step = pl.program_id(0)
-    tiles = limit_ref.shape[0]
-    rows = own_first.shape[0]
-
-    @pl.when(step == 0)
-    def _():
-        for tile in range(tiles):
-            at = slice(tile * LINE, tile * LINE + LINE)
-            limit_col[at] = column_of(limit_ref[tile : tile + 1])
-            shift_col[at] = column_of(shift_ref[tile : tile + 1])
-
-    def work(own_ref, other_ref):
-        first = place_ref[1] == 0
-        own, other = own_ref[...], other_ref[...]
-        base = lax.rem(place_ref[0] + step // 2, 4) * LINE + lax.rem(step, 2) * rows
-        planes = []
-        for plane, expert in enumerate(
-            (jnp.where(first, own, other), jnp.where(first, other, own))
-        ):
-            at = pl.ds(pl.multiple_of(base + plane * tiles // 2 * LINE, 8), rows)
-            planes.append(
-                expert - shift_col[at, :1] + jnp.minimum(expert + limit_col[at, :1], 0.0)
+    arrivals = [
+        pltpu.make_async_copy(source, target, sem_in.at[i])
+        for i, (source, target) in enumerate(
+            (
+                (own_first_in, own_first),
+                (other_first_in, other_first),
+                (amateur_in, amateur_ref),
+                (own_rest_in, own_rest),
+                (other_rest_in, other_rest),
             )
-        pieces = []
-        for source in range(0, rows, 8):
-            pieces += [plane[source : source + 8] for plane in planes]
-        out_ref[...] = jnp.concatenate(pieces, axis=0) - amateur_ref[...].astype(jnp.float32)
-
-    @pl.when(step < 2)
-    def _():
-        work(own_first, other_first)
-
-    @pl.when(step >= 2)
-    def _():
-        work(own_rest, other_rest)
-
-
-def contrast(place, own, other, limit, shift, amateur):
+        )
+    ]
+    for copy in arrivals:
+        copy.start()
+    core = place_ref[1]
+    first = core == 0
+    quarters = limit_ref.shape[0] // 2
+    tall = 2 * LINE
+    step_rows = 32
+    copies = []
+    for piece in range(quarters):
+        quarter = lax.rem(place_ref[0] + piece, quarters)
+        start = pl.multiple_of(quarter * tall, tall)
+        sides = []
+        for stats, plane in ((mine_ref, core), (theirs_ref, 1 - core)):
+            top = stats[pl.ds(quarter, 1)]
+            limit = limit_ref[pl.ds(plane * quarters + quarter, 1)]
+            sides.append(
+                (column_of(limit - top), column_of(stats[pl.ds(quarters + quarter, 1)]))
+            )
+        for copy in (arrivals[:3], arrivals[3:], (), ())[piece]:
+            copy.wait()
+        experts = (own_first, other_first) if piece == 0 else (own_rest, other_rest)
+        offset = 0 if piece == 0 else (piece - 1) * LINE
+        for at in range(0, LINE, step_rows):
+            rows = slice(at, at + step_rows)
+            own, other = (
+                expert - shift[rows, :1] + jnp.minimum(expert + limit[rows, :1], 0.0)
+                for expert, (limit, shift) in zip(
+                    (ref[offset + at : offset + at + step_rows] for ref in experts), sides
+                )
+            )
+            planes = (jnp.where(first, own, other), jnp.where(first, other, own))
+            mixed = jnp.concatenate(
+                [plane[i : i + 8] for i in range(0, step_rows, 8) for plane in planes], axis=0
+            )
+            amateur = amateur_ref[pl.ds(pl.multiple_of(start + 2 * at, 2 * step_rows), 2 * step_rows)]
+            result_ref[piece, 2 * at : 2 * at + 2 * step_rows] = mixed - amateur.astype(jnp.float32)
+        copy = pltpu.make_async_copy(
+            result_ref.at[piece], out_ref.at[pl.ds(start, tall)], sem.at[piece]
+        )
+        copy.start()
+        copies.append(copy)
+    for copy in copies:
+        copy.wait()
+
+
+def contrast(place, mine, theirs, limit, own, other, amateur):
     rows, columns = amateur.shape
-    half = LINE // 2
-    first = pl.BlockSpec((half, columns), lambda i, place: (jnp.minimum(i, 1), 0))
-    rest = pl.BlockSpec((half, columns), lambda i, place: (jnp.maximum(i - 2, 0), 0))
-    whole = pl.BlockSpec((rows // LINE, LINE), lambda i, place: (0, 0))
-    spread = pl.BlockSpec(
-        (LINE, columns), lambda i, place: (lax.rem(place[0] + i // 2, 4) * 2 + lax.rem(i, 2), 0)
-    )
+    vmem = pl.BlockSpec(memory_space=pltpu.VMEM)
     return pl.pallas_call(
         contrast_kernel,
-        grid_spec=pltpu.PrefetchScalarGridSpec(
-            num_scalar_prefetch=1,
-            grid=(8,),
-            in_specs=[first, rest, first, rest, whole, whole, spread],
-            out_specs=spread,
-            scratch_shapes=[pltpu.VMEM((rows, LINE), jnp.float32)] * 2,
-        ),
+        in_specs=[pl.BlockSpec(memory_space=pltpu.SMEM)]
+        + [vmem] * 3
+        + [pl.BlockSpec(memory_space=pl.ANY)] * 5,
+        out_specs=pl.BlockSpec(memory_space=pl.ANY),
         out_shape=jax.ShapeDtypeStruct((rows, columns), jnp.float32),
-        compiler_params=params(),
+        scratch_shapes=[pltpu.VMEM(a.shape, a.dtype) for a in (*own, *other, amateur)]
+        + [
+            pltpu.VMEM((rows // (2 * LINE), 2 * LINE, columns), jnp.float32),
+            pltpu.SemaphoreType.DMA((rows // (2 * LINE),)),
+            pltpu.SemaphoreType.DMA((5,)),
+        ],
+        compiler_params=params(60),
         cost_estimate=pl.CostEstimate(
             flops=6 * rows * columns, bytes_accessed=10 * rows * columns, transcendentals=0
         ),
         name="contrast",
-    )(place, own[0], own[1], other[0], other[1], limit, shift, amateur)
+    )(place, mine, theirs, limit, own[0], own[1], other[0], other[1], amateur)
 
 
 def body(
@@ -401,6 +503,15 @@
     heads = QH // depth
     quarter = quarter_of(z, y, x)
 
+    attention = attend(queries, cache_keys, cache_values, new_keys, new_values, lengths)
+    slabs = attention.reshape(per, depth, heads, LINE).transpose(1, 2, 0, 3)
+    copies = jnp.broadcast_to(
+        slabs.reshape(depth, 1, heads * per, LINE), (depth, chips // depth, heads * per, LINE)
+    ).reshape(chips * heads * per, LINE)
+    copies, residual = lax.optimization_barrier((copies, residual))
+    everyone = lax.all_gather(amateur_hidden, "z", axis=0, tiled=True)
+    arrived = lax.all_to_all(copies, CHIPS, split_axis=0, concat_axis=0, tiled=True)
+
     other_weight = shift(head_weight, "core", 1)
 
     turned = out_weight.T
@@ -420,70 +531,49 @@
     base = jnp.concatenate([jnp.where(first, kept, given), jnp.where(first, given, kept)], axis=0)
     base = base.reshape(-1, chips * per).T
 
-    attention = attend(queries, cache_keys, cache_values, new_keys, new_values, lengths)
-    slabs = attention.reshape(per, depth, heads, LINE).transpose(1, 2, 0, 3)
-    copies = jnp.broadcast_to(
-        slabs.reshape(depth, 1, heads * per, LINE), (depth, chips // depth, heads * per, LINE)
-    ).reshape(chips * heads * per, LINE)
-    arrived = lax.all_to_all(copies, CHIPS, split_axis=0, concat_axis=0, tiled=True)
     left = arrived.reshape(chips, heads, per, LINE).transpose(0, 2, 1, 3).reshape(chips * per, slab)
-    total, sent = project(left, projection, base)
-    parts = [shift(sent[step - 1], "z", -step) for step in range(1, depth)]
-
-    places = [quarter_of(*place) for place in np.ndindex(*sizes)]
-    quarters = lax.all_to_all(
-        hidden_copies(total, parts, places), CHIPS, split_axis=0, concat_axis=0, tiled=True
-    )
-    moves = (
-        ((0, 0, -1), (-1, 0, 0)),
-        ((0, -1, 0), (0, 1, 0)),
-        ((0, 0, 1), (1, 0, 0)),
-    )
-    half = chips // 2
-    halves = [
-        [shift_chips(quarters[at : at + half], move) for move in moves] for at in (0, half)
-    ]
-
-    everyone = lax.all_gather(amateur_hidden, "z", axis=0, tiled=True)
+    total, *sent = project(left, projection, base)
+    parts = [shift(part, "z", -step) for step, part in enumerate(sent, 1)]
+    total, everyone = lax.optimization_barrier((total, everyone))
+
+    turns = [quarter_of(*place, 0) for place in np.ndindex(*sizes[:2])]
+    copies = hidden_copies(total, parts, turns).reshape(chips, LINE, LINE)
+    quarters = lax.all_to_all(copies, CHIPS, split_axis=0, concat_axis=0, tiled=True)
     amateur, amateur_stats = amateur_logits(everyone, amateur_head, z.reshape(1), columns)
     by_plane = amateur_stats.transpose(1, 0, 2, 3)
     kept = lax.dynamic_index_in_dim(by_plane, core, 0, False)
     given = shift(lax.dynamic_index_in_dim(by_plane, 1 - core, 0, False), "core", 1)
     amateur_chip = jnp.stack(merged(jnp.stack([kept, given])), axis=1)
 
+    limit = thresholds.astype(jnp.float32).reshape(chips, 2, per).transpose(1, 0, 2)
+    limit = limit.reshape(rows // LINE, LINE) * LOG_TWO
+    place = jnp.stack([quarter, core])
+    quarters, amateur, amateur_chip, limit, place = lax.optimization_barrier(
+        (quarters, amateur, amateur_chip, limit, place)
+    )
+    moves = (
+        ((0, 0, -1), (-1, 0, 0)),
+        ((0, -1, 0), (0, 1, 0)),
+        ((0, 0, 1), (1, 0, 0)),
+    )
+    half = chips * 5 // 8
+
     gain_lines = gain.reshape(-1, LINE)
+    halves = [[shift_chips(quarters[:half], move) for move in moves]]
+    halves.append([shift_chips(quarters[half:], move) for move in moves[:2]])
     own_0, other_0, stats_0 = head([quarters], head_weight, other_weight, gain_lines)
+    later, own_0 = lax.optimization_barrier((quarters[half:], own_0))
+    halves[1].append(shift_chips(later, moves[2]))
     begun = head(halves[0], head_weight, other_weight, gain_lines, finished=False)
     own_1, other_1, stats_1 = head(
         halves[1], head_weight, other_weight, gain_lines, start=half, before=begun
     )
     crossed = [shift(logits, "core", 1) for logits in (other_0, other_1)]
 
-    stats = jnp.concatenate([stats_0, stats_1] * 2).reshape(8, 2, LINE)
-    stats = lax.dynamic_slice_in_dim(stats, lax.rem(4 - quarter, 4), 4, 0)
-    stats = jnp.concatenate([stats, amateur_chip])
-    everywhere = lax.all_to_all(
-        jnp.broadcast_to(stats[None], (chips,) + stats.shape).reshape(-1, LINE),
-        CHIPS,
-        split_axis=0,
-        concat_axis=0,
-        tiled=True,
-    )
-    largest, totals = merged(everywhere.reshape((chips,) + stats.shape))
-    lse = largest + jnp.log(totals)
-    mine = jnp.concatenate([largest[:4], lse[:4] - lse[4:]])
+    copies = spread(place, stats_0, stats_1, amateur_chip.reshape(-1, LINE), chips)
+    mine = merge(lax.all_to_all(copies, CHIPS, split_axis=0, concat_axis=0, tiled=True))
     theirs = shift(mine, "core", 1)
-    both = jnp.where(first, jnp.stack([mine, theirs]), jnp.stack([theirs, mine]))
-    limit = thresholds.astype(jnp.float32).reshape(chips, 2, per).transpose(1, 0, 2)
-    limit = limit.reshape(rows // LINE, LINE) * LOG_TWO - both[:, :4].reshape(rows // LINE, LINE)
-    return contrast(
-        jnp.stack([quarter, core]),
-        (own_0, own_1),
-        crossed,
-        limit,
-        both[:, 4:].reshape(rows // LINE, LINE),
-        amateur,
-    )
+    return contrast(place, mine, theirs, limit, (own_0, own_1), crossed, amateur)
 
 
 def solution(mesh):

time: 228 us -> 196 us (0.86)
  waiting for transfers between devices: 79.3 us -> 55.1 us
  Pallas kernels: 56.6 us -> 39.5 us
  local copies, waits for them, and re-layouts: 17.7 us -> 26.4 us
  starting transfers between devices: 45.6 us -> 49.8 us
  other arithmetic: 8.29 us -> 5.45 us
    all_to_all x2 -> x0, waiting for transfers between devices: 36.3 us -> none  [the longest x1 27.2 us: body(): lax.all_to_all(hidden_copies(total, parts, places), CHIPS, split_axis=0,...]
    all_to_all x1 -> x3, waiting for transfers between devices: 17.7 us -> 46.2 us  [body(): lax.all_to_all(copies, CHIPS, split_axis=0, concat_axis=0, tiled=True)]
    all_to_all x2 -> x0, starting transfers between devices: 17.7 us -> none  [the longest x1 9.25 us: body(): lax.all_to_all(hidden_copies(total, parts, places), CHIPS, split_axis=0,...]
    all_to_all x1 -> x3, starting transfers between devices: 9.78 us -> 26.4 us  [body(): lax.all_to_all(copies, CHIPS, split_axis=0, concat_axis=0, tiled=True)]
    all_gather x1, waiting for transfers between devices: 16.4 us -> 2.15 us  [body(): everyone = lax.all_gather(amateur_hidden, 'z', axis=0, tiled=True)]
    unnamed x41 -> x52, local copies, waits for them, and re-layouts: 6.18 us -> 19.8 us
    pallas_call x3, Pallas kernels: 35.4 us -> 24.5 us  [head(): pl.pallas_call(functools.partial(head_kernel, pieces, steps, features, re...]
    ppermute x13, starting transfers between devices: 14.3 us -> 19.5 us  [shift(): return lax.ppermute(x, axis, [(i, (i + step) % size) for i in range(size)])]
  transfers between devices with their start and end apart: 23 -> 23, of which waited for: 9 -> 10; matrix products, arithmetic and copies ran while one was open for 11% -> 9% of each run, Pallas kernels for 16% -> 14%
where the time goes in v2:
time: 196 us; the launch traced here: 195 us
  waiting for transfers between devices  55.1 us (28%)
  starting transfers between devices  49.8 us (25%)
  Pallas kernels  39.5 us (20%)
  local copies, waits for them, and re-layouts  26.4 us (13%)
  between operations  13.9 us (7%)
  other arithmetic  5.45 us (3%)
  matrix products  4.55 us (2%)
    all_to_all x3, waiting for transfers between devices, body(): lax.all_to_all(copies, CHIPS, split_axis=0, concat_axis=0, tiled=True)  46.2 us
    all_to_all x3, starting transfers between devices, body(): lax.all_to_all(copies, CHIPS, split_axis=0, concat_axis=0, tiled=True)  26.4 us
    pallas_call x3, Pallas kernels, head(): pl.pallas_call(functools.partial(head_kernel, pieces, steps, features, re...  24.5 us
    unnamed x52, local copies, waits for them, and re-layouts  19.8 us
    ppermute x13, starting transfers between devices, shift(): return lax.ppermute(x, axis, [(i, (i + step) % size) for i in range(size)])  19.5 us
    ppermute x13, waiting for transfers between devices, shift(): return lax.ppermute(x, axis, [(i, (i + step) % size) for i in range(size)])  6.31 us
    pallas_call x1, Pallas kernels, contrast(): pl.pallas_call(contrast_kernel, in_specs=[pl.BlockSpec(memory_space=pltpu...  5.03 us
    pallas_call x1, Pallas kernels, amateur_logits(): pl.pallas_call(amateur_kernel, grid_spec=pltpu.PrefetchScalarGridSpec(num...  4.06 us
  transfers between devices with their start and end apart: 23, of which 10 were waited for; matrix products, arithmetic and copies ran while one was open for 9% of the time, Pallas kernels for 14%

profile of v2, /device:TPU:1, one launch (start us, length us, event | category | flops | bytes accessed | tf_op | source)
XLA Modules:
  0.0 194.6 jit_solution(7980126553064899546)
XLA Ops:
  6.5 1.5 collective-permute-start.9
  8.0 2.1 %dynamic-slice_bitcast_fusion.3 = (bf16[1,64,2048]{2,1,0:T(8,128)(2,1)S(1)}, bf16[64,2048]{1,0:T(8,128)(2,1)}, bf16[64,2048]{1,0:T(8,128)(2,1)S(1)}, bf16[64,2048]{1,0:T(8,128)(2,1)}) fusion(bf16[8192,64]{0,1:T(8,128)(2,1)} %param.21, s32[]{:T(128)S(6)} %select_n.63, s32[]{:T(128)S(6)} %select_n.64, s32[]{:T(128)S(6)} %select_n.66, s32[]{:T(128)S(6)} %select_n.65), kind=kLoop, calls=%fused_computation.20 | loop fusion | bytes 2097168 | tf_op jit(solution)/shard_map/stack | solution.py:522
  10.1 1.7 collective-permute-start
  11.9 3.3 %collective-permute-start.1 = (bf16[64,2048]{1,0:T(8,128)(2,1)}, bf16[64,2048]{1,0:T(8,128)(2,1)S(1)}, u32[]{:S(2)}, u32[]{:S(2)}) collective-permute-start(bf16[64,2048]{1,0:T(8,128)(2,1)} %get-tuple-element.62), channel_id=1, source_target_pairs={{0,64},{32,96},{64,0},{96,32},{1,65},{33,97},{65,1},{97,33},{2,66}... | collective-permute-start | bytes 786440 | tf_op jit(solution)/shard_map/ppermute | solution.py:68
  15.2 0.7 collective-permute-start.2
  16.2 3.6 %fusion.31 = (f32[8,8,8]{2,1,0:T(8,128)S(1)}, f32[8,8,8,256]{3,2,1,0:T(8,128)S(1)}) fusion(bf16[8,8,8,128]{3,0,2,1:T(8,128)(2,1)S(1)} %bitcast.113, pred[8,256]{1,0:T(8,128)(4,1)S(1)} %iota_compare_fusion, bf16[8,256,1024]{2,1,0:T(8,128)(2,1)} %param.14), kind=kOutput, calls=%fused_computation.52 | convolution fusion | flops 33947136 | bytes 4853760 | tf_op jit(solution)/shard_map/rkgd,rlkd->rkgl/dot_general | solution.py:35
  20.2 0.7 fusion.15
  21.1 1.8 broadcast_in_dim.36
  22.9 8.1 %all-to-all-start = ((bf16[64,128,128]{2,1,0:T(8,128)(2,1)}), bf16[64,128,128]{2,1,0:T(8,128)(2,1)S(1)}, u32[]{:S(2)}, u32[]{:S(2)}) async-start(bf16[64,128,128]{2,1,0:T(8,128)(2,1)} %bitcast.101), calls=%async_computation | async-start | bytes 4194304 | tf_op jit(solution)/shard_map/all_to_all | solution.py:513
  31.1 1.1 pad_maximum_fusion.1
  32.2 1.2 collective-permute-start.3
  33.6 2.3 %collective-permute-done.4 = bf16[64,64,8]{0,2,1:T(8,128)(2,1)} collective-permute-done((bf16[64,64,8]{0,2,1:T(8,128)(2,1)S(1)}, bf16[64,64,8]{0,2,1:T(8,128)(2,1)}, u32[]{:S(2)}, u32[]{:S(2)}) %collective-permute-start.4) | collective-permute-done | bytes 65568 | tf_op jit(solution)/shard_map/ppermute | solution.py:68
  36.0 0.9 bitcast_select_fusion.1
  37.0 1.4 select_bitcast_fusion.1
  38.6 1.4 copy.27
  40.1 19.2 %all-to-all-done = bf16[64,128,128]{2,1,0:T(8,128)(2,1)S(1)} async-done(((bf16[64,128,128]{2,1,0:T(8,128)(2,1)}), bf16[64,128,128]{2,1,0:T(8,128)(2,1)S(1)}, u32[]{:S(2)}, u32[]{:S(2)}) %all-to-all-start) | async-done | bytes 2097184 | tf_op jit(solution)/shard_map/all_to_all | solution.py:513
  59.3 1.6 copy-done.4
  60.9 1.3 projection.1
  62.2 0.7 copy-done.11
  63.4 1.4 collective-permute-start.6
  64.8 2.1 %all-gather.2.cloned.1.call-done.hidden_ref = bf16[1024,896]{1,0:T(8,128)(2,1)} async-done(((bf16[256,896]{1,0:T(8,128)(2,1)}), bf16[1024,896]{1,0:T(8,128)(2,1)}) %all-gather.2.cloned.1.call-update) | async-done | bytes 1835024 | tf_op jit(solution)/shard_map/all_gather | solution.py:512
  67.1 1.7 collective-permute-done.6.refs_1_
  68.8 1.4 collective-permute-done.7.refs_2_
  70.8 2.6 %hidden.1 = bf16[16,512,128]{2,1,0:T(8,128)(2,1)} custom-call(f32[512,128]{1,0:T(8,128)} %copy-done.11, bf16[512,128]{1,0:T(8,128)(2,1)} %copy-done.18, bf16[512,128]{1,0:T(8,128)(2,1)} %copy-done.19, bf16[512,128]{1,0:T(8,128)(2,1)} %copy-done.20), custom_call_target="tpu_custom_call" | custom-call | tf_op jit(solution)/shard_map/hidden/pallas_call | solution.py:148
  73.4 11.2 %all-to-all-start.1 = ((bf16[64,128,128]{2,1,0:T(8,128)(2,1)}), bf16[64,128,128]{2,1,0:T(8,128)(2,1)S(1)}, u32[]{:S(2)}, u32[]{:S(2)}) async-start(bf16[64,128,128]{2,1,0:T(8,128)(2,1)} %bitcast.100), calls=%async_computation.1 | async-start | bytes 4194304 | tf_op jit(solution)/shard_map/all_to_all | solution.py:541
  84.7 2.6 %copy-done.5 = bf16[896,3072]{1,0:T(8,128)(2,1)S(1)} copy-done((bf16[896,3072]{1,0:T(8,128)(2,1)S(1)}, bf16[896,3072]{1,0:T(8,128)(2,1)}, u32[]{:S(2)}) %copy-start.5) | copy-done | bytes 5505048
  87.2 1.5 copy-done.6
  88.7 4.1 %amateur_head.1 = (bf16[1024,768]{1,0:T(8,128)(2,1)S(1)}, f32[4,2,2,128]{3,2,1,0:T(2,128)S(1)}) custom-call(s32[1]{0:T(128)} %bitcast.33.place_ref, bf16[1024,896]{1,0:T(8,128)(2,1)S(1)} %copy-done.6, bf16[896,3072]{1,0:T(8,128)(2,1)S(1)} %copy-done.5), custom_call_target="tpu_custom_call" | custom-call | flops 1409286144 | bytes 4784128 | tf_op jit(solution)/shard_map/amateur_head/pallas_call | solution.py:276
  92.8 1.1 copy-done.7
  93.9 1.2 collective-permute-start.8
  97.3 15.7 %all-to-all-done.1.refs_0_ = bf16[64,128,128]{2,1,0:T(8,128)(2,1)S(1)} async-done(((bf16[64,128,128]{2,1,0:T(8,128)(2,1)}), bf16[64,128,128]{2,1,0:T(8,128)(2,1)S(1)}, u32[]{:S(2)}, u32[]{:S(2)}) %all-to-all-start.1) | async-done | bytes 2097184 | tf_op jit(solution)/shard_map/all_to_all | solution.py:541
  114.1 1.1 collective-permute-start.15
  115.3 1.6 collective-permute-start.10
  117.0 4.6 %copy-done.2 = bf16[8192,768]{1,0:T(8,128)(2,1)S(1)} copy-done((bf16[8192,768]{1,0:T(8,128)(2,1)S(1)}, bf16[8192,768]{1,0:T(8,128)(2,1)}, u32[]{:S(2)}) %copy-start.2) | copy-done | bytes 12582936
  121.6 9.4 %expert_head.3 = (f32[128,768]{1,0:T(8,128)S(1)}, f32[128,768]{1,0:T(8,128)S(1)}, f32[2,128]{1,0:T(2,128)S(1)}) custom-call(bf16[64,128,128]{2,1,0:T(8,128)(2,1)S(1)} %all-to-all-done.1.refs_0_, bf16[8192,768]{1,0:T(8,128)(2,1)S(1)} %copy-done.2, bf16[8192,768]{1,0:T(8,128)(2,1)} %collective-permute-done.9.refs_2_.refs_4_, f32[64,128]{1,0:T(8,128)S(1)} %bitcast.97), custom_call_target="tpu_custom_call" | custom-call | flops 3221225472 | bytes 25165824 | tf_op jit(solution)/shard_map/expert_head/pallas_call | solution.py:240
  130.9 0.8 copy-done.9
  132.1 4.6 %copy-done.3 = bf16[8192,768]{1,0:T(8,128)(2,1)S(1)} copy-done((bf16[8192,768]{1,0:T(8,128)(2,1)S(1)}, bf16[8192,768]{1,0:T(8,128)(2,1)}, u32[]{:S(2)}) %copy-start.3) | copy-done | bytes 12582936
  136.7 8.6 %expert_head.4 = (f32[384,768]{1,0:T(8,128)S(1)}, f32[384,768]{1,0:T(8,128)S(1)}, f32[384,128]{1,0:T(8,128)S(1)}) custom-call(bf16[40,128,128]{2,1,0:T(8,128)(2,1)S(1)} %collective-permute-done.13.refs_0_, bf16[40,128,128]{2,1,0:T(8,128)(2,1)S(1)} %collective-permute-done.14.refs_1_, bf16[40,128,128]{2,1,0:T(8,128)(2,1)S(1)} %collective-permute-done.15.refs_2_, ...), custom_call_target="tpu_custom_call" | custom-call | flops 6039797760 | bytes 15728640 | tf_op jit(solution)/shard_map/expert_head/pallas_call | solution.py:240
  145.3 6.5 %expert_head.5 = (f32[384,768]{1,0:T(8,128)S(1)}, f32[384,768]{1,0:T(8,128)S(1)}, f32[6,128]{1,0:T(8,128)S(1)}) custom-call(bf16[24,128,128]{2,1,0:T(8,128)(2,1)S(1)} %collective-permute-done.10.refs_0_, bf16[24,128,128]{2,1,0:T(8,128)(2,1)S(1)} %collective-permute-done.11.refs_1_, bf16[24,128,128]{2,1,0:T(8,128)(2,1)S(1)} %collective-permute-done.12.refs_2_, ...), custom_call_target="tpu_custom_call" | custom-call | flops 3623878656 | bytes 9437184 | tf_op jit(solution)/shard_map/expert_head/pallas_call | solution.py:240
  151.9 1.1 copy-done.8
  153.0 4.8 %collective-permute-start.18 = (f32[384,768]{1,0:T(8,128)S(1)}, f32[384,768]{1,0:T(8,128)}, u32[]{:S(2)}, u32[]{:S(2)}) collective-permute-start(f32[384,768]{1,0:T(8,128)S(1)} %get-tuple-element.55), channel_id=1, source_target_pairs={{0,1},{1,0},{2,3},{3,2},{4,5},{5,4},{6,7},{7,6},{8,9},{9,8},{10,11... | collective-permute-start | bytes 3538952 | tf_op jit(solution)/shard_map/ppermute | solution.py:68
  157.8 1.7 spread_stats.1
  159.5 7.1 %all-to-all-start.2 = ((f32[64,16,128]{2,1,0:T(8,128)}), f32[64,16,128]{2,1,0:T(8,128)S(1)}, u32[]{:S(2)}, u32[]{:S(2)}) async-start(f32[64,16,128]{2,1,0:T(8,128)} %spread_stats.1), calls=%async_computation.2 | async-start | bytes 1048576 | tf_op jit(solution)/shard_map/all_to_all | solution.py:574
  166.6 0.9 collective-permute-start.17
  167.5 11.3 %all-to-all-done.2.parts_ref = f32[64,16,128]{2,1,0:T(8,128)S(1)} async-done(((f32[64,16,128]{2,1,0:T(8,128)}), f32[64,16,128]{2,1,0:T(8,128)S(1)}, u32[]{:S(2)}, u32[]{:S(2)}) %all-to-all-start.2) | async-done | bytes 524320 | tf_op jit(solution)/shard_map/all_to_all | solution.py:574
  179.2 2.2 %collective-permute-start.16 = (f32[8,128]{1,0:T(8,128)S(1)}, f32[8,128]{1,0:T(8,128)S(1)}, u32[]{:S(2)}, u32[]{:S(2)}) collective-permute-start(f32[8,128]{1,0:T(8,128)S(1)} %merge_stats.1.mine_ref), channel_id=1, source_target_pairs={{0,1},{1,0},{2,3},{3,2},{4,5},{5,4},{6,7},{7,6},{8,9},{9,8},{10,11... | collective-permute-start | bytes 12296 | tf_op jit(solution)/shard_map/ppermute | solution.py:68
  181.3 0.8 collective-permute-done.16.theirs_ref
  182.7 5.0 %contrast.1 = f32[1024,768]{1,0:T(8,128)} custom-call(s32[2]{0:T(128)} %pad_add_fusion.place_ref, f32[8,128]{1,0:T(8,128)} %copy-done.12, f32[8,128]{1,0:T(8,128)} %copy-done.22, f32[8,128]{1,0:T(8,128)} %mul.74.limit_ref, f32[128,768]{1,0:T(8,128)} %copy-done.9, f32[384,768]{1,0:T(8,128)} %copy-done.8, f32[128,768]{1,0:T(8,128)} %copy-done.15, ...), custom_call_target="tpu_custom_call" | custom-call | flops 4718592 | bytes 7864320 | tf_op jit(solution)/shard_map/contrast/pallas_call | solution.py:458
  (92 shorter events, 7.4 us)
Async XLA Ops:
  6.5 9.5 %copy-start = (bf16[8,1024]{1,0:T(8,128)(2,1)S(1)}, bf16[8,1024]{1,0:T(8,128)(2,1)}, u32[]{:S(2)}) copy-start(bf16[8,1024]{1,0:T(8,128)(2,1)} %param.16) | copy-start | bytes 49156
  6.5 9.4 %copy-start.24 = (s32[8]{0:T(128)S(1)}, s32[8]{0:T(128)}, u32[]{:S(2)}) copy-start(s32[8]{0:T(128)} %param.18) | copy-start | bytes 100
  6.5 9.5 %copy-start.16 = (bf16[8,8192]{1,0:T(8,128)(2,1)S(1)}, bf16[8,8192]{1,0:T(8,128)(2,1)}, u32[]{:S(2)}) copy-start(bf16[8,8192]{1,0:T(8,128)(2,1)} %param.13) | copy-start | bytes 393220
  6.5 60.4 %all-gather.2.cloned.1.call-start = ((), (), s32[]{:S(2)}) async-start(), calls=%async_computation.3 | async-start | bytes 2293760 | tf_op jit(solution)/shard_map/all_gather | solution.py:512
  6.5 110.4 %collective-permute-start.9 = (bf16[8192,768]{1,0:T(8,128)(2,1)}, bf16[8192,768]{1,0:T(8,128)(2,1)}, u32[]{:S(2)}, u32[]{:S(2)}) collective-permute-start(bf16[8192,768]{1,0:T(8,128)(2,1)} %refs_3_.3), channel_id=1, source_target_pairs={{0,1},{1,0},{2,3},{3,2},{4,5},{5,4},{6,7},{7,6},{8,9},{9,8},{10,11... | collective-permute-start | bytes 37748744 | tf_op jit(solution)/shard_map/ppermute | solution.py:68
  10.1 20.9 %collective-permute-start = (bf16[64,2048]{1,0:T(8,128)(2,1)}, bf16[64,2048]{1,0:T(8,128)(2,1)S(1)}, u32[]{:S(2)}, u32[]{:S(2)}) collective-permute-start(bf16[64,2048]{1,0:T(8,128)(2,1)} %get-tuple-element.60), channel_id=1, source_target_pairs={{0,32},{32,64},{64,96},{96,0},{1,33},{33,65},{65,97},{97,1},{2,34}... | collective-permute-start | bytes 786440 | tf_op jit(solution)/shard_map/ppermute | solution.py:68
  11.9 19.2 %collective-permute-start.1 = (bf16[64,2048]{1,0:T(8,128)(2,1)}, bf16[64,2048]{1,0:T(8,128)(2,1)S(1)}, u32[]{:S(2)}, u32[]{:S(2)}) collective-permute-start(bf16[64,2048]{1,0:T(8,128)(2,1)} %get-tuple-element.62), channel_id=1, source_target_pairs={{0,64},{32,96},{64,0},{96,32},{1,65},{33,97},{65,1},{97,33},{2,66}... | collective-permute-start | bytes 786440 | tf_op jit(solution)/shard_map/ppermute | solution.py:68
  15.2 15.9 %collective-permute-start.2 = (bf16[64,2048]{1,0:T(8,128)(2,1)S(1)}, bf16[64,2048]{1,0:T(8,128)(2,1)S(1)}, u32[]{:S(2)}, u32[]{:S(2)}) collective-permute-start(bf16[64,2048]{1,0:T(8,128)(2,1)S(1)} %get-tuple-element.61), channel_id=1, source_target_pairs={{0,96},{32,0},{64,32},{96,64},{1,97},{33,1},{65,33},{97,65},{2,98}... | collective-permute-start | bytes 786440 | tf_op jit(solution)/shard_map/ppermute | solution.py:68
  16.2 4.0 %copy-start.21 = (bf16[8,1024]{1,0:T(8,128)(2,1)S(1)}, bf16[8,1024]{1,0:T(8,128)(2,1)}, u32[]{:S(2)}) copy-start(bf16[8,1024]{1,0:T(8,128)(2,1)} %param.17) | copy-start | bytes 49156
  16.2 4.0 %copy-start.25 = (bf16[8,256,1024]{2,1,0:T(8,128)(2,1)S(1)}, bf16[8,256,1024]{2,1,0:T(8,128)(2,1)}, u32[]{:S(2)}) copy-start(bf16[8,256,1024]{2,1,0:T(8,128)(2,1)} %param.15) | copy-start | bytes 12582916
  22.9 36.4 %all-to-all-start = ((bf16[64,128,128]{2,1,0:T(8,128)(2,1)}), bf16[64,128,128]{2,1,0:T(8,128)(2,1)S(1)}, u32[]{:S(2)}, u32[]{:S(2)}) async-start(bf16[64,128,128]{2,1,0:T(8,128)(2,1)} %bitcast.101), calls=%async_computation | async-start | bytes 4194304 | tf_op jit(solution)/shard_map/all_to_all | solution.py:513
  31.0 2.3 %copy-start.17 = (bf16[1024,64]{0,1:T(8,128)(2,1)S(1)}, bf16[1024,64]{0,1:T(8,128)(2,1)}, u32[]{:S(2)}) copy-start(bf16[1024,64]{0,1:T(8,128)(2,1)} %param.19) | copy-start | bytes 393220
  32.2 4.8 %collective-permute-start.3 = (bf16[4,64,2048]{2,1,0:T(8,128)(2,1)}, bf16[4,64,2048]{2,1,0:T(8,128)(2,1)}, u32[]{:S(2)}, u32[]{:S(2)}) collective-permute-start(bf16[4,64,2048]{2,1,0:T(8,128)(2,1)} %pad_maximum_fusion.1), channel_id=1, source_target_pairs={{0,1},{1,0},{2,3},{3,2},{4,5},{5,4},{6,7},{7,6},{8,9},{9,8},{10,11... | collective-permute-start | bytes 3145736 | tf_op jit(solution)/shard_map/ppermute | solution.py:68
  33.5 2.4 %collective-permute-start.4 = (bf16[64,64,8]{0,2,1:T(8,128)(2,1)S(1)}, bf16[64,64,8]{0,2,1:T(8,128)(2,1)}, u32[]{:S(2)}, u32[]{:S(2)}) collective-permute-start(bf16[64,64,8]{0,2,1:T(8,128)(2,1)S(1)} %dynamic-slice_bitcast_fusion.4), channel_id=1, source_target_pairs={{0,1},{1,0},{2,3},{3,2},{4,5},{5,4},{6,7},{7,6},{8,9},{9,8},{10,11... | collective-permute-start | bytes 196616 | tf_op jit(solution)/shard_map/ppermute | solution.py:68
  59.3 1.6 copy-start.4
  62.2 0.7 copy-start.11
  62.9 4.2 %collective-permute-start.5 = (bf16[512,128]{1,0:T(8,128)(2,1)S(1)}, bf16[512,128]{1,0:T(8,128)(2,1)S(1)}, u32[]{:S(2)}, u32[]{:S(2)}) collective-permute-start(bf16[512,128]{1,0:T(8,128)(2,1)S(1)} %get-tuple-element.35), channel_id=1, source_target_pairs={{0,96},{32,0},{64,32},{96,64},{1,97},{33,1},{65,33},{97,65},{2,98}... | collective-permute-start | bytes 393224 | tf_op jit(solution)/shard_map/ppermute | solution.py:68
  63.4 5.3 %collective-permute-start.6 = (bf16[512,128]{1,0:T(8,128)(2,1)S(1)}, bf16[512,128]{1,0:T(8,128)(2,1)S(1)}, u32[]{:S(2)}, u32[]{:S(2)}) collective-permute-start(bf16[512,128]{1,0:T(8,128)(2,1)S(1)} %get-tuple-element.36), channel_id=1, source_target_pairs={{0,64},{32,96},{64,0},{96,32},{1,65},{33,97},{65,1},{97,33},{2,66}... | collective-permute-start | bytes 393224 | tf_op jit(solution)/shard_map/ppermute | solution.py:68
  64.8 5.3 %collective-permute-start.7 = (bf16[512,128]{1,0:T(8,128)(2,1)S(1)}, bf16[512,128]{1,0:T(8,128)(2,1)S(1)}, u32[]{:S(2)}, u32[]{:S(2)}) collective-permute-start(bf16[512,128]{1,0:T(8,128)(2,1)S(1)} %get-tuple-element.37), channel_id=1, source_target_pairs={{0,32},{32,64},{64,96},{96,0},{1,33},{33,65},{65,97},{97,1},{2,34}... | collective-permute-start | bytes 393224 | tf_op jit(solution)/shard_map/ppermute | solution.py:68
  67.1 3.1 %copy-start.18 = (bf16[512,128]{1,0:T(8,128)(2,1)}, bf16[512,128]{1,0:T(8,128)(2,1)S(1)}, u32[]{:S(2)}) copy-start(bf16[512,128]{1,0:T(8,128)(2,1)S(1)} %collective-permute-done.5.refs_0_) | copy-start | bytes 393220
  68.8 1.4 copy-start.19
  70.2 0.7 copy-start.20
  73.4 11.2 %copy-start.23 = (s32[1024]{0:T(1024)S(1)}, s32[1024]{0:T(1024)}, u32[]{:S(2)}) copy-start(s32[1024]{0:T(1024)} %param.25) | copy-start | bytes 12292
  73.4 39.5 %all-to-all-start.1 = ((bf16[64,128,128]{2,1,0:T(8,128)(2,1)}), bf16[64,128,128]{2,1,0:T(8,128)(2,1)S(1)}, u32[]{:S(2)}, u32[]{:S(2)}) async-start(bf16[64,128,128]{2,1,0:T(8,128)(2,1)} %bitcast.100), calls=%async_computation.1 | async-start | bytes 4194304 | tf_op jit(solution)/shard_map/all_to_all | solution.py:541
  84.7 2.6 %copy-start.5 = (bf16[896,3072]{1,0:T(8,128)(2,1)S(1)}, bf16[896,3072]{1,0:T(8,128)(2,1)}, u32[]{:S(2)}) copy-start(bf16[896,3072]{1,0:T(8,128)(2,1)} %weight_ref.1) | copy-start | bytes 16515076
  87.2 1.5 copy-start.6
  92.8 1.1 copy-start.7
  93.9 2.7 %collective-permute-start.8 = (f32[4,2,128]{2,1,0:T(2,128)S(1)}, f32[4,2,128]{2,1,0:T(2,128)S(1)}, u32[]{:S(2)}, u32[]{:S(2)}) collective-permute-start(f32[4,2,128]{2,1,0:T(2,128)S(1)} %get-tuple-element.70), channel_id=1, source_target_pairs={{0,1},{1,0},{2,3},{3,2},{4,5},{5,4},{6,7},{7,6},{8,9},{9,8},{10,11... | collective-permute-start | bytes 12296 | tf_op jit(solution)/shard_map/ppermute | solution.py:68
  112.9 4.0 %copy-start.10 = (f32[8192]{0:T(1024)S(1)}, f32[8192]{0:T(1024)}, u32[]{:S(2)}) copy-start(f32[8192]{0:T(1024)} %param.20) | copy-start | bytes 98308
  113.0 18.7 %collective-permute-start.13 = (bf16[40,128,128]{2,1,0:T(8,128)(2,1)S(1)}, bf16[40,128,128]{2,1,0:T(8,128)(2,1)S(1)}, u32[]{:S(2)}, u32[]{:S(2)}) collective-permute-start(bf16[40,128,128]{2,1,0:T(8,128)(2,1)S(1)} %slice.20), channel_id=1, source_target_pairs={{0,6},{1,97},{2,0},{3,99},{4,2},{5,101},{6,4},{7,103},{8,14},{9,10... | collective-permute-start | bytes 3932168 | tf_op jit(solution)/shard_map/ppermute | solution.py:80
  113.6 18.1 %collective-permute-start.14 = (bf16[40,128,128]{2,1,0:T(8,128)(2,1)S(1)}, bf16[40,128,128]{2,1,0:T(8,128)(2,1)S(1)}, u32[]{:S(2)}, u32[]{:S(2)}) collective-permute-start(bf16[40,128,128]{2,1,0:T(8,128)(2,1)S(1)} %slice.20), channel_id=1, source_target_pairs={{0,24},{1,9},{2,26},{3,11},{4,28},{5,13},{6,30},{7,15},{8,0},{9,17... | collective-permute-start | bytes 3932168 | tf_op jit(solution)/shard_map/ppermute | solution.py:80
  114.1 18.0 %collective-permute-start.15 = (bf16[40,128,128]{2,1,0:T(8,128)(2,1)S(1)}, bf16[40,128,128]{2,1,0:T(8,128)(2,1)S(1)}, u32[]{:S(2)}, u32[]{:S(2)}) collective-permute-start(bf16[40,128,128]{2,1,0:T(8,128)(2,1)S(1)} %slice.20), channel_id=1, source_target_pairs={{0,2},{1,33},{2,4},{3,35},{4,6},{5,37},{6,0},{7,39},{8,10},{9,41},... | collective-permute-start | bytes 3932168 | tf_op jit(solution)/shard_map/ppermute | solution.py:80
  115.3 30.0 %collective-permute-start.10 = (bf16[24,128,128]{2,1,0:T(8,128)(2,1)S(1)}, bf16[24,128,128]{2,1,0:T(8,128)(2,1)S(1)}, u32[]{:S(2)}, u32[]{:S(2)}) collective-permute-start(bf16[24,128,128]{2,1,0:T(8,128)(2,1)S(1)} %slice.19), channel_id=1, source_target_pairs={{0,6},{1,97},{2,0},{3,99},{4,2},{5,101},{6,4},{7,103},{8,14},{9,10... | collective-permute-start | bytes 2359304 | tf_op jit(solution)/shard_map/ppermute | solution.py:80
  117.0 28.4 %collective-permute-start.11 = (bf16[24,128,128]{2,1,0:T(8,128)(2,1)S(1)}, bf16[24,128,128]{2,1,0:T(8,128)(2,1)S(1)}, u32[]{:S(2)}, u32[]{:S(2)}) collective-permute-start(bf16[24,128,128]{2,1,0:T(8,128)(2,1)S(1)} %slice.19), channel_id=1, source_target_pairs={{0,24},{1,9},{2,26},{3,11},{4,28},{5,13},{6,30},{7,15},{8,0},{9,17... | collective-permute-start | bytes 2359304 | tf_op jit(solution)/shard_map/ppermute | solution.py:80
  117.0 4.6 %copy-start.2 = (bf16[8192,768]{1,0:T(8,128)(2,1)S(1)}, bf16[8192,768]{1,0:T(8,128)(2,1)}, u32[]{:S(2)}) copy-start(bf16[8192,768]{1,0:T(8,128)(2,1)} %refs_3_.3) | copy-start | bytes 37748740
  130.9 0.8 copy-start.9
  131.7 13.6 %copy-start.14 = (f32[2,128]{1,0:T(2,128)}, f32[2,128]{1,0:T(2,128)S(1)}, u32[]{:S(2)}) copy-start(f32[2,128]{1,0:T(2,128)S(1)} %get-tuple-element.43.first_ref) | copy-start | bytes 3076
  131.7 13.6 %collective-permute-start.12 = (bf16[24,128,128]{2,1,0:T(8,128)(2,1)S(1)}, bf16[24,128,128]{2,1,0:T(8,128)(2,1)S(1)}, u32[]{:S(2)}, u32[]{:S(2)}) collective-permute-start(bf16[24,128,128]{2,1,0:T(8,128)(2,1)S(1)} %slice.19), channel_id=1, source_target_pairs={{0,2},{1,33},{2,4},{3,35},{4,6},{5,37},{6,0},{7,39},{8,10},{9,41},... | collective-permute-start | bytes 2359304 | tf_op jit(solution)/shard_map/ppermute | solution.py:80
  132.1 4.6 %copy-start.3 = (bf16[8192,768]{1,0:T(8,128)(2,1)S(1)}, bf16[8192,768]{1,0:T(8,128)(2,1)}, u32[]{:S(2)}) copy-start(bf16[8192,768]{1,0:T(8,128)(2,1)} %refs_3_.3) | copy-start | bytes 37748740
  151.9 1.1 copy-start.8
  153.0 4.8 %copy-start.13 = (f32[6,128]{1,0:T(8,128)}, f32[6,128]{1,0:T(8,128)S(1)}, u32[]{:S(2)}) copy-start(f32[6,128]{1,0:T(8,128)S(1)} %get-tuple-element.49.rest_ref) | copy-start | bytes 9220
  153.0 29.2 %collective-permute-start.18 = (f32[384,768]{1,0:T(8,128)S(1)}, f32[384,768]{1,0:T(8,128)}, u32[]{:S(2)}, u32[]{:S(2)}) collective-permute-start(f32[384,768]{1,0:T(8,128)S(1)} %get-tuple-element.55), channel_id=1, source_target_pairs={{0,1},{1,0},{2,3},{3,2},{4,5},{5,4},{6,7},{7,6},{8,9},{9,8},{10,11... | collective-permute-start | bytes 3538952 | tf_op jit(solution)/shard_map/ppermute | solution.py:68
  159.5 19.4 %all-to-all-start.2 = ((f32[64,16,128]{2,1,0:T(8,128)}), f32[64,16,128]{2,1,0:T(8,128)S(1)}, u32[]{:S(2)}, u32[]{:S(2)}) async-start(f32[64,16,128]{2,1,0:T(8,128)} %spread_stats.1), calls=%async_computation.2 | async-start | bytes 1048576 | tf_op jit(solution)/shard_map/all_to_all | solution.py:574
  166.6 14.7 %collective-permute-start.17 = (f32[128,768]{1,0:T(8,128)S(1)}, f32[128,768]{1,0:T(8,128)S(1)}, u32[]{:S(2)}, u32[]{:S(2)}) collective-permute-start(f32[128,768]{1,0:T(8,128)S(1)} %get-tuple-element.54), channel_id=1, source_target_pairs={{0,1},{1,0},{2,3},{3,2},{4,5},{5,4},{6,7},{7,6},{8,9},{9,8},{10,11... | collective-permute-start | bytes 1179656 | tf_op jit(solution)/shard_map/ppermute | solution.py:68
  179.2 3.0 %copy-start.12 = (f32[8,128]{1,0:T(8,128)}, f32[8,128]{1,0:T(8,128)S(1)}, u32[]{:S(2)}) copy-start(f32[8,128]{1,0:T(8,128)S(1)} %merge_stats.1.mine_ref) | copy-start | bytes 12292
  179.2 3.0 %collective-permute-start.16 = (f32[8,128]{1,0:T(8,128)S(1)}, f32[8,128]{1,0:T(8,128)S(1)}, u32[]{:S(2)}, u32[]{:S(2)}) collective-permute-start(f32[8,128]{1,0:T(8,128)S(1)} %merge_stats.1.mine_ref), channel_id=1, source_target_pairs={{0,1},{1,0},{2,3},{3,2},{4,5},{5,4},{6,7},{7,6},{8,9},{9,8},{10,11... | collective-permute-start | bytes 12296 | tf_op jit(solution)/shard_map/ppermute | solution.py:68
  181.3 0.8 copy-start.15
  182.2 5.6 %copy-start.1 = (bf16[8,1024]{1,0:T(8,128)(2,1)S(1)}, bf16[8,1024]{1,0:T(8,128)(2,1)}, u32[]{:S(2)}) copy-start(bf16[8,1024]{1,0:T(8,128)(2,1)} %param.16) | copy-start | bytes 49156
  (1 other events, 0.6 us)
Sparse Core Ops, SparseCore 0:
  16.0 50.9 all-gather.1

commit v3 on v2

--- a/solution.py
+++ b/solution.py
@@ -147,13 +147,13 @@
     rows = total.shape[0]
     return pl.pallas_call(
         functools.partial(hidden_kernel, turns),
-        out_specs=pl.BlockSpec(memory_space=pl.ANY),
-        out_shape=jax.ShapeDtypeStruct((len(turns), rows, LINE), jnp.bfloat16),
+        out_specs=pl.BlockSpec(memory_space=pltpu.HBM),
+        out_shape=pltpu.HBM((len(turns), rows, LINE), jnp.bfloat16),
         scratch_shapes=[
             pltpu.VMEM((2 * rows, LINE), jnp.bfloat16),
             pltpu.SemaphoreType.DMA((len(turns),)),
         ],
-        compiler_params=params(60),
+        compiler_params=params(8),
         name="hidden",
     )(total, *parts)
 
@@ -230,6 +230,7 @@
         in_specs += [whole, whole, lines]
     logits = jax.ShapeDtypeStruct((rows, columns), jnp.float32)
     if finished:
+        logits = pltpu.HBM(logits.shape, logits.dtype)
         last = jax.ShapeDtypeStruct((2 * pieces, LINE), jnp.float32)
         last_spec = pl.BlockSpec((2 * pieces, LINE), lambda i: (0, 0))
         scratch = [pltpu.VMEM((rows, LINE), jnp.float32)]
@@ -288,7 +289,7 @@
             ],
         ),
         out_shape=[
-            jax.ShapeDtypeStruct((rows, columns), jnp.bfloat16),
+            pltpu.HBM((rows, columns), jnp.bfloat16),
             jax.ShapeDtypeStruct((rows // tall, 2, 2, LINE), jnp.float32),
         ],
         compiler_params=params(16),
@@ -334,14 +335,14 @@
     return pl.pallas_call(
         spread_kernel,
         in_specs=[pl.BlockSpec(memory_space=pltpu.SMEM)] + [vmem] * 3,
-        out_specs=pl.BlockSpec(memory_space=pl.ANY),
-        out_shape=jax.ShapeDtypeStruct((targets, rows, LINE), jnp.float32),
+        out_specs=pl.BlockSpec(memory_space=pltpu.HBM),
+        out_shape=pltpu.HBM((targets, rows, LINE), jnp.float32),
         scratch_shapes=[
             pltpu.VMEM((rows, LINE), jnp.float32),
             pltpu.VMEM((8, rows, LINE), jnp.float32),
             pltpu.SemaphoreType.DMA((targets // 8,)),
         ],
-        compiler_params=params(60),
+        compiler_params=params(4),
         name="spread_stats",
     )(place, first, rest, amateur)
 
@@ -508,15 +509,15 @@
     copies = jnp.broadcast_to(
         slabs.reshape(depth, 1, heads * per, LINE), (depth, chips // depth, heads * per, LINE)
     ).reshape(chips * heads * per, LINE)
-    copies, residual = lax.optimization_barrier((copies, residual))
+    copies, residual, kept_weight = lax.optimization_barrier((copies, residual, out_weight))
     everyone = lax.all_gather(amateur_hidden, "z", axis=0, tiled=True)
     arrived = lax.all_to_all(copies, CHIPS, split_axis=0, concat_axis=0, tiled=True)
 
     other_weight = shift(head_weight, "core", 1)
 
-    turned = out_weight.T
     pieces = []
     for step in range(depth):
+        turned = (kept_weight if step == 0 else out_weight).T
         part = lax.dynamic_slice_in_dim(turned, lax.rem(z + step, depth) * slab, slab, 1)
         pieces.append(part if step == 0 else shift(part, "z", step))
     mine = jnp.stack(pieces)
@@ -532,6 +533,7 @@
     base = base.reshape(-1, chips * per).T
 
     left = arrived.reshape(chips, heads, per, LINE).transpose(0, 2, 1, 3).reshape(chips * per, slab)
+    projection = pltpu.with_memory_space_constraint(projection, pltpu.HBM)
     total, *sent = project(left, projection, base)
     parts = [shift(part, "z", -step) for step, part in enumerate(sent, 1)]
     total, everyone = lax.optimization_barrier((total, everyone))
@@ -556,12 +558,13 @@
         ((0, -1, 0), (0, 1, 0)),
         ((0, 0, 1), (1, 0, 0)),
     )
-    half = chips * 5 // 8
+    half = chips * 6 // 8
 
     gain_lines = gain.reshape(-1, LINE)
     halves = [[shift_chips(quarters[:half], move) for move in moves]]
     halves.append([shift_chips(quarters[half:], move) for move in moves[:2]])
-    own_0, other_0, stats_0 = head([quarters], head_weight, other_weight, gain_lines)
+    far = [pltpu.with_memory_space_constraint(w, pltpu.HBM) for w in (head_weight, other_weight)]
+    own_0, other_0, stats_0 = head([quarters], *far, gain_lines)
     later, own_0 = lax.optimization_barrier((quarters[half:], own_0))
     halves[1].append(shift_chips(later, moves[2]))
     begun = head(halves[0], head_weight, other_weight, gain_lines, finished=False)

time: 196 us -> 189 us (0.964)
  local copies, waits for them, and re-layouts: 26.4 us -> 12.7 us
  Pallas kernels: 39.5 us -> 47 us
  waiting for transfers between devices: 55.1 us -> 60.1 us
  starting transfers between devices: 49.8 us -> 45.8 us
    unnamed x52 -> x40, local copies, waits for them, and re-layouts: 19.8 us -> 5.16 us
    pallas_call x3, Pallas kernels: 24.5 us -> 31.4 us  [head(): pl.pallas_call(functools.partial(head_kernel, pieces, steps, features, re...]
    ppermute x6, waiting for transfers between devices: 0.4 us -> 3.14 us  [shift_chips(): return lax.ppermute(x, ALL, pairs)]
    ppermute x13, starting transfers between devices: 19.5 us -> 17.4 us  [shift(): return lax.ppermute(x, axis, [(i, (i + step) % size) for i in range(size)])]
    all_to_all x3, waiting for transfers between devices: 46.2 us -> 48.3 us  [body(): lax.all_to_all(copies, CHIPS, split_axis=0, concat_axis=0, tiled=True)]
    dynamic_slice x0 -> x1, local copies, waits for them, and re-layouts: none -> 1.99 us  [body(): lax.dynamic_slice_in_dim(turned, lax.rem(z + step, depth) * slab, slab, 1)]
  transfers between devices with their start and end apart: 23 -> 23, of which waited for: 10 -> 12; matrix products, arithmetic and copies ran while one was open for 9% -> 9% of each run, Pallas kernels for 14% -> 19%
where the time goes in v3:
time: 189 us; the launch traced here: 188 us
  waiting for transfers between devices  60.1 us (32%)
  Pallas kernels  47 us (25%)
  starting transfers between devices  45.8 us (24%)
  between operations  13.9 us (7%)
  local copies, waits for them, and re-layouts  12.7 us (7%)
  matrix products  4.55 us (2%)
  other arithmetic  4.29 us (2%)
    all_to_all x3, waiting for transfers between devices, body(): lax.all_to_all(copies, CHIPS, split_axis=0, concat_axis=0, tiled=True)  48.3 us
    pallas_call x3, Pallas kernels, head(): pl.pallas_call(functools.partial(head_kernel, pieces, steps, features, re...  31.4 us
    all_to_all x3, starting transfers between devices, body(): lax.all_to_all(copies, CHIPS, split_axis=0, concat_axis=0, tiled=True)  24.6 us
    ppermute x13, starting transfers between devices, shift(): return lax.ppermute(x, axis, [(i, (i + step) % size) for i in range(size)])  17.4 us
    ppermute x13, waiting for transfers between devices, shift(): return lax.ppermute(x, axis, [(i, (i + step) % size) for i in range(size)])  5.78 us
    unnamed x40, local copies, waits for them, and re-layouts  5.16 us
    pallas_call x1, Pallas kernels, contrast(): pl.pallas_call(contrast_kernel, in_specs=[pl.BlockSpec(memory_space=pltpu...  5.03 us
    pallas_call x1, Pallas kernels, amateur_logits(): pl.pallas_call(amateur_kernel, grid_spec=pltpu.PrefetchScalarGridSpec(num...  4.42 us
  transfers between devices with their start and end apart: 23, of which 12 were waited for; matrix products, arithmetic and copies ran while one was open for 9% of the time, Pallas kernels for 19%

profile of v3, /device:TPU:1, one launch (start us, length us, event | category | flops | bytes accessed | tf_op | source)
XLA Modules:
  0.0 188.3 jit_solution(2358358786884310596)
XLA Ops:
  6.6 1.5 collective-permute-start.9
  8.1 2.0 %dynamic-slice_bitcast_fusion.2 = (bf16[64,2048]{1,0:T(8,128)(2,1)}, bf16[64,2048]{1,0:T(8,128)(2,1)S(1)}, bf16[64,2048]{1,0:T(8,128)(2,1)}) fusion(bf16[8192,64]{0,1:T(8,128)(2,1)} %param.21, s32[]{:T(128)S(6)} %select_n.64, s32[]{:T(128)S(6)} %select_n.66, s32[]{:T(128)S(6)} %select_n.65), kind=kLoop, calls=%fused_computation.19 | loop fusion | bytes 1572876 | tf_op jit(solution)/shard_map/dynamic_slice | solution.py:521
  10.1 1.7 collective-permute-start
  11.8 3.3 %collective-permute-start.1 = (bf16[64,2048]{1,0:T(8,128)(2,1)}, bf16[64,2048]{1,0:T(8,128)(2,1)S(1)}, u32[]{:S(2)}, u32[]{:S(2)}) collective-permute-start(bf16[64,2048]{1,0:T(8,128)(2,1)} %get-tuple-element.63), channel_id=1, source_target_pairs={{0,64},{32,96},{64,0},{96,32},{1,65},{33,97},{65,1},{97,33},{2,66}... | collective-permute-start | bytes 786440 | tf_op jit(solution)/shard_map/ppermute | solution.py:68
  15.1 0.7 collective-permute-start.2
  16.2 3.6 %fusion.31 = (f32[8,8,8]{2,1,0:T(8,128)S(1)}, f32[8,8,8,256]{3,2,1,0:T(8,128)S(1)}) fusion(bf16[8,8,8,128]{3,0,2,1:T(8,128)(2,1)S(1)} %bitcast.116, pred[8,256]{1,0:T(8,128)(4,1)S(1)} %iota_compare_fusion, bf16[8,256,1024]{2,1,0:T(8,128)(2,1)} %param.14), kind=kOutput, calls=%fused_computation.52 | convolution fusion | flops 33947136 | bytes 4853760 | tf_op jit(solution)/shard_map/rkgd,rlkd->rkgl/dot_general | solution.py:35
  20.1 0.7 fusion.15
  21.0 1.8 broadcast_in_dim.36
  22.8 8.1 %all-to-all-start = ((bf16[64,128,128]{2,1,0:T(8,128)(2,1)}), bf16[64,128,128]{2,1,0:T(8,128)(2,1)S(1)}, u32[]{:S(2)}, u32[]{:S(2)}) async-start(bf16[64,128,128]{2,1,0:T(8,128)(2,1)} %bitcast.102), calls=%async_computation | async-start | bytes 4194304 | tf_op jit(solution)/shard_map/all_to_all | solution.py:514
  31.0 1.0 dynamic-slice_bitcast_fusion.3
  32.0 1.1 pad_maximum_fusion.1
  33.1 1.2 collective-permute-start.3
  34.6 2.3 %collective-permute-done.4 = bf16[64,64,8]{0,2,1:T(8,128)(2,1)} collective-permute-done((bf16[64,64,8]{0,2,1:T(8,128)(2,1)S(1)}, bf16[64,64,8]{0,2,1:T(8,128)(2,1)}, u32[]{:S(2)}, u32[]{:S(2)}) %collective-permute-start.4) | collective-permute-done | bytes 65568 | tf_op jit(solution)/shard_map/ppermute | solution.py:68
  36.9 0.9 bitcast_select_fusion.1
  38.0 1.4 select_bitcast_fusion.1
  39.6 1.4 copy.27
  41.0 18.2 %all-to-all-done = bf16[64,128,128]{2,1,0:T(8,128)(2,1)S(1)} async-done(((bf16[64,128,128]{2,1,0:T(8,128)(2,1)}), bf16[64,128,128]{2,1,0:T(8,128)(2,1)S(1)}, u32[]{:S(2)}, u32[]{:S(2)}) %all-to-all-start) | async-done | bytes 2097184 | tf_op jit(solution)/shard_map/all_to_all | solution.py:514
  59.3 2.9 %projection.1 = (f32[512,128]{1,0:T(8,128)S(1)}, bf16[512,128]{1,0:T(8,128)(2,1)S(1)}, bf16[512,128]{1,0:T(8,128)(2,1)S(1)}, bf16[512,128]{1,0:T(8,128)(2,1)S(1)}) custom-call(bf16[512,2048]{1,0:T(8,128)(2,1)S(1)} %bitcast.97, bf16[512,2048]{1,0:T(8,128)(2,1)} %bitcast.104, bf16[512,128]{1,0:T(8,128)(2,1)S(1)} %maximum_bitcast_fusion.base_ref), custom_call_target="tpu_custom_call" | custom-call | flops 1073741824 | bytes 4194304 | tf_op jit(solution)/shard_map/projection/pallas_call | solution.py:111
  62.2 0.6 collective-permute-start.5
  62.7 1.4 collective-permute-start.6
  64.1 2.8 %all-gather.2.cloned.1.call-done.hidden_ref = bf16[1024,896]{1,0:T(8,128)(2,1)} async-done(((bf16[256,896]{1,0:T(8,128)(2,1)}), bf16[1024,896]{1,0:T(8,128)(2,1)}) %all-gather.2.cloned.1.call-update) | async-done | bytes 1835024 | tf_op jit(solution)/shard_map/all_gather | solution.py:513
  67.0 1.2 collective-permute-done.6.refs_1_
  68.2 1.4 collective-permute-done.7.refs_2_
  69.6 1.5 hidden.1
  71.1 11.1 %all-to-all-start.1 = ((bf16[64,128,128]{2,1,0:T(8,128)(2,1)}), bf16[64,128,128]{2,1,0:T(8,128)(2,1)S(1)}, u32[]{:S(2)}, u32[]{:S(2)}) async-start(bf16[64,128,128]{2,1,0:T(8,128)(2,1)} %bitcast.103), calls=%async_computation.1 | async-start | bytes 4194304 | tf_op jit(solution)/shard_map/all_to_all | solution.py:543
  82.2 2.6 %copy-done.2 = bf16[896,3072]{1,0:T(8,128)(2,1)S(1)} copy-done((bf16[896,3072]{1,0:T(8,128)(2,1)S(1)}, bf16[896,3072]{1,0:T(8,128)(2,1)}, u32[]{:S(2)}) %copy-start.2) | copy-done | bytes 5505048
  84.8 1.5 copy-done.3
  86.3 4.4 %amateur_head.1 = (bf16[1024,768]{1,0:T(8,128)(2,1)}, f32[4,2,2,128]{3,2,1,0:T(2,128)S(1)}) custom-call(s32[1]{0:T(128)} %bitcast.33.place_ref, bf16[1024,896]{1,0:T(8,128)(2,1)S(1)} %copy-done.3, bf16[896,3072]{1,0:T(8,128)(2,1)S(1)} %copy-done.2), custom_call_target="tpu_custom_call" | custom-call | flops 1409286144 | bytes 4784128 | tf_op jit(solution)/shard_map/amateur_head/pallas_call | solution.py:277
  90.7 1.2 collective-permute-start.8
  92.1 0.7 mul.74.limit_ref
  92.8 17.6 %all-to-all-done.1.refs_0_ = bf16[64,128,128]{2,1,0:T(8,128)(2,1)S(1)} async-done(((bf16[64,128,128]{2,1,0:T(8,128)(2,1)}), bf16[64,128,128]{2,1,0:T(8,128)(2,1)S(1)}, u32[]{:S(2)}, u32[]{:S(2)}) %all-to-all-start.1) | async-done | bytes 2097184 | tf_op jit(solution)/shard_map/all_to_all | solution.py:543
  111.1 0.6 collective-permute-start.14
  111.7 1.1 collective-permute-start.15
  112.9 1.6 collective-permute-start.10
  114.5 14.8 %expert_head.3 = (f32[128,768]{1,0:T(8,128)}, f32[128,768]{1,0:T(8,128)}, f32[2,128]{1,0:T(2,128)S(1)}) custom-call(bf16[64,128,128]{2,1,0:T(8,128)(2,1)S(1)} %all-to-all-done.1.refs_0_, bf16[8192,768]{1,0:T(8,128)(2,1)} %refs_3_.3, bf16[8192,768]{1,0:T(8,128)(2,1)} %collective-permute-done.9.refs_2_.refs_4_, f32[64,128]{1,0:T(8,128)S(1)} %bitcast.98), custom_call_target="tpu_custom_call" | custom-call | flops 3221225472 | bytes 25165824 | tf_op jit(solution)/shard_map/expert_head/pallas_call | solution.py:241
  129.3 0.9 collective-permute-done.13.refs_0_
  130.2 1.7 collective-permute-done.14.refs_1_
  131.9 0.6 collective-permute-done.15.refs_2_
  132.5 10.0 %expert_head.4 = (f32[384,768]{1,0:T(8,128)S(1)}, f32[384,768]{1,0:T(8,128)S(1)}, f32[384,128]{1,0:T(8,128)S(1)}) custom-call(bf16[48,128,128]{2,1,0:T(8,128)(2,1)S(1)} %collective-permute-done.13.refs_0_, bf16[48,128,128]{2,1,0:T(8,128)(2,1)S(1)} %collective-permute-done.14.refs_1_, bf16[48,128,128]{2,1,0:T(8,128)(2,1)S(1)} %collective-permute-done.15.refs_2_, ...), custom_call_target="tpu_custom_call" | custom-call | flops 7247757312 | bytes 18874368 | tf_op jit(solution)/shard_map/expert_head/pallas_call | solution.py:241
  142.6 6.6 %expert_head.5 = (f32[384,768]{1,0:T(8,128)}, f32[384,768]{1,0:T(8,128)}, f32[6,128]{1,0:T(8,128)S(1)}) custom-call(bf16[16,128,128]{2,1,0:T(8,128)(2,1)S(1)} %collective-permute-done.10.refs_0_, bf16[16,128,128]{2,1,0:T(8,128)(2,1)S(1)} %collective-permute-done.11.refs_1_, bf16[16,128,128]{2,1,0:T(8,128)(2,1)S(1)} %collective-permute-done.12.refs_2_, ...), custom_call_target="tpu_custom_call" | custom-call | flops 2415919104 | bytes 6291456 | tf_op jit(solution)/shard_map/expert_head/pallas_call | solution.py:241
  149.2 3.8 %collective-permute-start.18 = (f32[384,768]{1,0:T(8,128)}, f32[384,768]{1,0:T(8,128)S(1)}, u32[]{:S(2)}, u32[]{:S(2)}) collective-permute-start(f32[384,768]{1,0:T(8,128)} %get-tuple-element.57), channel_id=1, source_target_pairs={{0,1},{1,0},{2,3},{3,2},{4,5},{5,4},{6,7},{7,6},{8,9},{9,8},{10,11... | collective-permute-start | bytes 3538952 | tf_op jit(solution)/shard_map/ppermute | solution.py:68
  153.0 1.4 spread_stats.1
  154.4 5.4 %all-to-all-start.2 = ((f32[64,16,128]{2,1,0:T(8,128)}), f32[64,16,128]{2,1,0:T(8,128)S(1)}, u32[]{:S(2)}, u32[]{:S(2)}) async-start(f32[64,16,128]{2,1,0:T(8,128)} %spread_stats.1), calls=%async_computation.2 | async-start | bytes 1048576 | tf_op jit(solution)/shard_map/all_to_all | solution.py:577
  160.2 12.5 %all-to-all-done.2.parts_ref = f32[64,16,128]{2,1,0:T(8,128)S(1)} async-done(((f32[64,16,128]{2,1,0:T(8,128)}), f32[64,16,128]{2,1,0:T(8,128)S(1)}, u32[]{:S(2)}, u32[]{:S(2)}) %all-to-all-start.2) | async-done | bytes 524320 | tf_op jit(solution)/shard_map/all_to_all | solution.py:577
  173.0 1.6 collective-permute-start.16
  174.5 0.8 collective-permute-done.16.theirs_ref
  175.4 0.5 copy-done.12
  176.4 5.0 %contrast.1 = f32[1024,768]{1,0:T(8,128)} custom-call(s32[2]{0:T(128)} %copy-done.6, f32[8,128]{1,0:T(8,128)} %copy-done.5, f32[8,128]{1,0:T(8,128)} %copy-done.12, f32[8,128]{1,0:T(8,128)} %mul.74.limit_ref, f32[128,768]{1,0:T(8,128)} %get-tuple-element.54.own_first_in, f32[384,768]{1,0:T(8,128)} %get-tuple-element.55.own_rest_in, f32[128,768]{1,0:T(8,128)} %copy-done.8, ...), custom_call_target="tpu_custom_call" | custom-call | flops 4718592 | bytes 7864320 | tf_op jit(solution)/shard_map/contrast/pallas_call | solution.py:459
  (82 shorter events, 3.7 us)
Async XLA Ops:
  6.5 9.4 %copy-start = (bf16[8,1024]{1,0:T(8,128)(2,1)S(1)}, bf16[8,1024]{1,0:T(8,128)(2,1)}, u32[]{:S(2)}) copy-start(bf16[8,1024]{1,0:T(8,128)(2,1)} %param.16) | copy-start | bytes 49156
  6.5 9.3 %copy-start.11 = (bf16[8,1024]{1,0:T(8,128)(2,1)S(1)}, bf16[8,1024]{1,0:T(8,128)(2,1)}, u32[]{:S(2)}) copy-start(bf16[8,1024]{1,0:T(8,128)(2,1)} %param.17) | copy-start | bytes 49156
  6.5 9.4 %copy-start.14 = (s32[8]{0:T(128)S(1)}, s32[8]{0:T(128)}, u32[]{:S(2)}) copy-start(s32[8]{0:T(128)} %param.18) | copy-start | bytes 100
  6.5 9.4 %copy-start.9 = (bf16[8,8192]{1,0:T(8,128)(2,1)S(1)}, bf16[8,8192]{1,0:T(8,128)(2,1)}, u32[]{:S(2)}) copy-start(bf16[8,8192]{1,0:T(8,128)(2,1)} %param.13) | copy-start | bytes 393220
  6.5 60.4 %all-gather.2.cloned.1.call-start = ((), (), s32[]{:S(2)}) async-start(), calls=%async_computation.3 | async-start | bytes 2293760 | tf_op jit(solution)/shard_map/all_gather | solution.py:513
  6.6 107.9 %collective-permute-start.9 = (bf16[8192,768]{1,0:T(8,128)(2,1)}, bf16[8192,768]{1,0:T(8,128)(2,1)}, u32[]{:S(2)}, u32[]{:S(2)}) collective-permute-start(bf16[8192,768]{1,0:T(8,128)(2,1)} %refs_3_.3), channel_id=1, source_target_pairs={{0,1},{1,0},{2,3},{3,2},{4,5},{5,4},{6,7},{7,6},{8,9},{9,8},{10,11... | collective-permute-start | bytes 37748744 | tf_op jit(solution)/shard_map/ppermute | solution.py:68
  10.1 21.9 %collective-permute-start = (bf16[64,2048]{1,0:T(8,128)(2,1)}, bf16[64,2048]{1,0:T(8,128)(2,1)S(1)}, u32[]{:S(2)}, u32[]{:S(2)}) collective-permute-start(bf16[64,2048]{1,0:T(8,128)(2,1)} %get-tuple-element.61), channel_id=1, source_target_pairs={{0,32},{32,64},{64,96},{96,0},{1,33},{33,65},{65,97},{97,1},{2,34}... | collective-permute-start | bytes 786440 | tf_op jit(solution)/shard_map/ppermute | solution.py:68
  11.8 20.2 %collective-permute-start.1 = (bf16[64,2048]{1,0:T(8,128)(2,1)}, bf16[64,2048]{1,0:T(8,128)(2,1)S(1)}, u32[]{:S(2)}, u32[]{:S(2)}) collective-permute-start(bf16[64,2048]{1,0:T(8,128)(2,1)} %get-tuple-element.63), channel_id=1, source_target_pairs={{0,64},{32,96},{64,0},{96,32},{1,65},{33,97},{65,1},{97,33},{2,66}... | collective-permute-start | bytes 786440 | tf_op jit(solution)/shard_map/ppermute | solution.py:68
  15.1 16.9 %collective-permute-start.2 = (bf16[64,2048]{1,0:T(8,128)(2,1)S(1)}, bf16[64,2048]{1,0:T(8,128)(2,1)S(1)}, u32[]{:S(2)}, u32[]{:S(2)}) collective-permute-start(bf16[64,2048]{1,0:T(8,128)(2,1)S(1)} %get-tuple-element.62), channel_id=1, source_target_pairs={{0,96},{32,0},{64,32},{96,64},{1,97},{33,1},{65,33},{97,65},{2,98}... | collective-permute-start | bytes 786440 | tf_op jit(solution)/shard_map/ppermute | solution.py:68
  16.2 3.9 %copy-start.15 = (bf16[8,256,1024]{2,1,0:T(8,128)(2,1)S(1)}, bf16[8,256,1024]{2,1,0:T(8,128)(2,1)}, u32[]{:S(2)}) copy-start(bf16[8,256,1024]{2,1,0:T(8,128)(2,1)} %param.15) | copy-start | bytes 12582916
  22.8 36.4 %all-to-all-start = ((bf16[64,128,128]{2,1,0:T(8,128)(2,1)}), bf16[64,128,128]{2,1,0:T(8,128)(2,1)S(1)}, u32[]{:S(2)}, u32[]{:S(2)}) async-start(bf16[64,128,128]{2,1,0:T(8,128)(2,1)} %bitcast.102), calls=%async_computation | async-start | bytes 4194304 | tf_op jit(solution)/shard_map/all_to_all | solution.py:514
  30.9 3.4 %copy-start.10 = (bf16[1024,64]{0,1:T(8,128)(2,1)S(1)}, bf16[1024,64]{0,1:T(8,128)(2,1)}, u32[]{:S(2)}) copy-start(bf16[1024,64]{0,1:T(8,128)(2,1)} %param.19) | copy-start | bytes 393220
  33.1 4.8 %collective-permute-start.3 = (bf16[4,64,2048]{2,1,0:T(8,128)(2,1)}, bf16[4,64,2048]{2,1,0:T(8,128)(2,1)}, u32[]{:S(2)}, u32[]{:S(2)}) collective-permute-start(bf16[4,64,2048]{2,1,0:T(8,128)(2,1)} %pad_maximum_fusion.1), channel_id=1, source_target_pairs={{0,1},{1,0},{2,3},{3,2},{4,5},{5,4},{6,7},{7,6},{8,9},{9,8},{10,11... | collective-permute-start | bytes 3145736 | tf_op jit(solution)/shard_map/ppermute | solution.py:68
  34.5 2.4 %collective-permute-start.4 = (bf16[64,64,8]{0,2,1:T(8,128)(2,1)S(1)}, bf16[64,64,8]{0,2,1:T(8,128)(2,1)}, u32[]{:S(2)}, u32[]{:S(2)}) collective-permute-start(bf16[64,64,8]{0,2,1:T(8,128)(2,1)S(1)} %dynamic-slice_bitcast_fusion.4), channel_id=1, source_target_pairs={{0,1},{1,0},{2,3},{3,2},{4,5},{5,4},{6,7},{7,6},{8,9},{9,8},{10,11... | collective-permute-start | bytes 196616 | tf_op jit(solution)/shard_map/ppermute | solution.py:68
  62.2 4.9 %collective-permute-start.5 = (bf16[512,128]{1,0:T(8,128)(2,1)S(1)}, bf16[512,128]{1,0:T(8,128)(2,1)S(1)}, u32[]{:S(2)}, u32[]{:S(2)}) collective-permute-start(bf16[512,128]{1,0:T(8,128)(2,1)S(1)} %get-tuple-element.37), channel_id=1, source_target_pairs={{0,96},{32,0},{64,32},{96,64},{1,97},{33,1},{65,33},{97,65},{2,98}... | collective-permute-start | bytes 393224 | tf_op jit(solution)/shard_map/ppermute | solution.py:68
  62.7 5.5 %collective-permute-start.6 = (bf16[512,128]{1,0:T(8,128)(2,1)S(1)}, bf16[512,128]{1,0:T(8,128)(2,1)S(1)}, u32[]{:S(2)}, u32[]{:S(2)}) collective-permute-start(bf16[512,128]{1,0:T(8,128)(2,1)S(1)} %get-tuple-element.38), channel_id=1, source_target_pairs={{0,64},{32,96},{64,0},{96,32},{1,65},{33,97},{65,1},{97,33},{2,66}... | collective-permute-start | bytes 393224 | tf_op jit(solution)/shard_map/ppermute | solution.py:68
  64.1 5.4 %collective-permute-start.7 = (bf16[512,128]{1,0:T(8,128)(2,1)S(1)}, bf16[512,128]{1,0:T(8,128)(2,1)S(1)}, u32[]{:S(2)}, u32[]{:S(2)}) collective-permute-start(bf16[512,128]{1,0:T(8,128)(2,1)S(1)} %get-tuple-element.39), channel_id=1, source_target_pairs={{0,32},{32,64},{64,96},{96,0},{1,33},{33,65},{65,97},{97,1},{2,34}... | collective-permute-start | bytes 393224 | tf_op jit(solution)/shard_map/ppermute | solution.py:68
  71.1 11.1 %copy-start.13 = (s32[1024]{0:T(1024)S(1)}, s32[1024]{0:T(1024)}, u32[]{:S(2)}) copy-start(s32[1024]{0:T(1024)} %param.25) | copy-start | bytes 12292
  71.1 39.4 %all-to-all-start.1 = ((bf16[64,128,128]{2,1,0:T(8,128)(2,1)}), bf16[64,128,128]{2,1,0:T(8,128)(2,1)S(1)}, u32[]{:S(2)}, u32[]{:S(2)}) async-start(bf16[64,128,128]{2,1,0:T(8,128)(2,1)} %bitcast.103), calls=%async_computation.1 | async-start | bytes 4194304 | tf_op jit(solution)/shard_map/all_to_all | solution.py:543
  82.2 2.6 %copy-start.2 = (bf16[896,3072]{1,0:T(8,128)(2,1)S(1)}, bf16[896,3072]{1,0:T(8,128)(2,1)}, u32[]{:S(2)}) copy-start(bf16[896,3072]{1,0:T(8,128)(2,1)} %weight_ref.1) | copy-start | bytes 16515076
  84.8 1.5 copy-start.3
  90.7 2.1 %collective-permute-start.8 = (f32[4,2,128]{2,1,0:T(2,128)S(1)}, f32[4,2,128]{2,1,0:T(2,128)S(1)}, u32[]{:S(2)}, u32[]{:S(2)}) collective-permute-start(f32[4,2,128]{2,1,0:T(2,128)S(1)} %get-tuple-element.71), channel_id=1, source_target_pairs={{0,1},{1,0},{2,3},{3,2},{4,5},{5,4},{6,7},{7,6},{8,9},{9,8},{10,11... | collective-permute-start | bytes 12296 | tf_op jit(solution)/shard_map/ppermute | solution.py:68
  91.9 61.0 %copy-start.6 = (s32[2]{0:T(128)}, s32[2]{0:T(128)S(1)}, u32[]{:S(2)}) copy-start(s32[2]{0:T(128)S(1)} %pad_add_fusion.place_ref) | copy-start | bytes 28
  110.5 4.0 %copy-start.4 = (f32[8192]{0:T(1024)S(1)}, f32[8192]{0:T(1024)}, u32[]{:S(2)}) copy-start(f32[8192]{0:T(1024)} %param.20) | copy-start | bytes 98308
  110.6 19.6 %collective-permute-start.13 = (bf16[48,128,128]{2,1,0:T(8,128)(2,1)S(1)}, bf16[48,128,128]{2,1,0:T(8,128)(2,1)S(1)}, u32[]{:S(2)}, u32[]{:S(2)}) collective-permute-start(bf16[48,128,128]{2,1,0:T(8,128)(2,1)S(1)} %slice.20), channel_id=1, source_target_pairs={{0,6},{1,97},{2,0},{3,99},{4,2},{5,101},{6,4},{7,103},{8,14},{9,10... | collective-permute-start | bytes 4718600 | tf_op jit(solution)/shard_map/ppermute | solution.py:80
  111.1 20.8 %collective-permute-start.14 = (bf16[48,128,128]{2,1,0:T(8,128)(2,1)S(1)}, bf16[48,128,128]{2,1,0:T(8,128)(2,1)S(1)}, u32[]{:S(2)}, u32[]{:S(2)}) collective-permute-start(bf16[48,128,128]{2,1,0:T(8,128)(2,1)S(1)} %slice.20), channel_id=1, source_target_pairs={{0,24},{1,9},{2,26},{3,11},{4,28},{5,13},{6,30},{7,15},{8,0},{9,17... | collective-permute-start | bytes 4718600 | tf_op jit(solution)/shard_map/ppermute | solution.py:80
  111.7 20.8 %collective-permute-start.15 = (bf16[48,128,128]{2,1,0:T(8,128)(2,1)S(1)}, bf16[48,128,128]{2,1,0:T(8,128)(2,1)S(1)}, u32[]{:S(2)}, u32[]{:S(2)}) collective-permute-start(bf16[48,128,128]{2,1,0:T(8,128)(2,1)S(1)} %slice.20), channel_id=1, source_target_pairs={{0,2},{1,33},{2,4},{3,35},{4,6},{5,37},{6,0},{7,39},{8,10},{9,41},... | collective-permute-start | bytes 4718600 | tf_op jit(solution)/shard_map/ppermute | solution.py:80
  112.9 29.7 %collective-permute-start.10 = (bf16[16,128,128]{2,1,0:T(8,128)(2,1)S(1)}, bf16[16,128,128]{2,1,0:T(8,128)(2,1)S(1)}, u32[]{:S(2)}, u32[]{:S(2)}) collective-permute-start(bf16[16,128,128]{2,1,0:T(8,128)(2,1)S(1)} %slice.19), channel_id=1, source_target_pairs={{0,6},{1,97},{2,0},{3,99},{4,2},{5,101},{6,4},{7,103},{8,14},{9,10... | collective-permute-start | bytes 1572872 | tf_op jit(solution)/shard_map/ppermute | solution.py:80
  114.5 28.1 %collective-permute-start.11 = (bf16[16,128,128]{2,1,0:T(8,128)(2,1)S(1)}, bf16[16,128,128]{2,1,0:T(8,128)(2,1)S(1)}, u32[]{:S(2)}, u32[]{:S(2)}) collective-permute-start(bf16[16,128,128]{2,1,0:T(8,128)(2,1)S(1)} %slice.19), channel_id=1, source_target_pairs={{0,24},{1,9},{2,26},{3,11},{4,28},{5,13},{6,30},{7,15},{8,0},{9,17... | collective-permute-start | bytes 1572872 | tf_op jit(solution)/shard_map/ppermute | solution.py:80
  114.5 18.0 %slice-start = ((s8[12582912]{0:T(1024)(128)(4,1)}), s8[4194304]{0:T(1024)(128)(4,1)S(1)}, s32[]{:S(2)}) async-start(s8[12582912]{0:T(1024)(128)(4,1)} %bitcast.95), calls=%async_computation.4 | async-start | bytes 8388608
  114.5 18.0 %slice-start.1 = ((s8[12582912]{0:T(1024)(128)(4,1)}), s8[4194304]{0:T(1024)(128)(4,1)S(1)}, s32[]{:S(2)}) async-start(s8[12582912]{0:T(1024)(128)(4,1)} %bitcast.95), calls=%async_computation.5 | async-start | bytes 8388608
  114.5 18.0 %slice-start.2 = ((s8[12582912]{0:T(1024)(128)(4,1)}), s8[4194304]{0:T(1024)(128)(4,1)S(1)}, s32[]{:S(2)}) async-start(s8[12582912]{0:T(1024)(128)(4,1)} %bitcast.95), calls=%async_computation.6 | async-start | bytes 8388608
  130.2 12.3 %collective-permute-start.12 = (bf16[16,128,128]{2,1,0:T(8,128)(2,1)S(1)}, bf16[16,128,128]{2,1,0:T(8,128)(2,1)S(1)}, u32[]{:S(2)}, u32[]{:S(2)}) collective-permute-start(bf16[16,128,128]{2,1,0:T(8,128)(2,1)S(1)} %slice.19), channel_id=1, source_target_pairs={{0,2},{1,33},{2,4},{3,35},{4,6},{5,37},{6,0},{7,39},{8,10},{9,41},... | collective-permute-start | bytes 1572872 | tf_op jit(solution)/shard_map/ppermute | solution.py:80
  142.5 17.2 %copy-start.16 = (f32[128,768]{1,0:T(8,128)S(1)}, f32[128,768]{1,0:T(8,128)}, u32[]{:S(2)}) copy-start(f32[128,768]{1,0:T(8,128)} %get-tuple-element.56) | copy-start | bytes 1179652
  149.2 26.2 %collective-permute-start.18 = (f32[384,768]{1,0:T(8,128)}, f32[384,768]{1,0:T(8,128)S(1)}, u32[]{:S(2)}, u32[]{:S(2)}) collective-permute-start(f32[384,768]{1,0:T(8,128)} %get-tuple-element.57), channel_id=1, source_target_pairs={{0,1},{1,0},{2,3},{3,2},{4,5},{5,4},{6,7},{7,6},{8,9},{9,8},{10,11... | collective-permute-start | bytes 3538952 | tf_op jit(solution)/shard_map/ppermute | solution.py:68
  154.4 18.2 %all-to-all-start.2 = ((f32[64,16,128]{2,1,0:T(8,128)}), f32[64,16,128]{2,1,0:T(8,128)S(1)}, u32[]{:S(2)}, u32[]{:S(2)}) async-start(f32[64,16,128]{2,1,0:T(8,128)} %spread_stats.1), calls=%async_computation.2 | async-start | bytes 1048576 | tf_op jit(solution)/shard_map/all_to_all | solution.py:577
  159.8 14.7 %collective-permute-start.17 = (f32[128,768]{1,0:T(8,128)S(1)}, f32[128,768]{1,0:T(8,128)S(1)}, u32[]{:S(2)}, u32[]{:S(2)}) collective-permute-start(f32[128,768]{1,0:T(8,128)S(1)} %copy-done.16), channel_id=1, source_target_pairs={{0,1},{1,0},{2,3},{3,2},{4,5},{5,4},{6,7},{7,6},{8,9},{9,8},{10,11... | collective-permute-start | bytes 1179656 | tf_op jit(solution)/shard_map/ppermute | solution.py:68
  172.9 2.4 %copy-start.5 = (f32[8,128]{1,0:T(8,128)}, f32[8,128]{1,0:T(8,128)S(1)}, u32[]{:S(2)}) copy-start(f32[8,128]{1,0:T(8,128)S(1)} %merge_stats.1.mine_ref) | copy-start | bytes 12292
  173.0 2.4 %collective-permute-start.16 = (f32[8,128]{1,0:T(8,128)S(1)}, f32[8,128]{1,0:T(8,128)S(1)}, u32[]{:S(2)}, u32[]{:S(2)}) collective-permute-start(f32[8,128]{1,0:T(8,128)S(1)} %merge_stats.1.mine_ref), channel_id=1, source_target_pairs={{0,1},{1,0},{2,3},{3,2},{4,5},{5,4},{6,7},{7,6},{8,9},{9,8},{10,11... | collective-permute-start | bytes 12296 | tf_op jit(solution)/shard_map/ppermute | solution.py:68
  174.5 0.8 copy-start.8
  175.3 0.6 copy-start.12
  175.3 1.1 copy-start.7
  175.3 6.1 %copy-start.1 = (bf16[8,1024]{1,0:T(8,128)(2,1)S(1)}, bf16[8,1024]{1,0:T(8,128)(2,1)}, u32[]{:S(2)}) copy-start(bf16[8,1024]{1,0:T(8,128)(2,1)} %param.16) | copy-start | bytes 49156
Sparse Core Ops, SparseCore 0:
  16.0 50.9 all-gather.1

commit v4 on v3

--- a/solution.py
+++ b/solution.py
@@ -315,10 +315,23 @@
     for piece in range(quarters):
         at = pl.ds(2 * lax.rem(place_ref[0] + piece, quarters), 2)
         stats_ref[at] = first_ref[...] if piece == 0 else rest_ref[2 * piece - 2 : 2 * piece]
-    stats_ref[2 * quarters :] = amateur_ref[...]
-    for target in range(group_ref.shape[0]):
-        group_ref[target] = stats_ref[...]
+    amateur = amateur_ref[...]
+    rows = []
+    for quarter in range(quarters):
+        at = 2 * quarter
+        largest = stats_ref[at : at + 1]
+        coarse = largest.astype(jnp.bfloat16).astype(jnp.float32)
+        amateur_lse = amateur[at : at + 1] + jnp.log(amateur[at + 1 : at + 2])
+        rows += [
+            coarse,
+            largest - coarse,
+            stats_ref[at + 1 : at + 2],
+            amateur_lse - largest,
+        ]
+    packed = jnp.concatenate(rows, axis=0).astype(jnp.bfloat16)
     many = group_ref.shape[0]
+    for target in range(many):
+        group_ref[target] = packed
     copies = [
         pltpu.make_async_copy(group_ref, out_ref.at[pl.ds(at, many)], sem.at[at // many])
         for at in range(0, out_ref.shape[0], many)
@@ -331,16 +344,17 @@
 
 def spread(place, first, rest, amateur, targets):
     rows = 2 * amateur.shape[0]
+    many = 16
     vmem = pl.BlockSpec(memory_space=pltpu.VMEM)
     return pl.pallas_call(
         spread_kernel,
         in_specs=[pl.BlockSpec(memory_space=pltpu.SMEM)] + [vmem] * 3,
         out_specs=pl.BlockSpec(memory_space=pltpu.HBM),
-        out_shape=pltpu.HBM((targets, rows, LINE), jnp.float32),
+        out_shape=pltpu.HBM((targets, rows, LINE), jnp.bfloat16),
         scratch_shapes=[
-            pltpu.VMEM((rows, LINE), jnp.float32),
-            pltpu.VMEM((8, rows, LINE), jnp.float32),
-            pltpu.SemaphoreType.DMA((targets // 8,)),
+            pltpu.VMEM(amateur.shape, jnp.float32),
+            pltpu.VMEM((many, rows, LINE), jnp.bfloat16),
+            pltpu.SemaphoreType.DMA((targets // many,)),
         ],
         compiler_params=params(4),
         name="spread_stats",
@@ -348,19 +362,19 @@
 
 
 def merge_kernel(parts_ref, out_ref):
-    parts = parts_ref[...]
-    largest = jnp.max(parts, axis=0)
-    quarters = out_ref.shape[0] // 2
-    tops, sums = [], []
-    for tile in range(2 * quarters):
-        top = largest[2 * tile : 2 * tile + 1]
-        scales = jnp.exp(parts[:, 2 * tile] - top)
+    parts = parts_ref[...].astype(jnp.float32)
+    tops, shifts = [], []
+    for quarter in range(out_ref.shape[0] // 2):
+        coarse, fine, sums, apart = (parts[:, 4 * quarter + i] for i in range(4))
+        largest = coarse + fine
+        amateur = largest + apart
+        top = jnp.max(largest, axis=0, keepdims=True)
+        amateur_top = jnp.max(amateur, axis=0, keepdims=True)
+        total = jnp.sum(sums * jnp.exp(largest - top), axis=0, keepdims=True)
+        amateur_total = jnp.sum(jnp.exp(amateur - amateur_top), axis=0, keepdims=True)
         tops.append(top)
-        sums.append(
-            top + jnp.log(jnp.sum(parts[:, 2 * tile + 1] * scales, axis=0, keepdims=True))
-        )
-    shifts = [sums[tile] - sums[quarters + tile] for tile in range(quarters)]
-    out_ref[...] = jnp.concatenate(tops[:quarters] + shifts, axis=0)
+        shifts.append((top + jnp.log(total)) - (amateur_top + jnp.log(amateur_total)))
+    out_ref[...] = jnp.concatenate(tops + shifts, axis=0)
 
 
 def merge(parts):

time: 189 us -> 186 us (0.984)
  blocking collectives: 0 us -> 15.1 us
  waiting for transfers between devices: 60.1 us -> 47.6 us
  starting transfers between devices: 45.8 us -> 40.4 us
    all_to_all x0 -> x1, blocking collectives: none -> 15.1 us  [body(): lax.all_to_all(copies, CHIPS, split_axis=0, concat_axis=0, tiled=True)]
    all_to_all x3 -> x2, waiting for transfers between devices: 48.3 us -> 35.9 us  [body(): lax.all_to_all(copies, CHIPS, split_axis=0, concat_axis=0, tiled=True)]
    all_to_all x3 -> x2, starting transfers between devices: 24.6 us -> 19.2 us  [body(): lax.all_to_all(copies, CHIPS, split_axis=0, concat_axis=0, tiled=True)]
  transfers between devices with their start and end apart: 23 -> 22, of which waited for: 12 -> 11; matrix products, arithmetic and copies ran while one was open for 9% -> 9% of each run, Pallas kernels for 19% -> 19%
where the time goes in v4:
time: 186 us
  waiting for transfers between devices  47.6 us (26%)
  Pallas kernels  47.1 us (25%)
  starting transfers between devices  40.4 us (22%)
  blocking collectives  15.1 us (8%)
  between operations  13.8 us (7%)
  local copies, waits for them, and re-layouts  12.7 us (7%)
  matrix products  4.55 us (2%)
  other arithmetic  4.28 us (2%)
    all_to_all x2, waiting for transfers between devices, body(): lax.all_to_all(copies, CHIPS, split_axis=0, concat_axis=0, tiled=True)  35.9 us
    pallas_call x3, Pallas kernels, head(): pl.pallas_call(functools.partial(head_kernel, pieces, steps, features, re...  31.5 us
    all_to_all x2, starting transfers between devices, body(): lax.all_to_all(copies, CHIPS, split_axis=0, concat_axis=0, tiled=True)  19.2 us
    ppermute x13, starting transfers between devices, shift(): return lax.ppermute(x, axis, [(i, (i + step) % size) for i in range(size)])  17.3 us
    all_to_all x1, blocking collectives, body(): lax.all_to_all(copies, CHIPS, split_axis=0, concat_axis=0, tiled=True)  15.1 us
    ppermute x13, waiting for transfers between devices, shift(): return lax.ppermute(x, axis, [(i, (i + step) % size) for i in range(size)])  5.78 us
    unnamed x40, local copies, waits for them, and re-layouts  5.15 us
    pallas_call x1, Pallas kernels, contrast(): pl.pallas_call(contrast_kernel, in_specs=[pl.BlockSpec(memory_space=pltpu...  5.03 us
  transfers between devices with their start and end apart: 22, of which 11 were waited for; matrix products, arithmetic and copies ran while one was open for 9% of the time, Pallas kernels for 19%

profile of v4, /device:TPU:1, one launch (start us, length us, event | category | flops | bytes accessed | tf_op | source)
XLA Modules:
  0.0 185.6 jit_solution(15004282415840971941)
XLA Ops:
  6.6 1.5 collective-permute-start.9
  8.1 2.0 %dynamic-slice_bitcast_fusion.2 = (bf16[64,2048]{1,0:T(8,128)(2,1)}, bf16[64,2048]{1,0:T(8,128)(2,1)S(1)}, bf16[64,2048]{1,0:T(8,128)(2,1)}) fusion(bf16[8192,64]{0,1:T(8,128)(2,1)} %param.21, s32[]{:T(128)S(6)} %select_n.64, s32[]{:T(128)S(6)} %select_n.66, s32[]{:T(128)S(6)} %select_n.65), kind=kLoop, calls=%fused_computation.19 | loop fusion | bytes 1572876 | tf_op jit(solution)/shard_map/dynamic_slice | solution.py:535
  10.1 1.7 collective-permute-start
  11.8 3.3 %collective-permute-start.1 = (bf16[64,2048]{1,0:T(8,128)(2,1)}, bf16[64,2048]{1,0:T(8,128)(2,1)S(1)}, u32[]{:S(2)}, u32[]{:S(2)}) collective-permute-start(bf16[64,2048]{1,0:T(8,128)(2,1)} %get-tuple-element.63), channel_id=1, source_target_pairs={{0,64},{32,96},{64,0},{96,32},{1,65},{33,97},{65,1},{97,33},{2,66}... | collective-permute-start | bytes 786440 | tf_op jit(solution)/shard_map/ppermute | solution.py:68
  15.1 0.7 collective-permute-start.2
  16.2 3.6 %fusion.31 = (f32[8,8,8]{2,1,0:T(8,128)S(1)}, f32[8,8,8,256]{3,2,1,0:T(8,128)S(1)}) fusion(bf16[8,8,8,128]{3,0,2,1:T(8,128)(2,1)S(1)} %bitcast.116, pred[8,256]{1,0:T(8,128)(4,1)S(1)} %iota_compare_fusion, bf16[8,256,1024]{2,1,0:T(8,128)(2,1)} %param.14), kind=kOutput, calls=%fused_computation.52 | convolution fusion | flops 33947136 | bytes 4853760 | tf_op jit(solution)/shard_map/rkgd,rlkd->rkgl/dot_general | solution.py:35
  20.1 0.7 fusion.15
  21.0 1.8 broadcast_in_dim.36
  22.8 8.1 %all-to-all-start = ((bf16[64,128,128]{2,1,0:T(8,128)(2,1)}), bf16[64,128,128]{2,1,0:T(8,128)(2,1)S(1)}, u32[]{:S(2)}, u32[]{:S(2)}) async-start(bf16[64,128,128]{2,1,0:T(8,128)(2,1)} %bitcast.102), calls=%async_computation | async-start | bytes 4194304 | tf_op jit(solution)/shard_map/all_to_all | solution.py:528
  31.0 1.0 dynamic-slice_bitcast_fusion.3
  32.0 1.1 pad_maximum_fusion.1
  33.1 1.2 collective-permute-start.3
  34.6 2.3 %collective-permute-done.4 = bf16[64,64,8]{0,2,1:T(8,128)(2,1)} collective-permute-done((bf16[64,64,8]{0,2,1:T(8,128)(2,1)S(1)}, bf16[64,64,8]{0,2,1:T(8,128)(2,1)}, u32[]{:S(2)}, u32[]{:S(2)}) %collective-permute-start.4) | collective-permute-done | bytes 65568 | tf_op jit(solution)/shard_map/ppermute | solution.py:68
  36.9 0.9 bitcast_select_fusion.1
  38.0 1.4 select_bitcast_fusion.1
  39.6 1.4 copy.27
  41.0 18.2 %all-to-all-done = bf16[64,128,128]{2,1,0:T(8,128)(2,1)S(1)} async-done(((bf16[64,128,128]{2,1,0:T(8,128)(2,1)}), bf16[64,128,128]{2,1,0:T(8,128)(2,1)S(1)}, u32[]{:S(2)}, u32[]{:S(2)}) %all-to-all-start) | async-done | bytes 2097184 | tf_op jit(solution)/shard_map/all_to_all | solution.py:528
  59.3 2.9 %projection.1 = (f32[512,128]{1,0:T(8,128)S(1)}, bf16[512,128]{1,0:T(8,128)(2,1)S(1)}, bf16[512,128]{1,0:T(8,128)(2,1)S(1)}, bf16[512,128]{1,0:T(8,128)(2,1)S(1)}) custom-call(bf16[512,2048]{1,0:T(8,128)(2,1)S(1)} %bitcast.97, bf16[512,2048]{1,0:T(8,128)(2,1)} %bitcast.104, bf16[512,128]{1,0:T(8,128)(2,1)S(1)} %maximum_bitcast_fusion.base_ref), custom_call_target="tpu_custom_call" | custom-call | flops 1073741824 | bytes 4194304 | tf_op jit(solution)/shard_map/projection/pallas_call | solution.py:111
  62.1 0.6 collective-permute-start.5
  62.7 1.4 collective-permute-start.6
  64.1 2.8 %all-gather.2.cloned.1.call-done.hidden_ref = bf16[1024,896]{1,0:T(8,128)(2,1)} async-done(((bf16[256,896]{1,0:T(8,128)(2,1)}), bf16[1024,896]{1,0:T(8,128)(2,1)}) %all-gather.2.cloned.1.call-update) | async-done | bytes 1835024 | tf_op jit(solution)/shard_map/all_gather | solution.py:527
  67.0 1.2 collective-permute-done.6.refs_1_
  68.2 1.4 collective-permute-done.7.refs_2_
  69.5 1.5 hidden.1
  71.1 11.1 %all-to-all-start.1 = ((bf16[64,128,128]{2,1,0:T(8,128)(2,1)}), bf16[64,128,128]{2,1,0:T(8,128)(2,1)S(1)}, u32[]{:S(2)}, u32[]{:S(2)}) async-start(bf16[64,128,128]{2,1,0:T(8,128)(2,1)} %bitcast.103), calls=%async_computation.1 | async-start | bytes 4194304 | tf_op jit(solution)/shard_map/all_to_all | solution.py:557
  82.2 2.6 %copy-done.2 = bf16[896,3072]{1,0:T(8,128)(2,1)S(1)} copy-done((bf16[896,3072]{1,0:T(8,128)(2,1)S(1)}, bf16[896,3072]{1,0:T(8,128)(2,1)}, u32[]{:S(2)}) %copy-start.2) | copy-done | bytes 5505048
  84.7 1.5 copy-done.3
  86.2 4.4 %amateur_head.1 = (bf16[1024,768]{1,0:T(8,128)(2,1)}, f32[4,2,2,128]{3,2,1,0:T(2,128)S(1)}) custom-call(s32[1]{0:T(128)} %bitcast.33.place_ref, bf16[1024,896]{1,0:T(8,128)(2,1)S(1)} %copy-done.3, bf16[896,3072]{1,0:T(8,128)(2,1)S(1)} %copy-done.2), custom_call_target="tpu_custom_call" | custom-call | flops 1409286144 | bytes 4784128 | tf_op jit(solution)/shard_map/amateur_head/pallas_call | solution.py:277
  90.7 1.2 collective-permute-start.8
  92.1 0.7 mul.74.limit_ref
  92.8 17.6 %all-to-all-done.1.refs_0_ = bf16[64,128,128]{2,1,0:T(8,128)(2,1)S(1)} async-done(((bf16[64,128,128]{2,1,0:T(8,128)(2,1)}), bf16[64,128,128]{2,1,0:T(8,128)(2,1)S(1)}, u32[]{:S(2)}, u32[]{:S(2)}) %all-to-all-start.1) | async-done | bytes 2097184 | tf_op jit(solution)/shard_map/all_to_all | solution.py:557
  110.6 0.5 collective-permute-start.13
  111.1 0.6 collective-permute-start.14
  111.7 1.1 collective-permute-start.15
  112.9 1.6 collective-permute-start.10
  114.5 14.8 %expert_head.3 = (f32[128,768]{1,0:T(8,128)}, f32[128,768]{1,0:T(8,128)}, f32[2,128]{1,0:T(2,128)S(1)}) custom-call(bf16[64,128,128]{2,1,0:T(8,128)(2,1)S(1)} %all-to-all-done.1.refs_0_, bf16[8192,768]{1,0:T(8,128)(2,1)} %refs_3_.3, bf16[8192,768]{1,0:T(8,128)(2,1)} %collective-permute-done.9.refs_2_.refs_4_, f32[64,128]{1,0:T(8,128)S(1)} %bitcast.98), custom_call_target="tpu_custom_call" | custom-call | flops 3221225472 | bytes 25165824 | tf_op jit(solution)/shard_map/expert_head/pallas_call | solution.py:241
  129.3 0.9 collective-permute-done.13.refs_0_
  130.2 1.7 collective-permute-done.14.refs_1_
  131.9 0.6 collective-permute-done.15.refs_2_
  132.5 10.0 %expert_head.4 = (f32[384,768]{1,0:T(8,128)S(1)}, f32[384,768]{1,0:T(8,128)S(1)}, f32[384,128]{1,0:T(8,128)S(1)}) custom-call(bf16[48,128,128]{2,1,0:T(8,128)(2,1)S(1)} %collective-permute-done.13.refs_0_, bf16[48,128,128]{2,1,0:T(8,128)(2,1)S(1)} %collective-permute-done.14.refs_1_, bf16[48,128,128]{2,1,0:T(8,128)(2,1)S(1)} %collective-permute-done.15.refs_2_, ...), custom_call_target="tpu_custom_call" | custom-call | flops 7247757312 | bytes 18874368 | tf_op jit(solution)/shard_map/expert_head/pallas_call | solution.py:241
  142.6 6.6 %expert_head.5 = (f32[384,768]{1,0:T(8,128)}, f32[384,768]{1,0:T(8,128)}, f32[6,128]{1,0:T(8,128)S(1)}) custom-call(bf16[16,128,128]{2,1,0:T(8,128)(2,1)S(1)} %collective-permute-done.10.refs_0_, bf16[16,128,128]{2,1,0:T(8,128)(2,1)S(1)} %collective-permute-done.11.refs_1_, bf16[16,128,128]{2,1,0:T(8,128)(2,1)S(1)} %collective-permute-done.12.refs_2_, ...), custom_call_target="tpu_custom_call" | custom-call | flops 2415919104 | bytes 6291456 | tf_op jit(solution)/shard_map/expert_head/pallas_call | solution.py:241
  149.2 3.8 %collective-permute-start.18 = (f32[384,768]{1,0:T(8,128)}, f32[384,768]{1,0:T(8,128)S(1)}, u32[]{:S(2)}, u32[]{:S(2)}) collective-permute-start(f32[384,768]{1,0:T(8,128)} %get-tuple-element.57), channel_id=1, source_target_pairs={{0,1},{1,0},{2,3},{3,2},{4,5},{5,4},{6,7},{7,6},{8,9},{9,8},{10,11... | collective-permute-start | bytes 3538952 | tf_op jit(solution)/shard_map/ppermute | solution.py:68
  153.0 1.3 spread_stats.1
  154.3 15.1 %all_to_all.19.parts_ref = bf16[64,16,128]{2,1,0:T(8,128)(2,1)S(1)} all-to-all(bf16[64,16,128]{2,1,0:T(8,128)(2,1)} %spread_stats.1), channel_id=1, replica_groups=mesh['z'=4,'y'=4,'x'=4,'core'=2] {'z','y','x'}, dimensions={0} | all-to-all | bytes 524288 | tf_op jit(solution)/shard_map/all_to_all | solution.py:591
  169.9 1.9 %collective-permute-start.16 = (f32[8,128]{1,0:T(8,128)S(1)}, f32[8,128]{1,0:T(8,128)S(1)}, u32[]{:S(2)}, u32[]{:S(2)}) collective-permute-start(f32[8,128]{1,0:T(8,128)S(1)} %merge_stats.1.mine_ref), channel_id=1, source_target_pairs={{0,1},{1,0},{2,3},{3,2},{4,5},{5,4},{6,7},{7,6},{8,9},{9,8},{10,11... | collective-permute-start | bytes 12296 | tf_op jit(solution)/shard_map/ppermute | solution.py:68
  171.8 0.8 collective-permute-done.16.theirs_ref
  172.7 0.6 copy-done.12
  173.7 5.0 %contrast.1 = f32[1024,768]{1,0:T(8,128)} custom-call(s32[2]{0:T(128)} %copy-done.6, f32[8,128]{1,0:T(8,128)} %copy-done.5, f32[8,128]{1,0:T(8,128)} %copy-done.12, f32[8,128]{1,0:T(8,128)} %mul.74.limit_ref, f32[128,768]{1,0:T(8,128)} %get-tuple-element.54.own_first_in, f32[384,768]{1,0:T(8,128)} %get-tuple-element.55.own_rest_in, f32[128,768]{1,0:T(8,128)} %copy-done.8, ...), custom_call_target="tpu_custom_call" | custom-call | flops 4718592 | bytes 7864320 | tf_op jit(solution)/shard_map/contrast/pallas_call | solution.py:473
  (81 shorter events, 3.0 us)
Async XLA Ops:
  6.5 9.4 %copy-start = (bf16[8,1024]{1,0:T(8,128)(2,1)S(1)}, bf16[8,1024]{1,0:T(8,128)(2,1)}, u32[]{:S(2)}) copy-start(bf16[8,1024]{1,0:T(8,128)(2,1)} %param.16) | copy-start | bytes 49156
  6.5 9.3 %copy-start.11 = (bf16[8,1024]{1,0:T(8,128)(2,1)S(1)}, bf16[8,1024]{1,0:T(8,128)(2,1)}, u32[]{:S(2)}) copy-start(bf16[8,1024]{1,0:T(8,128)(2,1)} %param.17) | copy-start | bytes 49156
  6.5 9.3 %copy-start.14 = (s32[8]{0:T(128)S(1)}, s32[8]{0:T(128)}, u32[]{:S(2)}) copy-start(s32[8]{0:T(128)} %param.18) | copy-start | bytes 100
  6.5 9.4 %copy-start.9 = (bf16[8,8192]{1,0:T(8,128)(2,1)S(1)}, bf16[8,8192]{1,0:T(8,128)(2,1)}, u32[]{:S(2)}) copy-start(bf16[8,8192]{1,0:T(8,128)(2,1)} %param.13) | copy-start | bytes 393220
  6.5 60.4 %all-gather.2.cloned.1.call-start = ((), (), s32[]{:S(2)}) async-start(), calls=%async_computation.3 | async-start | bytes 2293760 | tf_op jit(solution)/shard_map/all_gather | solution.py:527
  6.6 107.9 %collective-permute-start.9 = (bf16[8192,768]{1,0:T(8,128)(2,1)}, bf16[8192,768]{1,0:T(8,128)(2,1)}, u32[]{:S(2)}, u32[]{:S(2)}) collective-permute-start(bf16[8192,768]{1,0:T(8,128)(2,1)} %refs_3_.3), channel_id=1, source_target_pairs={{0,1},{1,0},{2,3},{3,2},{4,5},{5,4},{6,7},{7,6},{8,9},{9,8},{10,11... | collective-permute-start | bytes 37748744 | tf_op jit(solution)/shard_map/ppermute | solution.py:68
  10.1 21.9 %collective-permute-start = (bf16[64,2048]{1,0:T(8,128)(2,1)}, bf16[64,2048]{1,0:T(8,128)(2,1)S(1)}, u32[]{:S(2)}, u32[]{:S(2)}) collective-permute-start(bf16[64,2048]{1,0:T(8,128)(2,1)} %get-tuple-element.61), channel_id=1, source_target_pairs={{0,32},{32,64},{64,96},{96,0},{1,33},{33,65},{65,97},{97,1},{2,34}... | collective-permute-start | bytes 786440 | tf_op jit(solution)/shard_map/ppermute | solution.py:68
  11.8 20.2 %collective-permute-start.1 = (bf16[64,2048]{1,0:T(8,128)(2,1)}, bf16[64,2048]{1,0:T(8,128)(2,1)S(1)}, u32[]{:S(2)}, u32[]{:S(2)}) collective-permute-start(bf16[64,2048]{1,0:T(8,128)(2,1)} %get-tuple-element.63), channel_id=1, source_target_pairs={{0,64},{32,96},{64,0},{96,32},{1,65},{33,97},{65,1},{97,33},{2,66}... | collective-permute-start | bytes 786440 | tf_op jit(solution)/shard_map/ppermute | solution.py:68
  15.1 16.9 %collective-permute-start.2 = (bf16[64,2048]{1,0:T(8,128)(2,1)S(1)}, bf16[64,2048]{1,0:T(8,128)(2,1)S(1)}, u32[]{:S(2)}, u32[]{:S(2)}) collective-permute-start(bf16[64,2048]{1,0:T(8,128)(2,1)S(1)} %get-tuple-element.62), channel_id=1, source_target_pairs={{0,96},{32,0},{64,32},{96,64},{1,97},{33,1},{65,33},{97,65},{2,98}... | collective-permute-start | bytes 786440 | tf_op jit(solution)/shard_map/ppermute | solution.py:68
  16.2 3.9 %copy-start.15 = (bf16[8,256,1024]{2,1,0:T(8,128)(2,1)S(1)}, bf16[8,256,1024]{2,1,0:T(8,128)(2,1)}, u32[]{:S(2)}) copy-start(bf16[8,256,1024]{2,1,0:T(8,128)(2,1)} %param.15) | copy-start | bytes 12582916
  22.8 36.4 %all-to-all-start = ((bf16[64,128,128]{2,1,0:T(8,128)(2,1)}), bf16[64,128,128]{2,1,0:T(8,128)(2,1)S(1)}, u32[]{:S(2)}, u32[]{:S(2)}) async-start(bf16[64,128,128]{2,1,0:T(8,128)(2,1)} %bitcast.102), calls=%async_computation | async-start | bytes 4194304 | tf_op jit(solution)/shard_map/all_to_all | solution.py:528
  30.9 3.4 %copy-start.10 = (bf16[1024,64]{0,1:T(8,128)(2,1)S(1)}, bf16[1024,64]{0,1:T(8,128)(2,1)}, u32[]{:S(2)}) copy-start(bf16[1024,64]{0,1:T(8,128)(2,1)} %param.19) | copy-start | bytes 393220
  33.1 4.8 %collective-permute-start.3 = (bf16[4,64,2048]{2,1,0:T(8,128)(2,1)}, bf16[4,64,2048]{2,1,0:T(8,128)(2,1)}, u32[]{:S(2)}, u32[]{:S(2)}) collective-permute-start(bf16[4,64,2048]{2,1,0:T(8,128)(2,1)} %pad_maximum_fusion.1), channel_id=1, source_target_pairs={{0,1},{1,0},{2,3},{3,2},{4,5},{5,4},{6,7},{7,6},{8,9},{9,8},{10,11... | collective-permute-start | bytes 3145736 | tf_op jit(solution)/shard_map/ppermute | solution.py:68
  34.5 2.4 %collective-permute-start.4 = (bf16[64,64,8]{0,2,1:T(8,128)(2,1)S(1)}, bf16[64,64,8]{0,2,1:T(8,128)(2,1)}, u32[]{:S(2)}, u32[]{:S(2)}) collective-permute-start(bf16[64,64,8]{0,2,1:T(8,128)(2,1)S(1)} %dynamic-slice_bitcast_fusion.4), channel_id=1, source_target_pairs={{0,1},{1,0},{2,3},{3,2},{4,5},{5,4},{6,7},{7,6},{8,9},{9,8},{10,11... | collective-permute-start | bytes 196616 | tf_op jit(solution)/shard_map/ppermute | solution.py:68
  62.1 4.9 %collective-permute-start.5 = (bf16[512,128]{1,0:T(8,128)(2,1)S(1)}, bf16[512,128]{1,0:T(8,128)(2,1)S(1)}, u32[]{:S(2)}, u32[]{:S(2)}) collective-permute-start(bf16[512,128]{1,0:T(8,128)(2,1)S(1)} %get-tuple-element.37), channel_id=1, source_target_pairs={{0,96},{32,0},{64,32},{96,64},{1,97},{33,1},{65,33},{97,65},{2,98}... | collective-permute-start | bytes 393224 | tf_op jit(solution)/shard_map/ppermute | solution.py:68
  62.7 5.5 %collective-permute-start.6 = (bf16[512,128]{1,0:T(8,128)(2,1)S(1)}, bf16[512,128]{1,0:T(8,128)(2,1)S(1)}, u32[]{:S(2)}, u32[]{:S(2)}) collective-permute-start(bf16[512,128]{1,0:T(8,128)(2,1)S(1)} %get-tuple-element.38), channel_id=1, source_target_pairs={{0,64},{32,96},{64,0},{96,32},{1,65},{33,97},{65,1},{97,33},{2,66}... | collective-permute-start | bytes 393224 | tf_op jit(solution)/shard_map/ppermute | solution.py:68
  64.1 5.4 %collective-permute-start.7 = (bf16[512,128]{1,0:T(8,128)(2,1)S(1)}, bf16[512,128]{1,0:T(8,128)(2,1)S(1)}, u32[]{:S(2)}, u32[]{:S(2)}) collective-permute-start(bf16[512,128]{1,0:T(8,128)(2,1)S(1)} %get-tuple-element.39), channel_id=1, source_target_pairs={{0,32},{32,64},{64,96},{96,0},{1,33},{33,65},{65,97},{97,1},{2,34}... | collective-permute-start | bytes 393224 | tf_op jit(solution)/shard_map/ppermute | solution.py:68
  71.1 11.1 %copy-start.13 = (s32[1024]{0:T(1024)S(1)}, s32[1024]{0:T(1024)}, u32[]{:S(2)}) copy-start(s32[1024]{0:T(1024)} %param.25) | copy-start | bytes 12292
  71.1 39.4 %all-to-all-start.1 = ((bf16[64,128,128]{2,1,0:T(8,128)(2,1)}), bf16[64,128,128]{2,1,0:T(8,128)(2,1)S(1)}, u32[]{:S(2)}, u32[]{:S(2)}) async-start(bf16[64,128,128]{2,1,0:T(8,128)(2,1)} %bitcast.103), calls=%async_computation.1 | async-start | bytes 4194304 | tf_op jit(solution)/shard_map/all_to_all | solution.py:557
  82.2 2.6 %copy-start.2 = (bf16[896,3072]{1,0:T(8,128)(2,1)S(1)}, bf16[896,3072]{1,0:T(8,128)(2,1)}, u32[]{:S(2)}) copy-start(bf16[896,3072]{1,0:T(8,128)(2,1)} %weight_ref.1) | copy-start | bytes 16515076
  84.7 1.5 copy-start.3
  90.7 2.1 %collective-permute-start.8 = (f32[4,2,128]{2,1,0:T(2,128)S(1)}, f32[4,2,128]{2,1,0:T(2,128)S(1)}, u32[]{:S(2)}, u32[]{:S(2)}) collective-permute-start(f32[4,2,128]{2,1,0:T(2,128)S(1)} %get-tuple-element.71), channel_id=1, source_target_pairs={{0,1},{1,0},{2,3},{3,2},{4,5},{5,4},{6,7},{7,6},{8,9},{9,8},{10,11... | collective-permute-start | bytes 12296 | tf_op jit(solution)/shard_map/ppermute | solution.py:68
  91.9 61.1 %copy-start.6 = (s32[2]{0:T(128)}, s32[2]{0:T(128)S(1)}, u32[]{:S(2)}) copy-start(s32[2]{0:T(128)S(1)} %pad_add_fusion.place_ref) | copy-start | bytes 28
  110.5 4.0 %copy-start.4 = (f32[8192]{0:T(1024)S(1)}, f32[8192]{0:T(1024)}, u32[]{:S(2)}) copy-start(f32[8192]{0:T(1024)} %param.20) | copy-start | bytes 98308
  110.6 19.6 %collective-permute-start.13 = (bf16[48,128,128]{2,1,0:T(8,128)(2,1)S(1)}, bf16[48,128,128]{2,1,0:T(8,128)(2,1)S(1)}, u32[]{:S(2)}, u32[]{:S(2)}) collective-permute-start(bf16[48,128,128]{2,1,0:T(8,128)(2,1)S(1)} %slice.20), channel_id=1, source_target_pairs={{0,6},{1,97},{2,0},{3,99},{4,2},{5,101},{6,4},{7,103},{8,14},{9,10... | collective-permute-start | bytes 4718600 | tf_op jit(solution)/shard_map/ppermute | solution.py:80
  111.1 20.8 %collective-permute-start.14 = (bf16[48,128,128]{2,1,0:T(8,128)(2,1)S(1)}, bf16[48,128,128]{2,1,0:T(8,128)(2,1)S(1)}, u32[]{:S(2)}, u32[]{:S(2)}) collective-permute-start(bf16[48,128,128]{2,1,0:T(8,128)(2,1)S(1)} %slice.20), channel_id=1, source_target_pairs={{0,24},{1,9},{2,26},{3,11},{4,28},{5,13},{6,30},{7,15},{8,0},{9,17... | collective-permute-start | bytes 4718600 | tf_op jit(solution)/shard_map/ppermute | solution.py:80
  111.7 20.8 %collective-permute-start.15 = (bf16[48,128,128]{2,1,0:T(8,128)(2,1)S(1)}, bf16[48,128,128]{2,1,0:T(8,128)(2,1)S(1)}, u32[]{:S(2)}, u32[]{:S(2)}) collective-permute-start(bf16[48,128,128]{2,1,0:T(8,128)(2,1)S(1)} %slice.20), channel_id=1, source_target_pairs={{0,2},{1,33},{2,4},{3,35},{4,6},{5,37},{6,0},{7,39},{8,10},{9,41},... | collective-permute-start | bytes 4718600 | tf_op jit(solution)/shard_map/ppermute | solution.py:80
  112.9 29.7 %collective-permute-start.10 = (bf16[16,128,128]{2,1,0:T(8,128)(2,1)S(1)}, bf16[16,128,128]{2,1,0:T(8,128)(2,1)S(1)}, u32[]{:S(2)}, u32[]{:S(2)}) collective-permute-start(bf16[16,128,128]{2,1,0:T(8,128)(2,1)S(1)} %slice.19), channel_id=1, source_target_pairs={{0,6},{1,97},{2,0},{3,99},{4,2},{5,101},{6,4},{7,103},{8,14},{9,10... | collective-permute-start | bytes 1572872 | tf_op jit(solution)/shard_map/ppermute | solution.py:80
  114.5 28.1 %collective-permute-start.11 = (bf16[16,128,128]{2,1,0:T(8,128)(2,1)S(1)}, bf16[16,128,128]{2,1,0:T(8,128)(2,1)S(1)}, u32[]{:S(2)}, u32[]{:S(2)}) collective-permute-start(bf16[16,128,128]{2,1,0:T(8,128)(2,1)S(1)} %slice.19), channel_id=1, source_target_pairs={{0,24},{1,9},{2,26},{3,11},{4,28},{5,13},{6,30},{7,15},{8,0},{9,17... | collective-permute-start | bytes 1572872 | tf_op jit(solution)/shard_map/ppermute | solution.py:80
  114.5 18.0 %slice-start = ((s8[12582912]{0:T(1024)(128)(4,1)}), s8[4194304]{0:T(1024)(128)(4,1)S(1)}, s32[]{:S(2)}) async-start(s8[12582912]{0:T(1024)(128)(4,1)} %bitcast.95), calls=%async_computation.4 | async-start | bytes 8388608
  114.5 18.0 %slice-start.1 = ((s8[12582912]{0:T(1024)(128)(4,1)}), s8[4194304]{0:T(1024)(128)(4,1)S(1)}, s32[]{:S(2)}) async-start(s8[12582912]{0:T(1024)(128)(4,1)} %bitcast.95), calls=%async_computation.5 | async-start | bytes 8388608
  114.5 18.0 %slice-start.2 = ((s8[12582912]{0:T(1024)(128)(4,1)}), s8[4194304]{0:T(1024)(128)(4,1)S(1)}, s32[]{:S(2)}) async-start(s8[12582912]{0:T(1024)(128)(4,1)} %bitcast.95), calls=%async_computation.6 | async-start | bytes 8388608
  130.2 12.3 %collective-permute-start.12 = (bf16[16,128,128]{2,1,0:T(8,128)(2,1)S(1)}, bf16[16,128,128]{2,1,0:T(8,128)(2,1)S(1)}, u32[]{:S(2)}, u32[]{:S(2)}) collective-permute-start(bf16[16,128,128]{2,1,0:T(8,128)(2,1)S(1)} %slice.19), channel_id=1, source_target_pairs={{0,2},{1,33},{2,4},{3,35},{4,6},{5,37},{6,0},{7,39},{8,10},{9,41},... | collective-permute-start | bytes 1572872 | tf_op jit(solution)/shard_map/ppermute | solution.py:80
  142.5 10.4 %copy-start.16 = (f32[128,768]{1,0:T(8,128)S(1)}, f32[128,768]{1,0:T(8,128)}, u32[]{:S(2)}) copy-start(f32[128,768]{1,0:T(8,128)} %get-tuple-element.56) | copy-start | bytes 1179652
  149.2 23.5 %collective-permute-start.18 = (f32[384,768]{1,0:T(8,128)}, f32[384,768]{1,0:T(8,128)S(1)}, u32[]{:S(2)}, u32[]{:S(2)}) collective-permute-start(f32[384,768]{1,0:T(8,128)} %get-tuple-element.57), channel_id=1, source_target_pairs={{0,1},{1,0},{2,3},{3,2},{4,5},{5,4},{6,7},{7,6},{8,9},{9,8},{10,11... | collective-permute-start | bytes 3538952 | tf_op jit(solution)/shard_map/ppermute | solution.py:68
  153.0 18.9 %collective-permute-start.17 = (f32[128,768]{1,0:T(8,128)S(1)}, f32[128,768]{1,0:T(8,128)S(1)}, u32[]{:S(2)}, u32[]{:S(2)}) collective-permute-start(f32[128,768]{1,0:T(8,128)S(1)} %copy-done.16), channel_id=1, source_target_pairs={{0,1},{1,0},{2,3},{3,2},{4,5},{5,4},{6,7},{7,6},{8,9},{9,8},{10,11... | collective-permute-start | bytes 1179656 | tf_op jit(solution)/shard_map/ppermute | solution.py:68
  169.9 2.7 %copy-start.5 = (f32[8,128]{1,0:T(8,128)}, f32[8,128]{1,0:T(8,128)S(1)}, u32[]{:S(2)}) copy-start(f32[8,128]{1,0:T(8,128)S(1)} %merge_stats.1.mine_ref) | copy-start | bytes 12292
  169.9 2.7 %collective-permute-start.16 = (f32[8,128]{1,0:T(8,128)S(1)}, f32[8,128]{1,0:T(8,128)S(1)}, u32[]{:S(2)}, u32[]{:S(2)}) collective-permute-start(f32[8,128]{1,0:T(8,128)S(1)} %merge_stats.1.mine_ref), channel_id=1, source_target_pairs={{0,1},{1,0},{2,3},{3,2},{4,5},{5,4},{6,7},{7,6},{8,9},{9,8},{10,11... | collective-permute-start | bytes 12296 | tf_op jit(solution)/shard_map/ppermute | solution.py:68
  171.8 0.8 copy-start.8
  172.6 0.6 copy-start.12
  172.7 1.1 copy-start.7
  172.7 6.1 %copy-start.1 = (bf16[8,1024]{1,0:T(8,128)(2,1)S(1)}, bf16[8,1024]{1,0:T(8,128)(2,1)}, u32[]{:S(2)}) copy-start(bf16[8,1024]{1,0:T(8,128)(2,1)} %param.16) | copy-start | bytes 49156
Sparse Core Ops, SparseCore 0:
  16.0 50.9 all-gather.1

commit v5 on v4

--- a/solution.py
+++ b/solution.py
@@ -91,6 +91,38 @@
 def laid_along_lanes(largest, totals):
     lane = lax.broadcasted_iota(jnp.int32, (LINE, LINE), 1)
     return jnp.transpose(jnp.where(lane == 0, largest, totals))[:2]
+
+
+def copies_kernel(slabs_ref, out_ref, many_ref, sem):
+    slabs, many = many_ref.shape[:2]
+    copies = []
+    for slab in range(slabs):
+        for i in range(many):
+            many_ref[slab, i] = slabs_ref[slab]
+        for at in range(0, out_ref.shape[1], many):
+            copy = pltpu.make_async_copy(
+                many_ref.at[slab], out_ref.at[slab, pl.ds(at, many)], sem.at[slab, at // many]
+            )
+            copy.start()
+            copies.append(copy)
+    for copy in copies:
+        copy.wait()
+
+
+def copied(slabs, targets):
+    count, rows, lanes = slabs.shape
+    many = 4
+    return pl.pallas_call(
+        copies_kernel,
+        out_specs=pl.BlockSpec(memory_space=pltpu.HBM),
+        out_shape=pltpu.HBM((count, targets, rows, lanes), slabs.dtype),
+        scratch_shapes=[
+            pltpu.VMEM((count, many, rows, lanes), slabs.dtype),
+            pltpu.SemaphoreType.DMA((count, targets // many)),
+        ],
+        compiler_params=params(8),
+        name="attention_copies",
+    )(slabs)
 
 
 def projection_kernel(left_ref, weight_ref, base_ref, total_ref, *sent):
@@ -410,24 +442,31 @@
     sem,
     sem_in,
 ):
-    arrivals = [
-        pltpu.make_async_copy(source, target, sem_in.at[i])
-        for i, (source, target) in enumerate(
-            (
-                (own_first_in, own_first),
-                (other_first_in, other_first),
-                (amateur_in, amateur_ref),
-                (own_rest_in, own_rest),
-                (other_rest_in, other_rest),
-            )
+    quarters = limit_ref.shape[0] // 2
+    tall = 2 * LINE
+
+    def arrivals(piece):
+        at = pl.ds(max(piece - 1, 0) * LINE, LINE)
+        sides = (
+            ((own_first_in, own_first), (other_first_in, other_first))
+            if piece == 0
+            else ((own_rest_in, own_rest), (other_rest_in, other_rest))
         )
-    ]
-    for copy in arrivals:
-        copy.start()
+        quarter = lax.rem(place_ref[0] + piece, quarters)
+        rows = pl.ds(pl.multiple_of(quarter * tall, tall), tall)
+        pairs = [(source.at[at], target.at[at]) for source, target in sides]
+        pairs.append((amateur_in.at[rows], amateur_ref.at[rows]))
+        return [
+            pltpu.make_async_copy(source, target, sem_in.at[piece, i])
+            for i, (source, target) in enumerate(pairs)
+        ]
+
+    ahead = 2
+    for piece in range(ahead):
+        for copy in arrivals(piece):
+            copy.start()
     core = place_ref[1]
     first = core == 0
-    quarters = limit_ref.shape[0] // 2
-    tall = 2 * LINE
     step_rows = 32
     copies = []
     for piece in range(quarters):
@@ -440,8 +479,11 @@
             sides.append(
                 (column_of(limit - top), column_of(stats[pl.ds(quarters + quarter, 1)]))
             )
-        for copy in (arrivals[:3], arrivals[3:], (), ())[piece]:
+        for copy in arrivals(piece):
             copy.wait()
+        if piece + ahead < quarters:
+            for copy in arrivals(piece + ahead):
+                copy.start()
         experts = (own_first, other_first) if piece == 0 else (own_rest, other_rest)
         offset = 0 if piece == 0 else (piece - 1) * LINE
         for at in range(0, LINE, step_rows):
@@ -481,7 +523,7 @@
         + [
             pltpu.VMEM((rows // (2 * LINE), 2 * LINE, columns), jnp.float32),
             pltpu.SemaphoreType.DMA((rows // (2 * LINE),)),
-            pltpu.SemaphoreType.DMA((5,)),
+            pltpu.SemaphoreType.DMA((4, 3)),
         ],
         compiler_params=params(60),
         cost_estimate=pl.CostEstimate(
@@ -520,9 +562,8 @@
 
     attention = attend(queries, cache_keys, cache_values, new_keys, new_values, lengths)
     slabs = attention.reshape(per, depth, heads, LINE).transpose(1, 2, 0, 3)
-    copies = jnp.broadcast_to(
-        slabs.reshape(depth, 1, heads * per, LINE), (depth, chips // depth, heads * per, LINE)
-    ).reshape(chips * heads * per, LINE)
+    copies = copied(slabs.reshape(depth, heads * per, LINE), chips // depth)
+    copies = copies.reshape(chips * heads * per, LINE)
     copies, residual, kept_weight = lax.optimization_barrier((copies, residual, out_weight))
     everyone = lax.all_gather(amateur_hidden, "z", axis=0, tiled=True)
     arrived = lax.all_to_all(copies, CHIPS, split_axis=0, concat_axis=0, tiled=True)

time: 186 us -> 187 us (level)
  Pallas kernels: 47.1 us -> 49 us
  transfers between devices with their start and end apart: 22 -> 22, of which waited for: 11 -> 11; matrix products, arithmetic and copies ran while one was open for 9% -> 8% of each run, Pallas kernels for 19% -> 20%
where the time goes in v5:
time: 187 us; the launch traced here: 186 us
  Pallas kernels  49 us (26%)
  waiting for transfers between devices  47.9 us (26%)
  starting transfers between devices  40.4 us (22%)
  blocking collectives  15.1 us (8%)
  between operations  13.8 us (7%)
  local copies, waits for them, and re-layouts  10.9 us (6%)
  matrix products  4.55 us (2%)
  other arithmetic  4.29 us (2%)
    all_to_all x2, waiting for transfers between devices, body(): lax.all_to_all(copies, CHIPS, split_axis=0, concat_axis=0, tiled=True)  35.8 us
    pallas_call x3, Pallas kernels, head(): pl.pallas_call(functools.partial(head_kernel, pieces, steps, features, re...  31.5 us
    all_to_all x2, starting transfers between devices, body(): lax.all_to_all(copies, CHIPS, split_axis=0, concat_axis=0, tiled=True)  19.2 us
    ppermute x13, starting transfers between devices, shift(): return lax.ppermute(x, axis, [(i, (i + step) % size) for i in range(size)])  17.3 us
    all_to_all x1, blocking collectives, body(): lax.all_to_all(copies, CHIPS, split_axis=0, concat_axis=0, tiled=True)  15.1 us
    ppermute x13, waiting for transfers between devices, shift(): return lax.ppermute(x, axis, [(i, (i + step) % size) for i in range(size)])  5.77 us
    pallas_call x1, Pallas kernels, contrast(): pl.pallas_call(contrast_kernel, in_specs=[pl.BlockSpec(memory_space=pltpu...  5.51 us
    unnamed x40, local copies, waits for them, and re-layouts  5.15 us
  transfers between devices with their start and end apart: 22, of which 11 were waited for; matrix products, arithmetic and copies ran while one was open for 8% of the time, Pallas kernels for 20%

profile of v5, /device:TPU:1, one launch (start us, length us, event | category | flops | bytes accessed | tf_op | source)
XLA Modules:
  0.0 186.1 jit_solution(11294258508797927915)
XLA Ops:
  6.6 1.5 collective-permute-start.9
  8.1 2.0 %dynamic-slice_bitcast_fusion.2 = (bf16[64,2048]{1,0:T(8,128)(2,1)}, bf16[64,2048]{1,0:T(8,128)(2,1)S(1)}, bf16[64,2048]{1,0:T(8,128)(2,1)}) fusion(bf16[8192,64]{0,1:T(8,128)(2,1)} %param.21, s32[]{:T(128)S(6)} %select_n.64, s32[]{:T(128)S(6)} %select_n.66, s32[]{:T(128)S(6)} %select_n.65), kind=kLoop, calls=%fused_computation.19 | loop fusion | bytes 1572876 | tf_op jit(solution)/shard_map/dynamic_slice | solution.py:576
  10.1 1.7 collective-permute-start
  11.8 3.3 %collective-permute-start.1 = (bf16[64,2048]{1,0:T(8,128)(2,1)}, bf16[64,2048]{1,0:T(8,128)(2,1)S(1)}, u32[]{:S(2)}, u32[]{:S(2)}) collective-permute-start(bf16[64,2048]{1,0:T(8,128)(2,1)} %get-tuple-element.63), channel_id=1, source_target_pairs={{0,64},{32,96},{64,0},{96,32},{1,65},{33,97},{65,1},{97,33},{2,66}... | collective-permute-start | bytes 786440 | tf_op jit(solution)/shard_map/ppermute | solution.py:68
  15.1 0.7 collective-permute-start.2
  16.2 3.6 %fusion.31 = (f32[8,8,8]{2,1,0:T(8,128)S(1)}, f32[8,8,8,256]{3,2,1,0:T(8,128)S(1)}) fusion(bf16[8,8,8,128]{3,0,2,1:T(8,128)(2,1)S(1)} %bitcast.116, pred[8,256]{1,0:T(8,128)(4,1)S(1)} %iota_compare_fusion, bf16[8,256,1024]{2,1,0:T(8,128)(2,1)} %param.14), kind=kOutput, calls=%fused_computation.52 | convolution fusion | flops 33947136 | bytes 4853760 | tf_op jit(solution)/shard_map/rkgd,rlkd->rkgl/dot_general | solution.py:35
  20.1 0.7 fusion.15
  21.0 1.5 attention_copies.1
  22.4 8.1 %all-to-all-start = ((bf16[64,128,128]{2,1,0:T(8,128)(2,1)}), bf16[64,128,128]{2,1,0:T(8,128)(2,1)S(1)}, u32[]{:S(2)}, u32[]{:S(2)}) async-start(bf16[64,128,128]{2,1,0:T(8,128)(2,1)} %bitcast.103), calls=%async_computation | async-start | bytes 4194304 | tf_op jit(solution)/shard_map/all_to_all | solution.py:569
  30.6 1.0 dynamic-slice_bitcast_fusion.3
  31.6 1.1 pad_maximum_fusion.1
  32.8 1.2 collective-permute-start.3
  34.2 2.3 %collective-permute-done.4 = bf16[64,64,8]{0,2,1:T(8,128)(2,1)} collective-permute-done((bf16[64,64,8]{0,2,1:T(8,128)(2,1)S(1)}, bf16[64,64,8]{0,2,1:T(8,128)(2,1)}, u32[]{:S(2)}, u32[]{:S(2)}) %collective-permute-start.4) | collective-permute-done | bytes 65568 | tf_op jit(solution)/shard_map/ppermute | solution.py:68
  36.5 0.9 bitcast_select_fusion.1
  37.6 1.4 select_bitcast_fusion.1
  39.2 1.4 copy.28
  40.7 18.2 %all-to-all-done = bf16[64,128,128]{2,1,0:T(8,128)(2,1)S(1)} async-done(((bf16[64,128,128]{2,1,0:T(8,128)(2,1)}), bf16[64,128,128]{2,1,0:T(8,128)(2,1)S(1)}, u32[]{:S(2)}, u32[]{:S(2)}) %all-to-all-start) | async-done | bytes 2097184 | tf_op jit(solution)/shard_map/all_to_all | solution.py:569
  58.9 2.9 %projection.1 = (f32[512,128]{1,0:T(8,128)S(1)}, bf16[512,128]{1,0:T(8,128)(2,1)S(1)}, bf16[512,128]{1,0:T(8,128)(2,1)S(1)}, bf16[512,128]{1,0:T(8,128)(2,1)S(1)}) custom-call(bf16[512,2048]{1,0:T(8,128)(2,1)S(1)} %bitcast.97, bf16[512,2048]{1,0:T(8,128)(2,1)} %bitcast.105, bf16[512,128]{1,0:T(8,128)(2,1)S(1)} %maximum_bitcast_fusion.base_ref), custom_call_target="tpu_custom_call" | custom-call | flops 1073741824 | bytes 4194304 | tf_op jit(solution)/shard_map/projection/pallas_call | solution.py:143
  61.8 0.6 collective-permute-start.5
  62.4 1.4 collective-permute-start.6
  63.7 3.2 %all-gather.2.cloned.1.call-done.hidden_ref = bf16[1024,896]{1,0:T(8,128)(2,1)} async-done(((bf16[256,896]{1,0:T(8,128)(2,1)}), bf16[1024,896]{1,0:T(8,128)(2,1)}) %all-gather.2.cloned.1.call-update) | async-done | bytes 1835024 | tf_op jit(solution)/shard_map/all_gather | solution.py:568
  67.2 1.0 collective-permute-done.6.refs_1_
  68.2 1.3 collective-permute-done.7.refs_2_
  69.5 1.5 hidden.1
  71.1 11.1 %all-to-all-start.1 = ((bf16[64,128,128]{2,1,0:T(8,128)(2,1)}), bf16[64,128,128]{2,1,0:T(8,128)(2,1)S(1)}, u32[]{:S(2)}, u32[]{:S(2)}) async-start(bf16[64,128,128]{2,1,0:T(8,128)(2,1)} %bitcast.104), calls=%async_computation.1 | async-start | bytes 4194304 | tf_op jit(solution)/shard_map/all_to_all | solution.py:598
  82.2 2.6 %copy-done.2 = bf16[896,3072]{1,0:T(8,128)(2,1)S(1)} copy-done((bf16[896,3072]{1,0:T(8,128)(2,1)S(1)}, bf16[896,3072]{1,0:T(8,128)(2,1)}, u32[]{:S(2)}) %copy-start.2) | copy-done | bytes 5505048
  84.7 1.5 copy-done.3
  86.2 4.4 %amateur_head.1 = (bf16[1024,768]{1,0:T(8,128)(2,1)}, f32[4,2,2,128]{3,2,1,0:T(2,128)S(1)}) custom-call(s32[1]{0:T(128)} %bitcast.33.place_ref, bf16[1024,896]{1,0:T(8,128)(2,1)S(1)} %copy-done.3, bf16[896,3072]{1,0:T(8,128)(2,1)S(1)} %copy-done.2), custom_call_target="tpu_custom_call" | custom-call | flops 1409286144 | bytes 4784128 | tf_op jit(solution)/shard_map/amateur_head/pallas_call | solution.py:309
  90.6 1.2 collective-permute-start.8
  92.1 0.7 mul.74.limit_ref
  92.8 17.6 %all-to-all-done.1.refs_0_ = bf16[64,128,128]{2,1,0:T(8,128)(2,1)S(1)} async-done(((bf16[64,128,128]{2,1,0:T(8,128)(2,1)}), bf16[64,128,128]{2,1,0:T(8,128)(2,1)S(1)}, u32[]{:S(2)}, u32[]{:S(2)}) %all-to-all-start.1) | async-done | bytes 2097184 | tf_op jit(solution)/shard_map/all_to_all | solution.py:598
  110.5 0.5 collective-permute-start.13
  111.1 0.6 collective-permute-start.14
  111.7 1.1 collective-permute-start.15
  112.8 1.6 collective-permute-start.10
  114.5 14.8 %expert_head.3 = (f32[128,768]{1,0:T(8,128)}, f32[128,768]{1,0:T(8,128)}, f32[2,128]{1,0:T(2,128)S(1)}) custom-call(bf16[64,128,128]{2,1,0:T(8,128)(2,1)S(1)} %all-to-all-done.1.refs_0_, bf16[8192,768]{1,0:T(8,128)(2,1)} %refs_3_.3, bf16[8192,768]{1,0:T(8,128)(2,1)} %collective-permute-done.9.refs_2_.refs_4_, f32[64,128]{1,0:T(8,128)S(1)} %bitcast.99), custom_call_target="tpu_custom_call" | custom-call | flops 3221225472 | bytes 25165824 | tf_op jit(solution)/shard_map/expert_head/pallas_call | solution.py:273
  129.3 0.9 collective-permute-done.13.refs_0_
  130.2 1.7 collective-permute-done.14.refs_1_
  131.8 0.6 collective-permute-done.15.refs_2_
  132.4 10.0 %expert_head.4 = (f32[384,768]{1,0:T(8,128)S(1)}, f32[384,768]{1,0:T(8,128)S(1)}, f32[384,128]{1,0:T(8,128)S(1)}) custom-call(bf16[48,128,128]{2,1,0:T(8,128)(2,1)S(1)} %collective-permute-done.13.refs_0_, bf16[48,128,128]{2,1,0:T(8,128)(2,1)S(1)} %collective-permute-done.14.refs_1_, bf16[48,128,128]{2,1,0:T(8,128)(2,1)S(1)} %collective-permute-done.15.refs_2_, ...), custom_call_target="tpu_custom_call" | custom-call | flops 7247757312 | bytes 18874368 | tf_op jit(solution)/shard_map/expert_head/pallas_call | solution.py:273
  142.5 6.6 %expert_head.5 = (f32[384,768]{1,0:T(8,128)}, f32[384,768]{1,0:T(8,128)}, f32[6,128]{1,0:T(8,128)S(1)}) custom-call(bf16[16,128,128]{2,1,0:T(8,128)(2,1)S(1)} %collective-permute-done.10.refs_0_, bf16[16,128,128]{2,1,0:T(8,128)(2,1)S(1)} %collective-permute-done.11.refs_1_, bf16[16,128,128]{2,1,0:T(8,128)(2,1)S(1)} %collective-permute-done.12.refs_2_, ...), custom_call_target="tpu_custom_call" | custom-call | flops 2415919104 | bytes 6291456 | tf_op jit(solution)/shard_map/expert_head/pallas_call | solution.py:273
  149.1 3.8 %collective-permute-start.18 = (f32[384,768]{1,0:T(8,128)}, f32[384,768]{1,0:T(8,128)S(1)}, u32[]{:S(2)}, u32[]{:S(2)}) collective-permute-start(f32[384,768]{1,0:T(8,128)} %get-tuple-element.57), channel_id=1, source_target_pairs={{0,1},{1,0},{2,3},{3,2},{4,5},{5,4},{6,7},{7,6},{8,9},{9,8},{10,11... | collective-permute-start | bytes 3538952 | tf_op jit(solution)/shard_map/ppermute | solution.py:68
  152.9 1.3 spread_stats.1
  154.3 15.1 %all_to_all.19.parts_ref = bf16[64,16,128]{2,1,0:T(8,128)(2,1)S(1)} all-to-all(bf16[64,16,128]{2,1,0:T(8,128)(2,1)} %spread_stats.1), channel_id=1, replica_groups=mesh['z'=4,'y'=4,'x'=4,'core'=2] {'z','y','x'}, dimensions={0} | all-to-all | bytes 524288 | tf_op jit(solution)/shard_map/all_to_all | solution.py:632
  169.9 1.9 %collective-permute-start.16 = (f32[8,128]{1,0:T(8,128)S(1)}, f32[8,128]{1,0:T(8,128)S(1)}, u32[]{:S(2)}, u32[]{:S(2)}) collective-permute-start(f32[8,128]{1,0:T(8,128)S(1)} %merge_stats.1.mine_ref), channel_id=1, source_target_pairs={{0,1},{1,0},{2,3},{3,2},{4,5},{5,4},{6,7},{7,6},{8,9},{9,8},{10,11... | collective-permute-start | bytes 12296 | tf_op jit(solution)/shard_map/ppermute | solution.py:68
  171.8 0.8 collective-permute-done.16.theirs_ref
  172.7 0.6 copy-done.12
  173.7 5.5 %contrast.1 = f32[1024,768]{1,0:T(8,128)} custom-call(s32[2]{0:T(128)} %copy-done.6, f32[8,128]{1,0:T(8,128)} %copy-done.5, f32[8,128]{1,0:T(8,128)} %copy-done.12, f32[8,128]{1,0:T(8,128)} %mul.74.limit_ref, f32[128,768]{1,0:T(8,128)} %get-tuple-element.54.own_first_in, f32[384,768]{1,0:T(8,128)} %get-tuple-element.55.own_rest_in, f32[128,768]{1,0:T(8,128)} %copy-done.8, ...), custom_call_target="tpu_custom_call" | custom-call | flops 4718592 | bytes 7864320 | tf_op jit(solution)/shard_map/contrast/pallas_call | solution.py:515
  (81 shorter events, 3.1 us)
Async XLA Ops:
  6.5 9.4 %copy-start = (bf16[8,1024]{1,0:T(8,128)(2,1)S(1)}, bf16[8,1024]{1,0:T(8,128)(2,1)}, u32[]{:S(2)}) copy-start(bf16[8,1024]{1,0:T(8,128)(2,1)} %param.16) | copy-start | bytes 49156
  6.5 9.3 %copy-start.11 = (bf16[8,1024]{1,0:T(8,128)(2,1)S(1)}, bf16[8,1024]{1,0:T(8,128)(2,1)}, u32[]{:S(2)}) copy-start(bf16[8,1024]{1,0:T(8,128)(2,1)} %param.17) | copy-start | bytes 49156
  6.5 9.3 %copy-start.14 = (s32[8]{0:T(128)S(1)}, s32[8]{0:T(128)}, u32[]{:S(2)}) copy-start(s32[8]{0:T(128)} %param.18) | copy-start | bytes 100
  6.5 9.4 %copy-start.9 = (bf16[8,8192]{1,0:T(8,128)(2,1)S(1)}, bf16[8,8192]{1,0:T(8,128)(2,1)}, u32[]{:S(2)}) copy-start(bf16[8,8192]{1,0:T(8,128)(2,1)} %param.13) | copy-start | bytes 393220
  6.5 60.4 %all-gather.2.cloned.1.call-start = ((), (), s32[]{:S(2)}) async-start(), calls=%async_computation.3 | async-start | bytes 2293760 | tf_op jit(solution)/shard_map/all_gather | solution.py:568
  6.6 107.9 %collective-permute-start.9 = (bf16[8192,768]{1,0:T(8,128)(2,1)}, bf16[8192,768]{1,0:T(8,128)(2,1)}, u32[]{:S(2)}, u32[]{:S(2)}) collective-permute-start(bf16[8192,768]{1,0:T(8,128)(2,1)} %refs_3_.3), channel_id=1, source_target_pairs={{0,1},{1,0},{2,3},{3,2},{4,5},{5,4},{6,7},{7,6},{8,9},{9,8},{10,11... | collective-permute-start | bytes 37748744 | tf_op jit(solution)/shard_map/ppermute | solution.py:68
  10.1 21.6 %collective-permute-start = (bf16[64,2048]{1,0:T(8,128)(2,1)}, bf16[64,2048]{1,0:T(8,128)(2,1)S(1)}, u32[]{:S(2)}, u32[]{:S(2)}) collective-permute-start(bf16[64,2048]{1,0:T(8,128)(2,1)} %get-tuple-element.61), channel_id=1, source_target_pairs={{0,32},{32,64},{64,96},{96,0},{1,33},{33,65},{65,97},{97,1},{2,34}... | collective-permute-start | bytes 786440 | tf_op jit(solution)/shard_map/ppermute | solution.py:68
  11.8 19.8 %collective-permute-start.1 = (bf16[64,2048]{1,0:T(8,128)(2,1)}, bf16[64,2048]{1,0:T(8,128)(2,1)S(1)}, u32[]{:S(2)}, u32[]{:S(2)}) collective-permute-start(bf16[64,2048]{1,0:T(8,128)(2,1)} %get-tuple-element.63), channel_id=1, source_target_pairs={{0,64},{32,96},{64,0},{96,32},{1,65},{33,97},{65,1},{97,33},{2,66}... | collective-permute-start | bytes 786440 | tf_op jit(solution)/shard_map/ppermute | solution.py:68
  15.1 16.5 %collective-permute-start.2 = (bf16[64,2048]{1,0:T(8,128)(2,1)S(1)}, bf16[64,2048]{1,0:T(8,128)(2,1)S(1)}, u32[]{:S(2)}, u32[]{:S(2)}) collective-permute-start(bf16[64,2048]{1,0:T(8,128)(2,1)S(1)} %get-tuple-element.62), channel_id=1, source_target_pairs={{0,96},{32,0},{64,32},{96,64},{1,97},{33,1},{65,33},{97,65},{2,98}... | collective-permute-start | bytes 786440 | tf_op jit(solution)/shard_map/ppermute | solution.py:68
  16.2 3.9 %copy-start.15 = (bf16[8,256,1024]{2,1,0:T(8,128)(2,1)S(1)}, bf16[8,256,1024]{2,1,0:T(8,128)(2,1)}, u32[]{:S(2)}) copy-start(bf16[8,256,1024]{2,1,0:T(8,128)(2,1)} %param.15) | copy-start | bytes 12582916
  22.4 36.4 %all-to-all-start = ((bf16[64,128,128]{2,1,0:T(8,128)(2,1)}), bf16[64,128,128]{2,1,0:T(8,128)(2,1)S(1)}, u32[]{:S(2)}, u32[]{:S(2)}) async-start(bf16[64,128,128]{2,1,0:T(8,128)(2,1)} %bitcast.103), calls=%async_computation | async-start | bytes 4194304 | tf_op jit(solution)/shard_map/all_to_all | solution.py:569
  30.6 3.3 %copy-start.10 = (bf16[1024,64]{0,1:T(8,128)(2,1)S(1)}, bf16[1024,64]{0,1:T(8,128)(2,1)}, u32[]{:S(2)}) copy-start(bf16[1024,64]{0,1:T(8,128)(2,1)} %param.19) | copy-start | bytes 393220
  32.8 4.8 %collective-permute-start.3 = (bf16[4,64,2048]{2,1,0:T(8,128)(2,1)}, bf16[4,64,2048]{2,1,0:T(8,128)(2,1)}, u32[]{:S(2)}, u32[]{:S(2)}) collective-permute-start(bf16[4,64,2048]{2,1,0:T(8,128)(2,1)} %pad_maximum_fusion.1), channel_id=1, source_target_pairs={{0,1},{1,0},{2,3},{3,2},{4,5},{5,4},{6,7},{7,6},{8,9},{9,8},{10,11... | collective-permute-start | bytes 3145736 | tf_op jit(solution)/shard_map/ppermute | solution.py:68
  34.1 2.4 %collective-permute-start.4 = (bf16[64,64,8]{0,2,1:T(8,128)(2,1)S(1)}, bf16[64,64,8]{0,2,1:T(8,128)(2,1)}, u32[]{:S(2)}, u32[]{:S(2)}) collective-permute-start(bf16[64,64,8]{0,2,1:T(8,128)(2,1)S(1)} %dynamic-slice_bitcast_fusion.4), channel_id=1, source_target_pairs={{0,1},{1,0},{2,3},{3,2},{4,5},{5,4},{6,7},{7,6},{8,9},{9,8},{10,11... | collective-permute-start | bytes 196616 | tf_op jit(solution)/shard_map/ppermute | solution.py:68
  61.8 5.4 %collective-permute-start.5 = (bf16[512,128]{1,0:T(8,128)(2,1)S(1)}, bf16[512,128]{1,0:T(8,128)(2,1)S(1)}, u32[]{:S(2)}, u32[]{:S(2)}) collective-permute-start(bf16[512,128]{1,0:T(8,128)(2,1)S(1)} %get-tuple-element.37), channel_id=1, source_target_pairs={{0,96},{32,0},{64,32},{96,64},{1,97},{33,1},{65,33},{97,65},{2,98}... | collective-permute-start | bytes 393224 | tf_op jit(solution)/shard_map/ppermute | solution.py:68
  62.4 5.8 %collective-permute-start.6 = (bf16[512,128]{1,0:T(8,128)(2,1)S(1)}, bf16[512,128]{1,0:T(8,128)(2,1)S(1)}, u32[]{:S(2)}, u32[]{:S(2)}) collective-permute-start(bf16[512,128]{1,0:T(8,128)(2,1)S(1)} %get-tuple-element.38), channel_id=1, source_target_pairs={{0,64},{32,96},{64,0},{96,32},{1,65},{33,97},{65,1},{97,33},{2,66}... | collective-permute-start | bytes 393224 | tf_op jit(solution)/shard_map/ppermute | solution.py:68
  63.7 5.8 %collective-permute-start.7 = (bf16[512,128]{1,0:T(8,128)(2,1)S(1)}, bf16[512,128]{1,0:T(8,128)(2,1)S(1)}, u32[]{:S(2)}, u32[]{:S(2)}) collective-permute-start(bf16[512,128]{1,0:T(8,128)(2,1)S(1)} %get-tuple-element.39), channel_id=1, source_target_pairs={{0,32},{32,64},{64,96},{96,0},{1,33},{33,65},{65,97},{97,1},{2,34}... | collective-permute-start | bytes 393224 | tf_op jit(solution)/shard_map/ppermute | solution.py:68
  71.1 11.1 %copy-start.13 = (s32[1024]{0:T(1024)S(1)}, s32[1024]{0:T(1024)}, u32[]{:S(2)}) copy-start(s32[1024]{0:T(1024)} %param.25) | copy-start | bytes 12292
  71.1 39.4 %all-to-all-start.1 = ((bf16[64,128,128]{2,1,0:T(8,128)(2,1)}), bf16[64,128,128]{2,1,0:T(8,128)(2,1)S(1)}, u32[]{:S(2)}, u32[]{:S(2)}) async-start(bf16[64,128,128]{2,1,0:T(8,128)(2,1)} %bitcast.104), calls=%async_computation.1 | async-start | bytes 4194304 | tf_op jit(solution)/shard_map/all_to_all | solution.py:598
  82.2 2.6 %copy-start.2 = (bf16[896,3072]{1,0:T(8,128)(2,1)S(1)}, bf16[896,3072]{1,0:T(8,128)(2,1)}, u32[]{:S(2)}) copy-start(bf16[896,3072]{1,0:T(8,128)(2,1)} %weight_ref.1) | copy-start | bytes 16515076
  84.7 1.5 copy-start.3
  90.6 2.1 %collective-permute-start.8 = (f32[4,2,128]{2,1,0:T(2,128)S(1)}, f32[4,2,128]{2,1,0:T(2,128)S(1)}, u32[]{:S(2)}, u32[]{:S(2)}) collective-permute-start(f32[4,2,128]{2,1,0:T(2,128)S(1)} %get-tuple-element.71), channel_id=1, source_target_pairs={{0,1},{1,0},{2,3},{3,2},{4,5},{5,4},{6,7},{7,6},{8,9},{9,8},{10,11... | collective-permute-start | bytes 12296 | tf_op jit(solution)/shard_map/ppermute | solution.py:68
  91.9 61.0 %copy-start.6 = (s32[2]{0:T(128)}, s32[2]{0:T(128)S(1)}, u32[]{:S(2)}) copy-start(s32[2]{0:T(128)S(1)} %pad_add_fusion.place_ref) | copy-start | bytes 28
  110.4 4.0 %copy-start.4 = (f32[8192]{0:T(1024)S(1)}, f32[8192]{0:T(1024)}, u32[]{:S(2)}) copy-start(f32[8192]{0:T(1024)} %param.20) | copy-start | bytes 98308
  110.5 19.6 %collective-permute-start.13 = (bf16[48,128,128]{2,1,0:T(8,128)(2,1)S(1)}, bf16[48,128,128]{2,1,0:T(8,128)(2,1)S(1)}, u32[]{:S(2)}, u32[]{:S(2)}) collective-permute-start(bf16[48,128,128]{2,1,0:T(8,128)(2,1)S(1)} %slice.20), channel_id=1, source_target_pairs={{0,6},{1,97},{2,0},{3,99},{4,2},{5,101},{6,4},{7,103},{8,14},{9,10... | collective-permute-start | bytes 4718600 | tf_op jit(solution)/shard_map/ppermute | solution.py:80
  111.1 20.8 %collective-permute-start.14 = (bf16[48,128,128]{2,1,0:T(8,128)(2,1)S(1)}, bf16[48,128,128]{2,1,0:T(8,128)(2,1)S(1)}, u32[]{:S(2)}, u32[]{:S(2)}) collective-permute-start(bf16[48,128,128]{2,1,0:T(8,128)(2,1)S(1)} %slice.20), channel_id=1, source_target_pairs={{0,24},{1,9},{2,26},{3,11},{4,28},{5,13},{6,30},{7,15},{8,0},{9,17... | collective-permute-start | bytes 4718600 | tf_op jit(solution)/shard_map/ppermute | solution.py:80
  111.7 20.8 %collective-permute-start.15 = (bf16[48,128,128]{2,1,0:T(8,128)(2,1)S(1)}, bf16[48,128,128]{2,1,0:T(8,128)(2,1)S(1)}, u32[]{:S(2)}, u32[]{:S(2)}) collective-permute-start(bf16[48,128,128]{2,1,0:T(8,128)(2,1)S(1)} %slice.20), channel_id=1, source_target_pairs={{0,2},{1,33},{2,4},{3,35},{4,6},{5,37},{6,0},{7,39},{8,10},{9,41},... | collective-permute-start | bytes 4718600 | tf_op jit(solution)/shard_map/ppermute | solution.py:80
  112.8 29.7 %collective-permute-start.10 = (bf16[16,128,128]{2,1,0:T(8,128)(2,1)S(1)}, bf16[16,128,128]{2,1,0:T(8,128)(2,1)S(1)}, u32[]{:S(2)}, u32[]{:S(2)}) collective-permute-start(bf16[16,128,128]{2,1,0:T(8,128)(2,1)S(1)} %slice.19), channel_id=1, source_target_pairs={{0,6},{1,97},{2,0},{3,99},{4,2},{5,101},{6,4},{7,103},{8,14},{9,10... | collective-permute-start | bytes 1572872 | tf_op jit(solution)/shard_map/ppermute | solution.py:80
  114.4 28.1 %collective-permute-start.11 = (bf16[16,128,128]{2,1,0:T(8,128)(2,1)S(1)}, bf16[16,128,128]{2,1,0:T(8,128)(2,1)S(1)}, u32[]{:S(2)}, u32[]{:S(2)}) collective-permute-start(bf16[16,128,128]{2,1,0:T(8,128)(2,1)S(1)} %slice.19), channel_id=1, source_target_pairs={{0,24},{1,9},{2,26},{3,11},{4,28},{5,13},{6,30},{7,15},{8,0},{9,17... | collective-permute-start | bytes 1572872 | tf_op jit(solution)/shard_map/ppermute | solution.py:80
  114.5 18.0 %slice-start = ((s8[12582912]{0:T(1024)(128)(4,1)}), s8[4194304]{0:T(1024)(128)(4,1)S(1)}, s32[]{:S(2)}) async-start(s8[12582912]{0:T(1024)(128)(4,1)} %bitcast.95), calls=%async_computation.4 | async-start | bytes 8388608
  114.5 18.0 %slice-start.1 = ((s8[12582912]{0:T(1024)(128)(4,1)}), s8[4194304]{0:T(1024)(128)(4,1)S(1)}, s32[]{:S(2)}) async-start(s8[12582912]{0:T(1024)(128)(4,1)} %bitcast.95), calls=%async_computation.5 | async-start | bytes 8388608
  114.5 18.0 %slice-start.2 = ((s8[12582912]{0:T(1024)(128)(4,1)}), s8[4194304]{0:T(1024)(128)(4,1)S(1)}, s32[]{:S(2)}) async-start(s8[12582912]{0:T(1024)(128)(4,1)} %bitcast.95), calls=%async_computation.6 | async-start | bytes 8388608
  130.2 12.4 %collective-permute-start.12 = (bf16[16,128,128]{2,1,0:T(8,128)(2,1)S(1)}, bf16[16,128,128]{2,1,0:T(8,128)(2,1)S(1)}, u32[]{:S(2)}, u32[]{:S(2)}) collective-permute-start(bf16[16,128,128]{2,1,0:T(8,128)(2,1)S(1)} %slice.19), channel_id=1, source_target_pairs={{0,2},{1,33},{2,4},{3,35},{4,6},{5,37},{6,0},{7,39},{8,10},{9,41},... | collective-permute-start | bytes 1572872 | tf_op jit(solution)/shard_map/ppermute | solution.py:80
  142.5 10.4 %copy-start.16 = (f32[128,768]{1,0:T(8,128)S(1)}, f32[128,768]{1,0:T(8,128)}, u32[]{:S(2)}) copy-start(f32[128,768]{1,0:T(8,128)} %get-tuple-element.56) | copy-start | bytes 1179652
  149.1 23.5 %collective-permute-start.18 = (f32[384,768]{1,0:T(8,128)}, f32[384,768]{1,0:T(8,128)S(1)}, u32[]{:S(2)}, u32[]{:S(2)}) collective-permute-start(f32[384,768]{1,0:T(8,128)} %get-tuple-element.57), channel_id=1, source_target_pairs={{0,1},{1,0},{2,3},{3,2},{4,5},{5,4},{6,7},{7,6},{8,9},{9,8},{10,11... | collective-permute-start | bytes 3538952 | tf_op jit(solution)/shard_map/ppermute | solution.py:68
  152.9 18.9 %collective-permute-start.17 = (f32[128,768]{1,0:T(8,128)S(1)}, f32[128,768]{1,0:T(8,128)S(1)}, u32[]{:S(2)}, u32[]{:S(2)}) collective-permute-start(f32[128,768]{1,0:T(8,128)S(1)} %copy-done.16), channel_id=1, source_target_pairs={{0,1},{1,0},{2,3},{3,2},{4,5},{5,4},{6,7},{7,6},{8,9},{9,8},{10,11... | collective-permute-start | bytes 1179656 | tf_op jit(solution)/shard_map/ppermute | solution.py:68
  169.9 2.7 %copy-start.5 = (f32[8,128]{1,0:T(8,128)}, f32[8,128]{1,0:T(8,128)S(1)}, u32[]{:S(2)}) copy-start(f32[8,128]{1,0:T(8,128)S(1)} %merge_stats.1.mine_ref) | copy-start | bytes 12292
  169.9 2.7 %collective-permute-start.16 = (f32[8,128]{1,0:T(8,128)S(1)}, f32[8,128]{1,0:T(8,128)S(1)}, u32[]{:S(2)}, u32[]{:S(2)}) collective-permute-start(f32[8,128]{1,0:T(8,128)S(1)} %merge_stats.1.mine_ref), channel_id=1, source_target_pairs={{0,1},{1,0},{2,3},{3,2},{4,5},{5,4},{6,7},{7,6},{8,9},{9,8},{10,11... | collective-permute-start | bytes 12296 | tf_op jit(solution)/shard_map/ppermute | solution.py:68
  171.8 0.8 copy-start.8
  172.6 0.6 copy-start.12
  172.6 1.1 copy-start.7
  172.6 6.6 %copy-start.1 = (bf16[8,1024]{1,0:T(8,128)(2,1)S(1)}, bf16[8,1024]{1,0:T(8,128)(2,1)}, u32[]{:S(2)}) copy-start(bf16[8,1024]{1,0:T(8,128)(2,1)} %param.16) | copy-start | bytes 49156
Sparse Core Ops, SparseCore 0:
  16.0 50.9 all-gather.1
